TPU v7x, 512 devices: a whole 4x4x16 slice. The times are simulated.
512 devices in a mesh: grp: 16 (over z), dev: 32 (over y, x, core).
Axes of the slice: x: 4, y: 4, z: 16, core: 2. Of those that a mesh axis runs over, the one named last changes fastest.
Arguments:
- student_patches: bfloat16 [131072, 256], P(('grp', 'dev')), may hold values from -8 to 8
- teacher_patches: bfloat16 [131072, 256], P(('grp', 'dev')), may hold values from -8 to 8
- mask_rows: int32 [8192], P(('grp', 'dev')), may hold values from 0 to 255, as said below
- student_proto: bfloat16 [131072, 256], P(('grp', 'dev')), may hold values from -2 to 2
- teacher_proto: bfloat16 [131072, 256], P(('grp', 'dev')), may hold values from -2 to 2
Outputs:
- loss: float32 [], replicated
- proto_grad: float32 [131072, 256], P(('grp', 'dev'))
Inputs may be any that keep to these rules, and one draw needn't show every extreme that they name: `mask_rows`: each aligned block of 16 entries (those of one device) holds distinct indices of that device's 256 patch tokens.
All inputs are finite; a program needn't handle non-finite values.
Results may differ from a plain program's by a relative error of at most 0.005.
Values may be sent and summed in bfloat16 or wider, within the bound.
No kernel may reach another device: no remote copies, remote signals or barrier semaphores. Data moves between devices by JAX's collectives and lax.ppermute only.
A program may use at most 128 MiB of HBM per device.

v0:
```python
import jax
import jax.numpy as jnp
from jax import lax
from jax.sharding import PartitionSpec as P

ITERS = 3


norm_eps = 1e-06
teacher_scale = 1.0 / 0.07
student_scale = 1.0 / 0.1


def scores(rows, weights):
    return lax.dot_general(
        rows, weights, (((1,), (1,)), ((), ())), preferred_element_type=jnp.float32
    )


def unit_rows(values):
    values = values.astype(jnp.float32)
    return values * lax.rsqrt(jnp.sum(values * values, axis=1, keepdims=True) + norm_eps)


def per_device(student_patches, teacher_patches, mask_rows, student_proto, teacher_proto):
    student_local = unit_rows(jnp.take(student_patches, mask_rows, axis=0)).astype(jnp.bfloat16)
    teacher_local = unit_rows(jnp.take(teacher_patches, mask_rows, axis=0)).astype(jnp.bfloat16)
    stacked = jnp.stack([student_local, teacher_local])
    gathered = lax.all_gather(stacked, ("grp", "dev"), axis=1, tiled=True)
    student_rows = gathered[0]
    teacher_rows = gathered[1]
    row_count = student_rows.shape[0]
    proto_f = student_proto.astype(jnp.float32)
    proto_scale = lax.rsqrt(jnp.sum(proto_f * proto_f, axis=1, keepdims=True) + norm_eps)
    unit_student = proto_f * proto_scale
    student_weights = unit_student.astype(jnp.bfloat16)
    teacher_weights = unit_rows(teacher_proto).astype(jnp.bfloat16)
    targets = jnp.exp(scores(teacher_rows, teacher_weights) * teacher_scale)
    targets = targets / jnp.sum(targets, axis=0, keepdims=True)
    first_part = jnp.sum(targets, axis=1)
    logits = scores(student_rows, student_weights) * student_scale
    expo = jnp.exp(logits)
    student_part = jnp.sum(expo, axis=1)
    first_total = lax.psum(first_part, ("grp", "dev"))
    targets = targets / first_total[:, None]
    for step in range(1, ITERS):
        targets = targets / jnp.sum(targets, axis=0, keepdims=True)
        row_total = lax.psum(jnp.sum(targets, axis=1), ("grp", "dev"))
        targets = targets / row_total[:, None]
    total = lax.psum(student_part, ("grp", "dev"))
    cross = lax.psum(jnp.sum(targets * logits), ("grp", "dev"))
    loss = (jnp.sum(jnp.log(total)) - cross) / row_count
    slope = ((expo / total[:, None] - targets) * student_scale).astype(jnp.bfloat16)
    unit_grad = lax.dot_general(
        slope, student_rows, (((0,), (0,)), ((), ())), preferred_element_type=jnp.float32
    )
    proto_grad = (
        unit_grad - unit_student * jnp.sum(unit_student * unit_grad, axis=1, keepdims=True)
    ) * proto_scale
    return (loss, proto_grad)


def solution(mesh):
    placed = (
        P(("grp", "dev"), None),
        P(("grp", "dev"), None),
        P(("grp", "dev")),
        P(("grp", "dev"), None),
        P(("grp", "dev"), None),
    )
    return jax.shard_map(
        per_device,
        mesh=mesh,
        in_specs=placed,
        out_specs=(P(), P(("grp", "dev"), None)),
        check_vma=False,
    )
```

profile of v0, /device:TPU:1, one launch (start us, length us, event | category | flops | bytes accessed | tf_op | source)
XLA Modules:
  0.0 682.2 jit_solution(5081655766250377625)
XLA Ops:
  7.2 0.7 compare_and_fusion
  7.9 0.7 compare_select_fusion
  8.6 0.6 gather_fusion.1
  9.2 1.5 gather_fusion
  11.0 0.6 pad_maximum_fusion
  11.6 1.0 copy.7
  12.6 1.0 fusion.20
  13.7 211.1 %all-gather.2.cloned.1.call-done = bf16[2,8192,256]{2,1,0:T(8,128)(2,1)} async-done(((bf16[2,16,256]{2,1,0:T(8,128)(2,1)}), bf16[2,8192,256]{2,1,0:T(8,128)(2,1)}) %all-gather.2.cloned.1.call-update) | async-done | bytes 8388624 | tf_op jit(solution)/shard_map/all_gather | solution.py:29
  224.8 3.5 fusion.34
  228.3 3.2 copy-done.1
  231.5 1.1 divide_reduce_fusion
  232.6 101.3 %psum.36 = f32[8192]{0:T(1024)S(1)} all-reduce(f32[8192]{0:T(1024)S(1)} %divide_reduce_fusion), channel_id=1, replica_groups=mesh['grp'=16,'dev'=32] {'grp','dev'}, use_global_device_ids=true, to_apply=%region_9.11 | all-reduce | flops 8192 | bytes 65536 | tf_op jit(solution)/shard_map/psum | solution.py:44
  334.0 4.9 fusion.8
  338.9 0.8 copy-done.2
  339.7 1.6 fusion.9
  341.4 99.3 %psum.37 = f32[8192]{0:T(1024)S(1)} all-reduce(f32[8192]{0:T(1024)S(1)} %fusion.9), channel_id=1, replica_groups=mesh['grp'=16,'dev'=32] {'grp','dev'}, use_global_device_ids=true, to_apply=%region_12.14 | all-reduce | flops 8192 | bytes 65536 | tf_op jit(solution)/shard_map/psum | solution.py:48
  440.7 4.6 fusion.10
  445.3 4.6 fusion.11
  449.9 100.3 %psum.38 = f32[8192]{0:T(1024)S(1)} all-reduce(f32[8192]{0:T(1024)S(1)} %fusion.11), channel_id=1, replica_groups=mesh['grp'=16,'dev'=32] {'grp','dev'}, use_global_device_ids=true, to_apply=%region_15.17 | all-reduce | flops 8192 | bytes 65536 | tf_op jit(solution)/shard_map/psum | solution.py:48
  550.2 11.0 %multiply_reduce_fusion = (f32[]{:T(128)}, f32[8192]{0:T(1024)S(1)}, f32[8192,256]{0,1:T(8,128)}) fusion(f32[8192,256]{0,1:T(8,128)} %copy-done.1, f32[8192]{0:T(1024)S(1)} %psum.38, f32[256]{0:T(256)S(1)} %fusion.10, f32[8192]{0:T(1024)S(1)} %psum.37, f32[256]{0:T(256)S(1)} %fusion.8, f32[8192]{0:T(1024)S(1)} %psum.36, f32[256]{0:T(256)S(1)} %get-tuple-element.13, ...), kind=kOutput, calls=%fused_computation.15 | convolution fusion | flops 1094901760 | bytes 21237764 | tf_op jit(solution)/shard_map/dot_general | solution.py:15
  561.2 99.9 %all-reduce = (f32[8192]{0:T(1024)S(1)}, f32[]{:T(128)}) all-reduce(f32[8192]{0:T(1024)S(1)} %get-tuple-element.6, f32[]{:T(128)} %get-tuple-element.5), channel_id=1, replica_groups=mesh['grp'=16,'dev'=32] {'grp','dev'}, use_global_device_ids=true, to_apply=%region_4.6 | all-reduce | flops 8193 | bytes 65544 | tf_op jit(solution)/shard_map/psum | solution.py:50
  661.1 0.6 log_reduce_fusion
  661.7 10.4 %fusion.16 = (f32[256]{0:T(256)S(1)}, f32[256,256]{0,1:T(8,128)S(1)}) fusion(bf16[256,256]{0,1:T(8,128)(2,1)S(1)} %copy.7, f32[256]{0:T(256)S(1)} %add_rsqrt_fusion.1, bf16[2,8192,256]{2,1,0:T(8,128)(2,1)} %all-gather.2.cloned.1.call-done, f32[8192,256]{0,1:T(8,128)} %get-tuple-element.15, f32[8192]{0:T(1024)S(1)} %get-tuple-element.9, ...), kind=kOutput, calls=%fused_computation.32 | convolution fusion | flops 1094975232 | bytes 21500928 | tf_op jit(solution)/shard_map/dot_general | solution.py:54
  672.1 0.8 copy.9
  (14 shorter events, 0.5 us)
Async XLA Ops:
  7.2 1.4 copy-start
  7.2 217.6 %all-gather.2.cloned.1.call-start = ((), (), s32[]{:S(2)}) async-start(), calls=%async_computation | async-start | bytes 8404992 | tf_op jit(solution)/shard_map/all_gather | solution.py:29
  228.3 3.2 copy-start.1
  334.0 5.8 copy-start.2
Sparse Core Ops, SparseCore 0:
  13.2 211.5 all-gather.1
where the time goes:
time: 683 us; the launch traced here: 682 us
  blocking collectives  401 us (59%)
  waiting for transfers between devices  211 us (31%)
  matrix products  24.9 us (4%)
  other arithmetic  20.8 us (3%)
  between operations  16.5 us (2%)
  local copies, waits for them, and re-layouts  7.97 us (1%)
    all_gather x1, waiting for transfers between devices, per_device(): gathered = lax.all_gather(stacked, ('grp', 'dev'), axis=1, tiled=True)  211 us
    psum x2, blocking collectives, per_device(): row_total = lax.psum(jnp.sum(targets, axis=1), ('grp', 'dev'))  200 us
    psum x1, blocking collectives, per_device(): first_total = lax.psum(first_part, ('grp', 'dev'))  101 us
    psum x1, blocking collectives, per_device(): total = lax.psum(student_part, ('grp', 'dev'))  99.9 us
    dot_general x2, matrix products, scores(): lax.dot_general(rows, weights, (((1,), (1,)), ((), ())), preferred_elemen...  14.5 us
  transfers between devices with their start and end apart: 1, of which 1 were waited for; matrix products, arithmetic and copies ran while one was open for 0% of the time, Pallas kernels for 0%

commit v1 on v0

v1 whole, which is shorter than its diff:
```python
import jax
import jax.numpy as jnp
from jax import lax
from jax.experimental import pallas as pl
from jax.experimental.pallas import tpu as pltpu
from jax.sharding import Mesh, PartitionSpec as P

ITERS = 3
LANES = 128

norm_eps = 1e-06
teacher_scale = 1.0 / 0.07
student_scale = 1.0 / 0.1

f32 = jnp.float32
bf16 = jnp.bfloat16
NT = (((1,), (1,)), ((), ()))
NN = (((1,), (0,)), ((), ()))


def dot(a, b, dims):
    return lax.dot_general(a, b, dims, preferred_element_type=f32)


def unit_rows(values):
    values = values.astype(f32)
    return values * lax.rsqrt(jnp.sum(values * values, axis=1, keepdims=True) + norm_eps)


def fold(row):
    n = row.shape[1] // LANES
    return jnp.concatenate([row[:, LANES * i : LANES * (i + 1)] for i in range(n)], axis=0)


def unfold(tile):
    return jnp.concatenate([tile[i : i + 1, :] for i in range(tile.shape[0])], axis=1)


def split_rows(row):
    high = row.astype(bf16).astype(f32)
    which = lax.broadcasted_iota(jnp.int32, (16, row.shape[1]), 0)
    return jnp.where(which == 0, high, jnp.where(which == 1, row - high, 0.0)).astype(bf16)


def matvec(row, matrix, dims):
    return jnp.sum(dot(split_rows(row), matrix, dims), axis=0, keepdims=True)


def spread(out_ref, tile):
    for i in range(out_ref.shape[0]):
        out_ref[i] = tile


def total_of(parts_ref):
    total = parts_ref[0]
    for i in range(1, parts_ref.shape[0]):
        total = total + parts_ref[i]
    return total


def prepare_kernel(mask_ref, sp_ref, tp_ref, sw_ref, tw_ref, rows_ref, weights_ref):
    count = mask_ref.shape[0]
    patches = sp_ref.shape[0]
    which = lax.broadcasted_iota(jnp.int32, (count, patches), 0)
    wanted = jnp.zeros((count, patches), jnp.int32)
    for i in range(count):
        wanted = jnp.where(which == i, mask_ref[i], wanted)
    onehot = (lax.broadcasted_iota(jnp.int32, (count, patches), 1) == wanted).astype(f32).astype(bf16)
    teacher = unit_rows(dot(onehot, tp_ref[...], NN)).astype(bf16)
    student = unit_rows(dot(onehot, sp_ref[...], NN)).astype(bf16)
    for i in range(rows_ref.shape[0]):
        rows_ref[i, :count] = teacher
        rows_ref[i, count:] = student
    weights_ref[0] = unit_rows(tw_ref[...]).astype(bf16)
    weights_ref[1] = unit_rows(sw_ref[...]).astype(bf16)


def divide_kernel(rows_ref, teacher_ref, student_ref):
    n, both, _ = rows_ref.shape
    count = both // 2
    for i in range(n):
        student_ref[count * i : count * (i + 1)] = rows_ref[i, count:]
        for j in range(teacher_ref.shape[0]):
            teacher_ref[j, count * i : count * (i + 1)] = rows_ref[i, :count]


def first_kernel(rows_ref, weights_ref, expo_ref, column_ref):
    groups, count, _ = rows_ref.shape
    width = weights_ref.shape[2]
    for i in range(weights_ref.shape[0]):
        for j in range(groups):
            score = dot(weights_ref[i, 0], rows_ref[j], NT) * teacher_scale
            expo_ref[width * i : width * (i + 1), count * j : count * (j + 1)] = jnp.exp(score).astype(bf16)
    ones = jnp.ones((1, groups * count), f32)
    spread(column_ref, fold(matvec(ones, expo_ref[...], NT)))


def column_kernel(parts_ref, expo_ref, column_ref):
    row = unfold(1.0 / total_of(parts_ref))
    spread(column_ref, fold(matvec(row, expo_ref[...], NT)))


def row_kernel(parts_ref, expo_ref, out_ref):
    column = unfold(1.0 / total_of(parts_ref))
    spread(out_ref, fold(matvec(column, expo_ref[...], NN)))


def student_kernel(rows_ref, weights_ref, expo_ref, product_ref, total_ref):
    groups, count, _ = rows_ref.shape
    width = weights_ref.shape[2]
    for j in range(groups):
        total = jnp.zeros((1, count), f32)
        for i in range(weights_ref.shape[0]):
            logits = dot(weights_ref[i, 1], rows_ref[j], NT) * student_scale
            total = total + jnp.sum(jnp.exp(logits), axis=0, keepdims=True)
            place = (slice(width * i, width * (i + 1)), slice(count * j, count * (j + 1)))
            product_ref[place] = (expo_ref[place].astype(f32) * logits).astype(bf16)
        per = count // LANES
        total_ref[per * j : per * (j + 1)] = fold(total)


def last_row_kernel(parts_ref, expo_ref, product_ref, total_ref, out_ref):
    column = unfold(1.0 / total_of(parts_ref))
    sums = fold(matvec(column, expo_ref[...], NN))
    cross = fold(matvec(column, product_ref[...], NN))
    spread(out_ref, jnp.concatenate([sums, cross, total_ref[...]], axis=0))


def add_kernel(parts_ref, out_ref):
    spread(out_ref, total_of(parts_ref))


def slope_kernel(parts_ref, column_ref, trows_ref, srows_ref, weights_ref, out_ref):
    groups, count, _ = trows_ref.shape
    n, _, width, depth = weights_ref.shape
    lines = groups * count // LANES
    sums = total_of(parts_ref)
    row = 1.0 / sums[:lines]
    student_total = sums[2 * lines :]
    partial = jnp.sum(jnp.log(student_total)) - jnp.sum(row * sums[lines : 2 * lines])
    row = unfold(row)
    inverse = unfold(1.0 / student_total)
    column = unfold(1.0 / total_of(column_ref))
    column = jnp.broadcast_to(column, (8, n * width)).T[:, 0:1]
    for i in range(n):
        grad = jnp.zeros((width, depth), f32)
        for j in range(groups):
            place = slice(count * j, count * (j + 1))
            target = jnp.exp(dot(weights_ref[i, 0], trows_ref[j], NT) * teacher_scale)
            expo = jnp.exp(dot(weights_ref[i, 1], srows_ref[j], NT) * student_scale)
            target = target * column[width * i : width * (i + 1)] * row[:, place]
            slope = ((expo * inverse[:, place] - target) * student_scale).astype(bf16)
            grad = grad + dot(slope, srows_ref[j], NN)
        out_ref[i, :width] = grad.astype(bf16)
    partial = jnp.full((16, depth), partial, f32)
    high = partial.astype(bf16).astype(f32)
    middle = (partial - high).astype(bf16).astype(f32)
    which = lax.broadcasted_iota(jnp.int32, (16, depth), 0)
    pieces = jnp.where(which == 0, high, jnp.where(which == 1, middle, jnp.where(which == 2, partial - high - middle, 0.0)))
    for i in range(n):
        out_ref[i, width:] = pieces.astype(bf16)


def finish_kernel(rows, parts_ref, proto_ref, loss_ref, grad_ref):
    width = proto_ref.shape[0]
    unit_grad = parts_ref[0, :width].astype(f32)
    pieces = parts_ref[0, width:].astype(f32)
    for i in range(1, parts_ref.shape[0]):
        unit_grad = unit_grad + parts_ref[i, :width].astype(f32)
        pieces = pieces + parts_ref[i, width:].astype(f32)
    loss_ref[...] = jnp.sum(pieces, axis=0, keepdims=True)[:, :LANES] / rows
    proto = proto_ref[...].astype(f32)
    scale = lax.rsqrt(jnp.sum(proto * proto, axis=1, keepdims=True) + norm_eps)
    unit = proto * scale
    grad_ref[...] = (unit_grad - unit * jnp.sum(unit * unit_grad, axis=1, keepdims=True)) * scale


def call(kernel, outs, *args, smem=()):
    vmem = pl.BlockSpec(memory_space=pltpu.VMEM)
    return pl.pallas_call(
        kernel,
        out_shape=outs,
        in_specs=[pl.BlockSpec(memory_space=pltpu.SMEM) if i in smem else vmem for i in range(len(args))],
        out_specs=jax.tree.map(lambda _: vmem, outs),
        compiler_params=pltpu.CompilerParams(vmem_limit_bytes=40 * 1024 * 1024),
    )(*args)


def per_device(nz, ny, nx, nc, student_patches, teacher_patches, mask_rows, student_proto, teacher_proto):
    shape = jax.ShapeDtypeStruct
    count = mask_rows.shape[0]
    width, depth = student_proto.shape
    near = ny * nc
    rows = count * nz * near
    columns = width * nx
    row_lines, column_lines = rows // LANES, columns // LANES

    def exchange(values, axes):
        return lax.all_to_all(values, axes, 0, 0, tiled=True)

    picked, weights = call(
        prepare_kernel,
        (shape((nz, 2 * count, depth), bf16), shape((2, width, depth), bf16)),
        mask_rows, student_patches, teacher_patches, student_proto, teacher_proto, smem=(0,),
    )
    weights = lax.all_gather(weights, "x", axis=0, tiled=False)
    picked = exchange(picked, "z")
    teacher_local, student_local = call(
        divide_kernel,
        (shape((near, nz * count, depth), bf16), shape((nz * count, depth), bf16)),
        picked,
    )
    student_rows = lax.all_gather(student_local, ("y", "c"), axis=0, tiled=False)
    teacher_rows = exchange(teacher_local, ("y", "c"))
    student_rows = student_rows.reshape(teacher_rows.shape)

    column_out = shape((nx, column_lines, LANES), f32)
    expo, column = call(
        first_kernel, (shape((columns, rows), bf16), column_out), teacher_rows, weights
    )
    for step in range(ITERS):
        if step:
            column = call(column_kernel, column_out, row, expo)
        column = exchange(column, "x")
        lines = row_lines
        if step < ITERS - 1:
            row = call(row_kernel, shape((near, lines, LANES), f32), column, expo)
        else:
            product, student_total = call(
                student_kernel, (shape((columns, rows), bf16), shape((lines, LANES), f32)),
                student_rows, weights, expo,
            )
            lines = 3 * row_lines
            row = call(
                last_row_kernel, shape((near, lines, LANES), f32), column, expo, product, student_total
            )
        row = exchange(row, ("y", "c"))
        row = call(add_kernel, shape((nz, lines, LANES), f32), row)
        row = exchange(row, "z")
    grads = call(
        slope_kernel, shape((nx, width + 16, depth), bf16), row, column, teacher_rows, student_rows, weights
    )
    grads = exchange(grads, "x")
    loss, proto_grad = call(
        lambda *refs: finish_kernel(rows * nx, *refs),
        (shape((1, LANES), f32), shape((width, depth), f32)),
        grads, student_proto,
    )
    return (loss[0, 0], proto_grad)


def solution(mesh):
    nz = mesh.shape["grp"]
    ny, nx, nc = 4, 4, 2
    axes = ("z", "y", "x", "c")
    inner = Mesh(mesh.devices.reshape(nz, ny, nx, nc), axes)
    placed = (P(axes, None), P(axes, None), P(axes), P(axes, None), P(axes, None))
    return jax.shard_map(
        lambda *args: per_device(nz, ny, nx, nc, *args),
        mesh=inner,
        in_specs=placed,
        out_specs=(P(), P(axes, None)),
        check_vma=False,
    )
```

time: 683 us -> 226 us (0.33)
  the two profiles are of different devices: /device:TPU:1 before, /device:TPU:64 now
where the time goes in v1:
time: 226 us; the launch traced here: 225 us
  blocking collectives  153 us (68%)
  Pallas kernels  18.7 us (8%)
  waiting for transfers between devices  15.9 us (7%)
  local copies, waits for them, and re-layouts  15.3 us (7%)
  between operations  14.2 us (6%)
  starting transfers between devices  7.79 us (3%)
    all_to_all x10, blocking collectives, exchange(): return lax.all_to_all(values, axes, 0, 0, tiled=True)  153 us
    pallas_call x14, Pallas kernels, call(): pl.pallas_call(kernel, out_shape=outs, in_specs=[pl.BlockSpec(memory_spac...  18.7 us
    unnamed x30, local copies, waits for them, and re-layouts  15.3 us
    all_to_all x2, waiting for transfers between devices, exchange(): return lax.all_to_all(values, axes, 0, 0, tiled=True)  15.2 us
    all_to_all x2, starting transfers between devices, exchange(): return lax.all_to_all(values, axes, 0, 0, tiled=True)  7.72 us
  transfers between devices with their start and end apart: 4, of which 1 were waited for; matrix products, arithmetic and copies ran while one was open for 0% of the time, Pallas kernels for 4%

profile of v1, /device:TPU:64, one launch (start us, length us, event | category | flops | bytes accessed | tf_op | source)
XLA Modules:
  0.0 225.1 jit_solution(3698090258605806521)
XLA Ops:
  11.5 1.5 shard_map.68
  13.0 32.7 %all_to_all.60.rows_ref = bf16[16,32,256]{2,1,0:T(8,128)(2,1)S(1)} all-to-all(bf16[16,32,256]{2,1,0:T(8,128)(2,1)S(1)} %get-tuple-element.12), channel_id=1, replica_groups=mesh['z'=16,'y'=4,'x'=4,'c'=2] {'z'}, dimensions={0} | all-to-all | bytes 524288 | tf_op jit(solution)/shard_map/all_to_all | solution.py:199
  46.8 4.5 %all-to-all-start.1 = ((bf16[8,256,256]{2,1,0:T(8,128)(2,1)}), bf16[8,256,256]{2,1,0:T(8,128)(2,1)S(1)}, u32[]{:S(2)}, u32[]{:S(2)}) async-start(bf16[8,256,256]{2,1,0:T(8,128)(2,1)} %get-tuple-element.13), calls=%async_computation.1 | async-start | bytes 2097152 | tf_op jit(solution)/shard_map/all_to_all | solution.py:199
  52.1 15.2 %all-to-all-done.1.rows_ref.trows_ref = bf16[8,256,256]{2,1,0:T(8,128)(2,1)S(1)} async-done(((bf16[8,256,256]{2,1,0:T(8,128)(2,1)}), bf16[8,256,256]{2,1,0:T(8,128)(2,1)S(1)}, u32[]{:S(2)}, u32[]{:S(2)}) %all-to-all-start.1) | async-done | bytes 1048608 | tf_op jit(solution)/shard_map/all_to_all | solution.py:199
  67.3 1.2 copy-done.3
  68.5 2.5 %shard_map.70 = (bf16[1024,2048]{1,0:T(8,128)(2,1)S(1)}, f32[4,8,128]{2,1,0:T(8,128)S(1)}) custom-call(bf16[8,256,256]{2,1,0:T(8,128)(2,1)S(1)} %all-to-all-done.1.rows_ref.trows_ref, bf16[4,2,256,256]{3,2,1,0:T(8,128)(2,1)S(1)} %bitcast.4), custom_call_target="tpu_custom_call" | custom-call | tf_op jit(solution)/shard_map/pallas_call | solution.py:180
  71.0 9.5 %all_to_all.61.parts_ref = f32[4,8,128]{2,1,0:T(8,128)S(1)} all-to-all(f32[4,8,128]{2,1,0:T(8,128)S(1)} %get-tuple-element.15), channel_id=1, replica_groups=mesh['z'=16,'y'=4,'x'=4,'c'=2] {'x'}, dimensions={0} | all-to-all | bytes 32768 | tf_op jit(solution)/shard_map/all_to_all | solution.py:199
  81.1 8.0 %all_to_all.62.parts_ref = f32[8,16,128]{2,1,0:T(8,128)S(1)} all-to-all(f32[8,16,128]{2,1,0:T(8,128)S(1)} %shard_map.71), channel_id=1, replica_groups=mesh['z'=16,'y'=4,'x'=4,'c'=2] {'y','c'}, dimensions={0} | all-to-all | bytes 131072 | tf_op jit(solution)/shard_map/all_to_all | solution.py:199
  89.2 19.1 %all_to_all.63.parts_ref = f32[16,16,128]{2,1,0:T(8,128)S(1)} all-to-all(f32[16,16,128]{2,1,0:T(8,128)S(1)} %shard_map.72), channel_id=1, replica_groups=mesh['z'=16,'y'=4,'x'=4,'c'=2] {'z'}, dimensions={0} | all-to-all | bytes 262144 | tf_op jit(solution)/shard_map/all_to_all | solution.py:199
  109.5 7.7 %all_to_all.64.parts_ref = f32[4,8,128]{2,1,0:T(8,128)S(1)} all-to-all(f32[4,8,128]{2,1,0:T(8,128)S(1)} %shard_map.73), channel_id=1, replica_groups=mesh['z'=16,'y'=4,'x'=4,'c'=2] {'x'}, dimensions={0} | all-to-all | bytes 32768 | tf_op jit(solution)/shard_map/all_to_all | solution.py:199
  117.9 8.4 %all_to_all.65.parts_ref = f32[8,16,128]{2,1,0:T(8,128)S(1)} all-to-all(f32[8,16,128]{2,1,0:T(8,128)S(1)} %shard_map.74), channel_id=1, replica_groups=mesh['z'=16,'y'=4,'x'=4,'c'=2] {'y','c'}, dimensions={0} | all-to-all | bytes 131072 | tf_op jit(solution)/shard_map/all_to_all | solution.py:199
  126.3 17.8 %all_to_all.66.parts_ref = f32[16,16,128]{2,1,0:T(8,128)S(1)} all-to-all(f32[16,16,128]{2,1,0:T(8,128)S(1)} %shard_map.75), channel_id=1, replica_groups=mesh['z'=16,'y'=4,'x'=4,'c'=2] {'z'}, dimensions={0} | all-to-all | bytes 262144 | tf_op jit(solution)/shard_map/all_to_all | solution.py:199
  144.1 1.8 shard_map.76
  145.9 3.3 %all-to-all-start.8 = ((f32[4,8,128]{2,1,0:T(8,128)}), f32[4,8,128]{2,1,0:T(8,128)S(1)}, u32[]{:S(2)}, u32[]{:S(2)}) async-start(f32[4,8,128]{2,1,0:T(8,128)} %shard_map.76), calls=%async_computation.8 | async-start | bytes 32768 | tf_op jit(solution)/shard_map/all_to_all | solution.py:199
  149.2 2.2 copy-done.1
  151.4 1.2 copy-done.7
  152.6 2.0 shard_map.77
  154.7 2.0 copy-done.5
  156.7 2.2 copy-done.2
  158.9 2.2 copy-done.6
  162.3 9.4 %all_to_all.67.parts_ref = f32[8,48,128]{2,1,0:T(8,128)S(1)} all-to-all(f32[8,48,128]{2,1,0:T(8,128)S(1)} %shard_map.78), channel_id=1, replica_groups=mesh['z'=16,'y'=4,'x'=4,'c'=2] {'y','c'}, dimensions={0} | all-to-all | bytes 393216 | tf_op jit(solution)/shard_map/all_to_all | solution.py:199
  171.7 27.7 %all_to_all.68.parts_ref = f32[16,48,128]{2,1,0:T(8,128)S(1)} all-to-all(f32[16,48,128]{2,1,0:T(8,128)S(1)} %shard_map.79), channel_id=1, replica_groups=mesh['z'=16,'y'=4,'x'=4,'c'=2] {'z'}, dimensions={0} | all-to-all | bytes 786432 | tf_op jit(solution)/shard_map/all_to_all | solution.py:199
  199.4 5.1 %shard_map.80 = bf16[4,272,256]{2,1,0:T(8,128)(2,1)S(1)} custom-call(f32[16,48,128]{2,1,0:T(8,128)S(1)} %all_to_all.68.parts_ref, f32[4,8,128]{2,1,0:T(8,128)S(1)} %all-to-all-done.8.parts_ref.column_ref, bf16[8,256,256]{2,1,0:T(8,128)(2,1)S(1)} %all-to-all-done.1.rows_ref.trows_ref, bf16[8,256,256]{2,1,0:T(8,128)(2,1)S(1)} %bitcast.8, ...), custom_call_target="tpu_custom_call" | custom-call | tf_op jit(solution)/shard_map/pallas_call | solution.py:180
  204.5 12.8 %all_to_all.69.refs_0_ = bf16[4,272,256]{2,1,0:T(8,128)(2,1)S(1)} all-to-all(bf16[4,272,256]{2,1,0:T(8,128)(2,1)S(1)} %shard_map.80), channel_id=1, replica_groups=mesh['z'=16,'y'=4,'x'=4,'c'=2] {'x'}, dimensions={0} | all-to-all | bytes 1114112 | tf_op jit(solution)/shard_map/all_to_all | solution.py:199
  (40 shorter events, 11.0 us)
Async XLA Ops:
  7.2 44.9 %all-gather.5.cloned.1.call-start = ((), (), s32[]{:S(2)}) async-start(), calls=%async_computation.12 | async-start | bytes 1310720 | tf_op jit(solution)/shard_map/all_gather | solution.py:206
  7.2 0.9 copy-start.9
  8.1 0.9 copy-start.11
  9.0 0.9 copy-start.12
  9.9 0.9 copy-start.13
  10.8 0.7 copy-start.14
  46.8 20.4 %all-to-all-start.1 = ((bf16[8,256,256]{2,1,0:T(8,128)(2,1)}), bf16[8,256,256]{2,1,0:T(8,128)(2,1)S(1)}, u32[]{:S(2)}, u32[]{:S(2)}) async-start(bf16[8,256,256]{2,1,0:T(8,128)(2,1)} %get-tuple-element.13), calls=%async_computation.1 | async-start | bytes 2097152 | tf_op jit(solution)/shard_map/all_to_all | solution.py:199
  51.3 97.9 %all-gather.7.cloned.1.call-start = ((), (), s32[]{:S(2)}) async-start(), calls=%async_computation.13 | async-start | bytes 1179648 | tf_op jit(solution)/shard_map/all_gather | solution.py:213
  67.3 1.2 copy-start.3
  71.0 73.1 %copy-start = (bf16[1024,2048]{1,0:T(8,128)(2,1)}, bf16[1024,2048]{1,0:T(8,128)(2,1)S(1)}, u32[]{:S(2)}) copy-start(bf16[1024,2048]{1,0:T(8,128)(2,1)S(1)} %get-tuple-element.16.expo_ref) | copy-start | bytes 12582916
  117.2 32.0 %copy-start.4 = (bf16[8,256,256]{2,1,0:T(8,128)(2,1)S(1)}, bf16[8,256,256]{2,1,0:T(8,128)(2,1)}, u32[]{:S(2)}) copy-start(bf16[8,256,256]{2,1,0:T(8,128)(2,1)} %all-gather.5.cloned.1.call-done) | copy-start | bytes 3145732
  145.9 10.8 %all-to-all-start.8 = ((f32[4,8,128]{2,1,0:T(8,128)}), f32[4,8,128]{2,1,0:T(8,128)S(1)}, u32[]{:S(2)}, u32[]{:S(2)}) async-start(f32[4,8,128]{2,1,0:T(8,128)} %shard_map.76), calls=%async_computation.8 | async-start | bytes 32768 | tf_op jit(solution)/shard_map/all_to_all | solution.py:199
  149.2 2.2 copy-start.1
  151.4 1.2 copy-start.7
  154.7 2.0 copy-start.5
  156.7 2.2 copy-start.2
  158.9 2.2 copy-start.6
  161.1 38.3 %copy-start.8 = (bf16[2048,256]{1,0:T(8,128)(2,1)S(1)}, bf16[2048,256]{1,0:T(8,128)(2,1)}, u32[]{:S(2)}) copy-start(bf16[2048,256]{1,0:T(8,128)(2,1)} %all-gather.7.cloned.1.call-done) | copy-start | bytes 3145732
  162.3 55.0 %copy-start.10 = (bf16[256,256]{1,0:T(8,128)(2,1)S(1)}, bf16[256,256]{1,0:T(8,128)(2,1)}, u32[]{:S(2)}) copy-start(bf16[256,256]{1,0:T(8,128)(2,1)} %refs_1_.1) | copy-start | bytes 393220
Sparse Core Ops, SparseCore 0:
  13.1 35.3 all-gather.4
  54.3 27.8 all-gather.6

commit v2 on v1

--- a/solution.py
+++ b/solution.py
@@ -5,7 +5,6 @@
 from jax.experimental.pallas import tpu as pltpu
 from jax.sharding import Mesh, PartitionSpec as P
 
-ITERS = 3
 LANES = 128
 
 norm_eps = 1e-06
@@ -58,21 +57,41 @@
     return total
 
 
-def prepare_kernel(mask_ref, sp_ref, tp_ref, sw_ref, tw_ref, rows_ref, weights_ref):
+def rows_kernel(mask_ref, sp_ref, tp_ref, rows_ref, mask, sp, tp, sems):
+    copies = [
+        pltpu.make_async_copy(source, target, sems.at[i])
+        for i, (source, target) in enumerate(((mask_ref, mask), (tp_ref, tp), (sp_ref, sp)))
+    ]
+    for copy in copies:
+        copy.start()
     count = mask_ref.shape[0]
     patches = sp_ref.shape[0]
+    copies[0].wait()
     which = lax.broadcasted_iota(jnp.int32, (count, patches), 0)
     wanted = jnp.zeros((count, patches), jnp.int32)
     for i in range(count):
-        wanted = jnp.where(which == i, mask_ref[i], wanted)
+        wanted = jnp.where(which == i, mask[i], wanted)
     onehot = (lax.broadcasted_iota(jnp.int32, (count, patches), 1) == wanted).astype(f32).astype(bf16)
-    teacher = unit_rows(dot(onehot, tp_ref[...], NN)).astype(bf16)
-    student = unit_rows(dot(onehot, sp_ref[...], NN)).astype(bf16)
+    copies[1].wait()
+    teacher = unit_rows(dot(onehot, tp[...], NN)).astype(bf16)
+    copies[2].wait()
+    student = unit_rows(dot(onehot, sp[...], NN)).astype(bf16)
     for i in range(rows_ref.shape[0]):
         rows_ref[i, :count] = teacher
         rows_ref[i, count:] = student
-    weights_ref[0] = unit_rows(tw_ref[...]).astype(bf16)
-    weights_ref[1] = unit_rows(sw_ref[...]).astype(bf16)
+
+
+def weights_kernel(tw_ref, sw_ref, weights_ref, tw, sw, sems):
+    copies = [
+        pltpu.make_async_copy(source, target, sems.at[i])
+        for i, (source, target) in enumerate(((tw_ref, tw), (sw_ref, sw)))
+    ]
+    for copy in copies:
+        copy.start()
+    copies[0].wait()
+    weights_ref[0] = unit_rows(tw[...]).astype(bf16)
+    copies[1].wait()
+    weights_ref[1] = unit_rows(sw[...]).astype(bf16)
 
 
 def divide_kernel(rows_ref, teacher_ref, student_ref):
@@ -105,51 +124,108 @@
     spread(out_ref, fold(matvec(column, expo_ref[...], NN)))
 
 
-def student_kernel(rows_ref, weights_ref, expo_ref, product_ref, total_ref):
+def load_kernel(gathered_ref, out_ref, sem):
+    copy = pltpu.make_async_copy(gathered_ref, out_ref, sem.at[0])
+    copy.start()
+    copy.wait()
+
+
+def student_kernel(rows_ref, weights_ref, expo_ref, total_ref, rows_t_ref, weights_t_ref):
     groups, count, _ = rows_ref.shape
     width = weights_ref.shape[2]
     for j in range(groups):
+        lanes = slice(count * j, count * (j + 1))
+        rows_t_ref[:, lanes] = rows_ref[j].astype(f32).T.astype(bf16)
         total = jnp.zeros((1, count), f32)
         for i in range(weights_ref.shape[0]):
-            logits = dot(weights_ref[i, 1], rows_ref[j], NT) * student_scale
-            total = total + jnp.sum(jnp.exp(logits), axis=0, keepdims=True)
-            place = (slice(width * i, width * (i + 1)), slice(count * j, count * (j + 1)))
-            product_ref[place] = (expo_ref[place].astype(f32) * logits).astype(bf16)
+            expo = jnp.exp(dot(weights_ref[i, 1], rows_ref[j], NT) * student_scale)
+            total = total + jnp.sum(expo, axis=0, keepdims=True)
+            expo_ref[width * i : width * (i + 1), lanes] = expo.astype(bf16)
         per = count // LANES
         total_ref[per * j : per * (j + 1)] = fold(total)
-
-
-def last_row_kernel(parts_ref, expo_ref, product_ref, total_ref, out_ref):
+    for i in range(weights_ref.shape[0]):
+        weights_t_ref[:, width * i : width * (i + 1)] = weights_ref[i, 1].astype(f32).T.astype(bf16)
+
+
+def second_row_kernel(parts_ref, expo_ref, total_ref, out_ref, kept_ref, sems):
+    pieces = sems.shape[0]
+    height = expo_ref.shape[0] // pieces
+    copies = [
+        pltpu.make_async_copy(expo_ref.at[pl.ds(height * i, height)], kept_ref.at[pl.ds(height * i, height)], sems.at[i])
+        for i in range(pieces)
+    ]
+    for copy in copies:
+        copy.start()
     column = unfold(1.0 / total_of(parts_ref))
-    sums = fold(matvec(column, expo_ref[...], NN))
-    cross = fold(matvec(column, product_ref[...], NN))
-    spread(out_ref, jnp.concatenate([sums, cross, total_ref[...]], axis=0))
+    sums = jnp.zeros((1, expo_ref.shape[1]), f32)
+    for i in range(pieces):
+        copies[i].wait()
+        place = slice(height * i, height * (i + 1))
+        sums = sums + matvec(column[:, place], kept_ref[place], NN)
+    spread(out_ref, jnp.concatenate([fold(sums), total_ref[...]], axis=0))
+
+
+def last_row_kernel(parts_ref, expo_ref, rows_t_ref, weights_t_ref, out_ref):
+    column = unfold(1.0 / total_of(parts_ref))
+    weighted = (weights_t_ref[...].astype(f32) * column).astype(bf16)
+    both = dot(jnp.concatenate([split_rows(column), weighted], axis=0), expo_ref[...], NN)
+    sums = jnp.sum(both[:16], axis=0, keepdims=True)
+    cross = jnp.sum(both[16:] * rows_t_ref[...].astype(f32), axis=0, keepdims=True) * student_scale
+    spread(out_ref, jnp.concatenate([fold(sums), fold(cross)], axis=0))
 
 
 def add_kernel(parts_ref, out_ref):
     spread(out_ref, total_of(parts_ref))
 
 
-def slope_kernel(parts_ref, column_ref, trows_ref, srows_ref, weights_ref, out_ref):
-    groups, count, _ = trows_ref.shape
-    n, _, width, depth = weights_ref.shape
-    lines = groups * count // LANES
-    sums = total_of(parts_ref)
-    row = 1.0 / sums[:lines]
-    student_total = sums[2 * lines :]
-    partial = jnp.sum(jnp.log(student_total)) - jnp.sum(row * sums[lines : 2 * lines])
-    row = unfold(row)
-    inverse = unfold(1.0 / student_total)
+def add_two_kernel(parts_ref, out_ref):
+    total = total_of(parts_ref)
+    lines = total.shape[0] // 2
+    sums = total[:lines]
+    high = sums.astype(bf16)
+    spread(out_ref, jnp.concatenate([high, (sums - high.astype(f32)).astype(bf16), total[lines:].astype(bf16)], axis=0))
+
+
+def halves_of(parts_ref):
+    total = parts_ref[0].astype(f32)
+    for i in range(1, parts_ref.shape[0]):
+        total = total + parts_ref[i].astype(f32)
+    lines = total.shape[0] // 3
+    return total[:lines] + total[lines : 2 * lines], total[2 * lines :]
+
+
+def third_column_kernel(parts_ref, expo_ref, column_ref, total_ref):
+    sums, total = halves_of(parts_ref)
+    spread(column_ref, fold(matvec(unfold(1.0 / sums), expo_ref[...], NT)))
+    total_ref[...] = total
+
+
+def slope_kernel(parts_ref, column_ref, total_ref, target_ref, expo_ref, srows_ref, out_ref, expo, sems):
+    groups, count, depth = srows_ref.shape
+    n = out_ref.shape[0]
+    width = target_ref.shape[0] // n
+    copies = [
+        pltpu.make_async_copy(expo_ref.at[pl.ds(width * i, width)], expo.at[pl.ds(width * i, width)], sems.at[i])
+        for i in range(n)
+    ]
+    for copy in copies:
+        copy.start()
+    sums, cross = halves_of(parts_ref)
+    row = 1.0 / sums
+    student_total = total_ref[...]
+    partial = jnp.sum(jnp.log(student_total)) - jnp.sum(row * cross)
+    row = unfold(row * student_scale)
+    inverse = unfold(student_scale / student_total)
     column = unfold(1.0 / total_of(column_ref))
     column = jnp.broadcast_to(column, (8, n * width)).T[:, 0:1]
     for i in range(n):
+        copies[i].wait()
         grad = jnp.zeros((width, depth), f32)
         for j in range(groups):
-            place = slice(count * j, count * (j + 1))
-            target = jnp.exp(dot(weights_ref[i, 0], trows_ref[j], NT) * teacher_scale)
-            expo = jnp.exp(dot(weights_ref[i, 1], srows_ref[j], NT) * student_scale)
-            target = target * column[width * i : width * (i + 1)] * row[:, place]
-            slope = ((expo * inverse[:, place] - target) * student_scale).astype(bf16)
+            lanes = slice(count * j, count * (j + 1))
+            place = (slice(width * i, width * (i + 1)), lanes)
+            target = target_ref[place].astype(f32) * column[width * i : width * (i + 1)] * row[:, lanes]
+            slope = (expo[place].astype(f32) * inverse[:, lanes] - target).astype(bf16)
             grad = grad + dot(slope, srows_ref[j], NN)
         out_ref[i, :width] = grad.astype(bf16)
     partial = jnp.full((16, depth), partial, f32)
@@ -175,33 +251,53 @@
     grad_ref[...] = (unit_grad - unit * jnp.sum(unit * unit_grad, axis=1, keepdims=True)) * scale
 
 
-def call(kernel, outs, *args, smem=()):
+def call(kernel, outs, *args, place=None, scratch=(), limit=20):
     vmem = pl.BlockSpec(memory_space=pltpu.VMEM)
+    place = place or {}
     return pl.pallas_call(
         kernel,
         out_shape=outs,
-        in_specs=[pl.BlockSpec(memory_space=pltpu.SMEM) if i in smem else vmem for i in range(len(args))],
+        in_specs=[pl.BlockSpec(memory_space=place[i]) if i in place else vmem for i in range(len(args))],
         out_specs=jax.tree.map(lambda _: vmem, outs),
-        compiler_params=pltpu.CompilerParams(vmem_limit_bytes=40 * 1024 * 1024),
+        scratch_shapes=scratch,
+        compiler_params=pltpu.CompilerParams(vmem_limit_bytes=limit * 1024 * 1024),
     )(*args)
 
 
 def per_device(nz, ny, nx, nc, student_patches, teacher_patches, mask_rows, student_proto, teacher_proto):
     shape = jax.ShapeDtypeStruct
+    held = pltpu.VMEM
     count = mask_rows.shape[0]
+    patches = student_patches.shape
     width, depth = student_proto.shape
     near = ny * nc
     rows = count * nz * near
     columns = width * nx
-    row_lines, column_lines = rows // LANES, columns // LANES
+    lines, column_lines = rows // LANES, columns // LANES
 
     def exchange(values, axes):
         return lax.all_to_all(values, axes, 0, 0, tiled=True)
 
-    picked, weights = call(
-        prepare_kernel,
-        (shape((nz, 2 * count, depth), bf16), shape((2, width, depth), bf16)),
-        mask_rows, student_patches, teacher_patches, student_proto, teacher_proto, smem=(0,),
+    def far(values):
+        return pltpu.with_memory_space_constraint(values, pltpu.HBM)
+
+    def sems(n):
+        return pltpu.SemaphoreType.DMA((n,))
+
+    picked = call(
+        rows_kernel,
+        shape((nz, 2 * count, depth), bf16),
+        far(mask_rows), far(student_patches), far(teacher_patches),
+        place={0: pltpu.HBM, 1: pltpu.HBM, 2: pltpu.HBM},
+        scratch=[pltpu.SMEM((count,), jnp.int32), pltpu.VMEM(patches, bf16), pltpu.VMEM(patches, bf16), sems(3)],
+    )
+    late_teacher, late_student, picked = lax.optimization_barrier((teacher_proto, student_proto, picked))
+    weights = call(
+        weights_kernel,
+        shape((2, width, depth), bf16),
+        far(late_teacher), far(late_student),
+        place={0: pltpu.HBM, 1: pltpu.HBM},
+        scratch=[pltpu.VMEM((width, depth), bf16), pltpu.VMEM((width, depth), bf16), sems(2)],
     )
     weights = lax.all_gather(weights, "x", axis=0, tiled=False)
     picked = exchange(picked, "z")
@@ -210,35 +306,55 @@
         (shape((near, nz * count, depth), bf16), shape((nz * count, depth), bf16)),
         picked,
     )
+    weights = call(
+        load_kernel, held(weights.shape, bf16), far(weights), place={0: pltpu.HBM}, scratch=[sems(1)]
+    )
     student_rows = lax.all_gather(student_local, ("y", "c"), axis=0, tiled=False)
     teacher_rows = exchange(teacher_local, ("y", "c"))
     student_rows = student_rows.reshape(teacher_rows.shape)
 
     column_out = shape((nx, column_lines, LANES), f32)
     expo, column = call(
-        first_kernel, (shape((columns, rows), bf16), column_out), teacher_rows, weights
-    )
-    for step in range(ITERS):
-        if step:
-            column = call(column_kernel, column_out, row, expo)
-        column = exchange(column, "x")
-        lines = row_lines
-        if step < ITERS - 1:
-            row = call(row_kernel, shape((near, lines, LANES), f32), column, expo)
-        else:
-            product, student_total = call(
-                student_kernel, (shape((columns, rows), bf16), shape((lines, LANES), f32)),
-                student_rows, weights, expo,
-            )
-            lines = 3 * row_lines
-            row = call(
-                last_row_kernel, shape((near, lines, LANES), f32), column, expo, product, student_total
-            )
-        row = exchange(row, ("y", "c"))
-        row = call(add_kernel, shape((nz, lines, LANES), f32), row)
-        row = exchange(row, "z")
+        first_kernel, (held((columns, rows), bf16), column_out), teacher_rows, weights
+    )
+    column = exchange(column, "x")
+    row = call(row_kernel, shape((near, lines, LANES), f32), column, expo)
+    row = exchange(row, ("y", "c"))
+    row = call(add_kernel, shape((nz, lines, LANES), f32), row)
+    row = exchange(row, "z")
+
+    column = call(column_kernel, column_out, row, expo)
+    student_rows, column = lax.optimization_barrier((student_rows, column))
+    student_expo, student_total, rows_t, weights_t = call(
+        student_kernel,
+        (shape((columns, rows), bf16), shape((lines, LANES), f32), shape((depth, rows), bf16), shape((depth, columns), bf16)),
+        student_rows, weights,
+    )
+    column = exchange(column, "x")
+    row, expo = call(
+        second_row_kernel,
+        (shape((near, 2 * lines, LANES), f32), held((columns, rows), bf16)),
+        column, far(expo), student_total,
+        place={1: pltpu.HBM},
+        scratch=[sems(4)],
+    )
+    row = exchange(row, ("y", "c"))
+    row = call(add_two_kernel, shape((nz, 3 * lines, LANES), bf16), row)
+    row = exchange(row, "z")
+
+    column, student_total = call(third_column_kernel, (column_out, shape((lines, LANES), f32)), row, expo)
+    column = exchange(column, "x")
+    row = call(last_row_kernel, shape((near, 2 * lines, LANES), f32), column, expo, rows_t, weights_t)
+    row = exchange(row, ("y", "c"))
+    row = call(add_two_kernel, shape((nz, 3 * lines, LANES), bf16), row)
+    row = exchange(row, "z")
+
     grads = call(
-        slope_kernel, shape((nx, width + 16, depth), bf16), row, column, teacher_rows, student_rows, weights
+        slope_kernel,
+        shape((nx, width + 16, depth), bf16),
+        row, column, student_total, expo, far(student_expo), student_rows,
+        place={4: pltpu.HBM},
+        scratch=[pltpu.VMEM((columns, rows), bf16), sems(nx)],
     )
     grads = exchange(grads, "x")
     loss, proto_grad = call(

time: 226 us -> 213 us (0.942)
  the two profiles are of different devices: /device:TPU:64 before, /device:TPU:32 now
where the time goes in v2:
time: 213 us; the launch traced here: 212 us
  blocking collectives  149 us (70%)
  Pallas kernels  22.8 us (11%)
  waiting for transfers between devices  15 us (7%)
  between operations  14.2 us (7%)
  starting transfers between devices  7.82 us (4%)
  local copies, waits for them, and re-layouts  3.2 us (2%)
    all_to_all x10, blocking collectives, exchange(): return lax.all_to_all(values, axes, 0, 0, tiled=True)  149 us
    pallas_call x16, Pallas kernels, call(): pl.pallas_call(kernel, out_shape=outs, in_specs=[pl.BlockSpec(memory_spac...  22.8 us
    all_to_all x2, waiting for transfers between devices, exchange(): return lax.all_to_all(values, axes, 0, 0, tiled=True)  14.9 us
    all_to_all x2, starting transfers between devices, exchange(): return lax.all_to_all(values, axes, 0, 0, tiled=True)  7.74 us
  transfers between devices with their start and end apart: 4, of which 2 were waited for; matrix products, arithmetic and copies ran while one was open for 0% of the time, Pallas kernels for 4%

profile of v2, /device:TPU:32, one launch (start us, length us, event | category | flops | bytes accessed | tf_op | source)
XLA Modules:
  0.0 212.4 jit_solution(2564866914042148545)
XLA Ops:
  7.2 1.4 shard_map.68
  8.6 1.9 shard_map.70
  10.6 32.9 %all_to_all.60.rows_ref = bf16[16,32,256]{2,1,0:T(8,128)(2,1)S(1)} all-to-all(bf16[16,32,256]{2,1,0:T(8,128)(2,1)S(1)} %shard_map.68), channel_id=1, replica_groups=mesh['z'=16,'y'=4,'x'=4,'c'=2] {'z'}, dimensions={0} | all-to-all | bytes 524288 | tf_op jit(solution)/shard_map/all_to_all | solution.py:279
  44.6 4.5 %all-to-all-start.1 = ((bf16[8,256,256]{2,1,0:T(8,128)(2,1)}), bf16[8,256,256]{2,1,0:T(8,128)(2,1)S(1)}, u32[]{:S(2)}, u32[]{:S(2)}) async-start(bf16[8,256,256]{2,1,0:T(8,128)(2,1)} %get-tuple-element.23), calls=%async_computation.1 | async-start | bytes 2097152 | tf_op jit(solution)/shard_map/all_to_all | solution.py:279
  49.1 1.2 shard_map.71.weights_ref
  50.4 14.7 %all-to-all-done.1.rows_ref = bf16[8,256,256]{2,1,0:T(8,128)(2,1)S(1)} async-done(((bf16[8,256,256]{2,1,0:T(8,128)(2,1)}), bf16[8,256,256]{2,1,0:T(8,128)(2,1)S(1)}, u32[]{:S(2)}, u32[]{:S(2)}) %all-to-all-start.1) | async-done | bytes 1048608 | tf_op jit(solution)/shard_map/all_to_all | solution.py:279
  65.1 2.5 %shard_map.72 = (bf16[1024,2048]{1,0:T(8,128)(2,1)S(1)}, f32[4,8,128]{2,1,0:T(8,128)S(1)}) custom-call(bf16[8,256,256]{2,1,0:T(8,128)(2,1)S(1)} %all-to-all-done.1.rows_ref, bf16[4,2,256,256]{3,2,1,0:T(8,128)(2,1)S(1)} %shard_map.71.weights_ref), custom_call_target="tpu_custom_call" | custom-call | tf_op jit(solution)/shard_map/pallas_call | solution.py:257
  67.6 9.5 %all_to_all.61.parts_ref = f32[4,8,128]{2,1,0:T(8,128)S(1)} all-to-all(f32[4,8,128]{2,1,0:T(8,128)S(1)} %get-tuple-element.26), channel_id=1, replica_groups=mesh['z'=16,'y'=4,'x'=4,'c'=2] {'x'}, dimensions={0} | all-to-all | bytes 32768 | tf_op jit(solution)/shard_map/all_to_all | solution.py:279
  77.7 8.0 %all_to_all.62.parts_ref = f32[8,16,128]{2,1,0:T(8,128)S(1)} all-to-all(f32[8,16,128]{2,1,0:T(8,128)S(1)} %shard_map.73), channel_id=1, replica_groups=mesh['z'=16,'y'=4,'x'=4,'c'=2] {'y','c'}, dimensions={0} | all-to-all | bytes 131072 | tf_op jit(solution)/shard_map/all_to_all | solution.py:279
  85.7 20.1 %all_to_all.63.parts_ref = f32[16,16,128]{2,1,0:T(8,128)S(1)} all-to-all(f32[16,16,128]{2,1,0:T(8,128)S(1)} %shard_map.74), channel_id=1, replica_groups=mesh['z'=16,'y'=4,'x'=4,'c'=2] {'z'}, dimensions={0} | all-to-all | bytes 262144 | tf_op jit(solution)/shard_map/all_to_all | solution.py:279
  105.8 1.8 shard_map.75
  107.6 3.3 %all-to-all-start.5 = ((f32[4,8,128]{2,1,0:T(8,128)}), f32[4,8,128]{2,1,0:T(8,128)S(1)}, u32[]{:S(2)}, u32[]{:S(2)}) async-start(f32[4,8,128]{2,1,0:T(8,128)} %shard_map.75), calls=%async_computation.5 | async-start | bytes 32768 | tf_op jit(solution)/shard_map/all_to_all | solution.py:279
  110.9 1.2 copy-done.1
  112.1 1.9 shard_map.76
  114.0 2.0 copy-done.3
  116.2 2.5 %shard_map.77 = (f32[8,32,128]{2,1,0:T(8,128)S(1)}, bf16[1024,2048]{1,0:T(8,128)(2,1)S(1)}) custom-call(f32[4,8,128]{2,1,0:T(8,128)S(1)} %all-to-all-done.5.parts_ref, bf16[1024,2048]{1,0:T(8,128)(2,1)} %copy-done, f32[16,128]{1,0:T(8,128)S(1)} %get-tuple-element.30.total_ref), custom_call_target="tpu_custom_call" | custom-call | tf_op jit(solution)/shard_map/pallas_call | solution.py:257
  118.7 8.5 %all_to_all.64.parts_ref = f32[8,32,128]{2,1,0:T(8,128)S(1)} all-to-all(f32[8,32,128]{2,1,0:T(8,128)S(1)} %get-tuple-element.31), channel_id=1, replica_groups=mesh['z'=16,'y'=4,'x'=4,'c'=2] {'y','c'}, dimensions={0} | all-to-all | bytes 262144 | tf_op jit(solution)/shard_map/all_to_all | solution.py:279
  127.2 19.5 %all_to_all.65.parts_ref = bf16[16,48,128]{2,1,0:T(8,128)(2,1)S(1)} all-to-all(bf16[16,48,128]{2,1,0:T(8,128)(2,1)S(1)} %shard_map.78), channel_id=1, replica_groups=mesh['z'=16,'y'=4,'x'=4,'c'=2] {'z'}, dimensions={0} | all-to-all | bytes 393216 | tf_op jit(solution)/shard_map/all_to_all | solution.py:279
  148.0 9.9 %all_to_all.66.parts_ref.column_ref = f32[4,8,128]{2,1,0:T(8,128)S(1)} all-to-all(f32[4,8,128]{2,1,0:T(8,128)S(1)} %get-tuple-element.33), channel_id=1, replica_groups=mesh['z'=16,'y'=4,'x'=4,'c'=2] {'x'}, dimensions={0} | all-to-all | bytes 32768 | tf_op jit(solution)/shard_map/all_to_all | solution.py:279
  157.9 1.4 shard_map.80
  159.2 8.7 %all_to_all.67.parts_ref = f32[8,32,128]{2,1,0:T(8,128)S(1)} all-to-all(f32[8,32,128]{2,1,0:T(8,128)S(1)} %shard_map.80), channel_id=1, replica_groups=mesh['z'=16,'y'=4,'x'=4,'c'=2] {'y','c'}, dimensions={0} | all-to-all | bytes 262144 | tf_op jit(solution)/shard_map/all_to_all | solution.py:279
  167.9 20.8 %all_to_all.68.parts_ref = bf16[16,48,128]{2,1,0:T(8,128)(2,1)S(1)} all-to-all(bf16[16,48,128]{2,1,0:T(8,128)(2,1)S(1)} %shard_map.81), channel_id=1, replica_groups=mesh['z'=16,'y'=4,'x'=4,'c'=2] {'z'}, dimensions={0} | all-to-all | bytes 393216 | tf_op jit(solution)/shard_map/all_to_all | solution.py:279
  188.8 4.3 %shard_map.82 = bf16[4,272,256]{2,1,0:T(8,128)(2,1)S(1)} custom-call(bf16[16,48,128]{2,1,0:T(8,128)(2,1)S(1)} %all_to_all.68.parts_ref, f32[4,8,128]{2,1,0:T(8,128)S(1)} %all_to_all.66.parts_ref.column_ref, f32[16,128]{1,0:T(8,128)S(1)} %get-tuple-element.36.total_ref, bf16[1024,2048]{1,0:T(8,128)(2,1)S(1)} %get-tuple-element.32.expo_ref.target_ref, ...), custom_call_target="tpu_custom_call" | custom-call | tf_op jit(solution)/shard_map/pallas_call | solution.py:257
  193.0 11.6 %all_to_all.69.refs_0_ = bf16[4,272,256]{2,1,0:T(8,128)(2,1)S(1)} all-to-all(bf16[4,272,256]{2,1,0:T(8,128)(2,1)S(1)} %shard_map.82), channel_id=1, replica_groups=mesh['z'=16,'y'=4,'x'=4,'c'=2] {'x'}, dimensions={0} | all-to-all | bytes 1114112 | tf_op jit(solution)/shard_map/all_to_all | solution.py:279
  (22 shorter events, 4.3 us)
Async XLA Ops:
  7.2 42.0 %all-gather.7.cloned.1.call-start = ((), (), s32[]{:S(2)}) async-start(), calls=%async_computation.13 | async-start | bytes 1310720 | tf_op jit(solution)/shard_map/all_gather | solution.py:302
  10.5 97.1 %all-gather.5.cloned.1.call-start = ((), (), s32[]{:S(2)}) async-start(), calls=%async_computation.12 | async-start | bytes 1179648 | tf_op jit(solution)/shard_map/all_gather | solution.py:312
  44.6 20.4 %all-to-all-start.1 = ((bf16[8,256,256]{2,1,0:T(8,128)(2,1)}), bf16[8,256,256]{2,1,0:T(8,128)(2,1)S(1)}, u32[]{:S(2)}, u32[]{:S(2)}) async-start(bf16[8,256,256]{2,1,0:T(8,128)(2,1)} %get-tuple-element.23), calls=%async_computation.1 | async-start | bytes 2097152 | tf_op jit(solution)/shard_map/all_to_all | solution.py:279
  67.6 38.3 %copy-start = (bf16[1024,2048]{1,0:T(8,128)(2,1)}, bf16[1024,2048]{1,0:T(8,128)(2,1)S(1)}, u32[]{:S(2)}) copy-start(bf16[1024,2048]{1,0:T(8,128)(2,1)S(1)} %get-tuple-element.27.expo_ref) | copy-start | bytes 12582916
  107.6 8.6 %all-to-all-start.5 = ((f32[4,8,128]{2,1,0:T(8,128)}), f32[4,8,128]{2,1,0:T(8,128)S(1)}, u32[]{:S(2)}, u32[]{:S(2)}) async-start(f32[4,8,128]{2,1,0:T(8,128)} %shard_map.75), calls=%async_computation.5 | async-start | bytes 32768 | tf_op jit(solution)/shard_map/all_to_all | solution.py:279
  110.9 1.2 copy-start.1
  114.0 2.0 copy-start.3
  148.0 40.8 %copy-start.2 = (bf16[2048,256]{1,0:T(8,128)(2,1)S(1)}, bf16[2048,256]{1,0:T(8,128)(2,1)}, u32[]{:S(2)}) copy-start(bf16[2048,256]{1,0:T(8,128)(2,1)} %all-gather.5.cloned.1.call-done) | copy-start | bytes 3145732
  188.8 15.9 %copy-start.4 = (bf16[256,256]{1,0:T(8,128)(2,1)S(1)}, bf16[256,256]{1,0:T(8,128)(2,1)}, u32[]{:S(2)}) copy-start(bf16[256,256]{1,0:T(8,128)(2,1)} %refs_1_.1) | copy-start | bytes 393220
Sparse Core Ops, SparseCore 0:
  10.7 35.7 all-gather.6
  48.6 31.4 all-gather.4

commit v3 on v2

v3 whole, which is shorter than its diff:
```python
import jax
import jax.numpy as jnp
from jax import lax
from jax.experimental import pallas as pl
from jax.experimental.pallas import tpu as pltpu
from jax.sharding import Mesh, PartitionSpec as P

LANES = 128

norm_eps = 1e-06
teacher_scale = 1.0 / 0.07
student_scale = 1.0 / 0.1

f32 = jnp.float32
bf16 = jnp.bfloat16
NT = (((1,), (1,)), ((), ()))
NN = (((1,), (0,)), ((), ()))


def dot(a, b, dims):
    return lax.dot_general(a, b, dims, preferred_element_type=f32)


def unit_rows(values):
    values = values.astype(f32)
    return values * lax.rsqrt(jnp.sum(values * values, axis=1, keepdims=True) + norm_eps)


def fold(row):
    n = row.shape[1] // LANES
    return jnp.concatenate([row[:, LANES * i : LANES * (i + 1)] for i in range(n)], axis=0)


def unfold(tile):
    return jnp.concatenate([tile[i : i + 1, :] for i in range(tile.shape[0])], axis=1)


def split_rows(row):
    high = row.astype(bf16).astype(f32)
    which = lax.broadcasted_iota(jnp.int32, (16, row.shape[1]), 0)
    return jnp.where(which == 0, high, jnp.where(which == 1, row - high, 0.0)).astype(bf16)


def matvec(row, matrix, dims):
    return jnp.sum(dot(split_rows(row), matrix, dims), axis=0, keepdims=True)


def spread(out_ref, tile):
    for i in range(out_ref.shape[0]):
        out_ref[i] = tile


def total_of(parts_ref):
    total = parts_ref[0]
    for i in range(1, parts_ref.shape[0]):
        total = total + parts_ref[i]
    return total


def rows_kernel(mask_ref, sp_ref, tp_ref, rows_ref, mask, sp, tp, sems):
    copies = [
        pltpu.make_async_copy(source, target, sems.at[i])
        for i, (source, target) in enumerate(((mask_ref, mask), (tp_ref, tp), (sp_ref, sp)))
    ]
    for copy in copies:
        copy.start()
    count = mask_ref.shape[0]
    patches = sp_ref.shape[0]
    copies[0].wait()
    which = lax.broadcasted_iota(jnp.int32, (count, patches), 0)
    wanted = jnp.zeros((count, patches), jnp.int32)
    for i in range(count):
        wanted = jnp.where(which == i, mask[i], wanted)
    onehot = (lax.broadcasted_iota(jnp.int32, (count, patches), 1) == wanted).astype(f32).astype(bf16)
    copies[1].wait()
    teacher = unit_rows(dot(onehot, tp[...], NN)).astype(bf16)
    copies[2].wait()
    student = unit_rows(dot(onehot, sp[...], NN)).astype(bf16)
    for i in range(rows_ref.shape[0]):
        rows_ref[i, :count] = teacher
        rows_ref[i, count:] = student


def weights_kernel(tw_ref, sw_ref, weights_ref, tw, sw, sems):
    copies = [
        pltpu.make_async_copy(source, target, sems.at[i])
        for i, (source, target) in enumerate(((tw_ref, tw), (sw_ref, sw)))
    ]
    for copy in copies:
        copy.start()
    copies[0].wait()
    weights_ref[0] = unit_rows(tw[...]).astype(bf16)
    copies[1].wait()
    weights_ref[1] = unit_rows(sw[...]).astype(bf16)


def divide_kernel(rows_ref, out_ref):
    n, both, _ = rows_ref.shape
    count = both // 2
    for i in range(n):
        for j in range(out_ref.shape[0]):
            out_ref[j, count * i : count * (i + 1)] = rows_ref[i, :count]
            out_ref[j, count * (n + i) : count * (n + i + 1)] = rows_ref[i, count:]


def stack_kernel(*refs):
    *parts, out_ref, sems = refs
    copies = [pltpu.make_async_copy(part, out_ref.at[i], sems.at[i]) for i, part in enumerate(parts)]
    for copy in copies:
        copy.start()
    for copy in copies:
        copy.wait()


def pair_kernel(place_ref, *refs):
    *parts, other_ref, out_ref, sems = refs
    n = len(parts)
    core = place_ref[n]
    copies = []
    for i, part in enumerate(parts):
        copies.append(pltpu.make_async_copy(part, out_ref.at[place_ref[i], core], sems.at[0, i]))
        copies.append(pltpu.make_async_copy(other_ref.at[i], out_ref.at[place_ref[i], 1 - core], sems.at[1, i]))
    for copy in copies:
        copy.start()
    for copy in copies:
        copy.wait()


def first_kernel(rows_ref, weights_ref, target_ref, expo_ref, product_ref, total_ref, column_ref):
    groups, both, _ = rows_ref.shape
    count = both // 2
    nx, nc, _, width, _ = weights_ref.shape
    for j in range(groups):
        total = jnp.zeros((1, count), f32)
        for i in range(nx * nc):
            place = (slice(width * i, width * (i + 1)), slice(count * j, count * (j + 1)))
            weights = weights_ref.at[i // nc, i % nc]
            target = jnp.exp(dot(weights[0], rows_ref[j, :count], NT) * teacher_scale)
            logits = dot(weights[1], rows_ref[j, count:], NT) * student_scale
            expo = jnp.exp(logits)
            total = total + jnp.sum(expo, axis=0, keepdims=True)
            target_ref[place] = target.astype(bf16)
            expo_ref[place] = expo.astype(bf16)
            product_ref[place] = (target * logits).astype(bf16)
        per = count // LANES
        total_ref[per * j : per * (j + 1)] = fold(total)
    ones = jnp.ones((1, groups * count), f32)
    spread(column_ref, fold(matvec(ones, target_ref[...], NT)))


def column_kernel(parts_ref, expo_ref, column_ref):
    row = unfold(1.0 / total_of(parts_ref))
    spread(column_ref, fold(matvec(row, expo_ref[...], NT)))


def row_kernel(parts_ref, expo_ref, out_ref):
    column = unfold(1.0 / total_of(parts_ref))
    spread(out_ref, fold(matvec(column, expo_ref[...], NN)))


def second_row_kernel(parts_ref, expo_ref, total_ref, out_ref):
    column = unfold(1.0 / total_of(parts_ref))
    sums = fold(matvec(column, expo_ref[...], NN))
    spread(out_ref, jnp.concatenate([sums, total_ref[...]], axis=0))


def last_row_kernel(parts_ref, expo_ref, product_ref, out_ref):
    column = unfold(1.0 / total_of(parts_ref))
    sums = fold(matvec(column, expo_ref[...], NN))
    cross = fold(matvec(column, product_ref[...], NN))
    spread(out_ref, jnp.concatenate([sums, cross], axis=0))


def add_kernel(parts_ref, out_ref):
    spread(out_ref, total_of(parts_ref))


def third_column_kernel(parts_ref, expo_ref, column_ref, total_ref):
    both = total_of(parts_ref)
    lines = both.shape[0] // 2
    spread(column_ref, fold(matvec(unfold(1.0 / both[:lines]), expo_ref[...], NT)))
    total_ref[...] = both[lines:]


def pieces_of(row):
    high = row.astype(bf16).astype(f32)
    middle = (row - high).astype(bf16).astype(f32)
    which = lax.broadcasted_iota(jnp.int32, (16, row.shape[1]), 0)
    pieces = jnp.where(which == 0, high, jnp.where(which == 1, middle, jnp.where(which == 2, row - high - middle, 0.0)))
    return pieces.astype(bf16)


def slope_kernel(core_ref, parts_ref, column_ref, total_ref, target_ref, expo_ref, rows_ref, out_ref, columns):
    groups, both, depth = rows_ref.shape
    count = both // 2
    n, width, _ = out_ref.shape
    width = width - 16
    nc = target_ref.shape[0] // (n * width)
    core = core_ref[0]
    per = width // LANES
    columns[...] = 1.0 / total_of(column_ref)
    sums = total_of(parts_ref)
    lines = sums.shape[0] // 2
    row = 1.0 / sums[:lines]
    student_total = total_ref[...]
    partial = jnp.sum(jnp.log(student_total)) - jnp.sum(row * sums[lines:])
    row = unfold(row * student_scale)
    inverse = unfold(student_scale / student_total)
    for i in range(n):
        block = i * nc + core
        column = jnp.concatenate([columns[pl.ds(block * per + k, 1), :] for k in range(per)], axis=1)
        column = jnp.broadcast_to(column, (8, width)).T[:, 0:1]
        start = pl.multiple_of(block * width, width)
        grad = jnp.zeros((width, depth), f32)
        for j in range(groups):
            lanes = slice(count * j, count * (j + 1))
            target = target_ref[pl.ds(start, width), lanes].astype(f32) * column * row[:, lanes]
            slope = (expo_ref[pl.ds(start, width), lanes].astype(f32) * inverse[:, lanes] - target).astype(bf16)
            grad = grad + dot(slope, rows_ref[j, count:], NN)
        out_ref[i, :width] = grad.astype(out_ref.dtype)
        out_ref[i, width:] = pieces_of(jnp.full((1, depth), partial, f32)).astype(out_ref.dtype)


def join_kernel(own_ref, other_ref, out_ref):
    width = own_ref.shape[1] - 16
    for i in range(own_ref.shape[0]):
        out_ref[i, :width] = (own_ref[i, :width] + other_ref[i, :width].astype(f32)).astype(bf16)
        pieces = own_ref[i, width:] + other_ref[i, width:].astype(f32)
        out_ref[i, width:] = pieces_of(jnp.sum(pieces, axis=0, keepdims=True))


def finish_kernel(rows, parts_ref, proto_ref, loss_ref, grad_ref):
    width = proto_ref.shape[0]
    unit_grad = parts_ref[0, :width].astype(f32)
    pieces = parts_ref[0, width:].astype(f32)
    for i in range(1, parts_ref.shape[0]):
        unit_grad = unit_grad + parts_ref[i, :width].astype(f32)
        pieces = pieces + parts_ref[i, width:].astype(f32)
    loss_ref[...] = jnp.sum(pieces, axis=0, keepdims=True)[:, :LANES] / rows
    proto = proto_ref[...].astype(f32)
    scale = lax.rsqrt(jnp.sum(proto * proto, axis=1, keepdims=True) + norm_eps)
    unit = proto * scale
    grad_ref[...] = (unit_grad - unit * jnp.sum(unit * unit_grad, axis=1, keepdims=True)) * scale


def call(kernel, outs, *args, place=None, scratch=(), limit=20):
    vmem = pl.BlockSpec(memory_space=pltpu.VMEM)
    place = place or {}
    return pl.pallas_call(
        kernel,
        out_shape=outs,
        in_specs=[pl.BlockSpec(memory_space=place[i]) if i in place else vmem for i in range(len(args))],
        out_specs=jax.tree.map(lambda _: vmem, outs),
        scratch_shapes=scratch,
        compiler_params=pltpu.CompilerParams(vmem_limit_bytes=limit * 1024 * 1024),
    )(*args)


def per_device(nz, ny, nx, nc, student_patches, teacher_patches, mask_rows, student_proto, teacher_proto):
    shape = jax.ShapeDtypeStruct
    held = pltpu.VMEM
    count = mask_rows.shape[0]
    patches = student_patches.shape
    width, depth = student_proto.shape
    rows = count * nz * ny
    columns = width * nx * nc
    lines, column_lines = rows // LANES, columns // LANES

    def exchange(values, axes):
        return lax.all_to_all(values, axes, 0, 0, tiled=True)

    def far(values):
        return pltpu.with_memory_space_constraint(values, pltpu.HBM)

    def sems(n):
        return pltpu.SemaphoreType.DMA((n,))

    picked = call(
        rows_kernel,
        shape((nz, 2 * count, depth), bf16),
        far(mask_rows), far(student_patches), far(teacher_patches),
        place={0: pltpu.HBM, 1: pltpu.HBM, 2: pltpu.HBM},
        scratch=[pltpu.SMEM((count,), jnp.int32), pltpu.VMEM(patches, bf16), pltpu.VMEM(patches, bf16), sems(3)],
    )
    late_teacher, late_student, picked = lax.optimization_barrier((teacher_proto, student_proto, picked))
    weights = call(
        weights_kernel,
        shape((2, width, depth), bf16),
        far(late_teacher), far(late_student),
        place={0: pltpu.HBM, 1: pltpu.HBM},
        scratch=[pltpu.VMEM((width, depth), bf16), pltpu.VMEM((width, depth), bf16), sems(2)],
    )
    parts = [weights] + [lax.ppermute(weights, "x", [(i, (i + k) % nx) for i in range(nx)]) for k in range(1, nx)]
    core = lax.axis_index("c").astype(jnp.int32).reshape(1)
    places = (lax.axis_index("x") - jnp.arange(nx, dtype=jnp.int32)) % nx
    places, core, other_core, picked = lax.optimization_barrier(
        (jnp.concatenate([places, core]), core, nc - 1 - core, picked)
    )
    picked = exchange(picked, "z")
    picked, parts[0] = lax.optimization_barrier((picked, parts[0]))
    picked = call(divide_kernel, shape((ny, 2 * nz * count, depth), bf16), picked)
    picked, *parts[1:] = lax.optimization_barrier((picked, *parts[1:]))
    parts = [far(part) for part in parts]
    stacked = call(
        stack_kernel,
        shape((nx, *weights.shape), bf16),
        *parts,
        place={i: pltpu.HBM for i in range(nx)},
        scratch=[sems(nx)],
    )
    other = lax.ppermute(stacked, "c", [(i, (i + 1) % nc) for i in range(nc)])
    weights = call(
        pair_kernel,
        held((nx, nc, *weights.shape), bf16),
        places, *parts, far(other),
        place={0: pltpu.SMEM, **{1 + i: pltpu.HBM for i in range(nx + 1)}},
        scratch=[pltpu.SemaphoreType.DMA((nc, nx))],
    )
    picked = exchange(picked, "y")

    column_out = shape((nx * nc, column_lines, LANES), f32)
    row_out = shape((ny, lines, LANES), f32)
    rows_out = shape((ny, 2 * lines, LANES), f32)
    matrix = held((columns, rows), bf16)
    target, expo, product, student_total, column = call(
        first_kernel, (matrix, matrix, matrix, shape((lines, LANES), f32), column_out), picked, weights
    )
    column = exchange(column, ("x", "c"))
    row = call(row_kernel, row_out, column, target)
    row = exchange(row, "y")
    row = call(add_kernel, shape((nz, lines, LANES), f32), row)
    row = exchange(row, "z")

    column = call(column_kernel, column_out, row, target)
    column = exchange(column, ("x", "c"))
    row = call(second_row_kernel, rows_out, column, target, student_total)
    row = exchange(row, "y")
    row = call(add_kernel, shape((nz, 2 * lines, LANES), f32), row)
    row = exchange(row, "z")

    column, student_total = call(third_column_kernel, (column_out, shape((lines, LANES), f32)), row, target)
    column = exchange(column, ("x", "c"))
    row = call(last_row_kernel, rows_out, column, target, product)
    row = exchange(row, "y")
    row = call(add_kernel, shape((nz, 2 * lines, LANES), f32), row)
    row = exchange(row, "z")

    halves = []
    for which, kind in ((other_core, bf16), (core, f32)):
        halves.append(
            call(
                slope_kernel,
                shape((nx, width + 16, depth), kind),
                which, row, column, student_total, target, expo, picked,
                place={0: pltpu.SMEM},
                scratch=[pltpu.VMEM((column_lines, LANES), f32)],
            )
        )
    other = lax.ppermute(halves[0], "c", [(i, (i + 1) % nc) for i in range(nc)])
    grads = call(join_kernel, shape((nx, width + 16, depth), bf16), halves[1], other)
    grads = exchange(grads, "x")
    loss, proto_grad = call(
        lambda *refs: finish_kernel(rows * nx * nc, *refs),
        (shape((1, LANES), f32), shape((width, depth), f32)),
        grads, student_proto,
    )
    return (loss[0, 0], proto_grad)


def solution(mesh):
    nz = mesh.shape["grp"]
    ny, nx, nc = 4, 4, 2
    axes = ("z", "y", "x", "c")
    inner = Mesh(mesh.devices.reshape(nz, ny, nx, nc), axes)
    placed = (P(axes, None), P(axes, None), P(axes), P(axes, None), P(axes, None))
    return jax.shard_map(
        lambda *args: per_device(nz, ny, nx, nc, *args),
        mesh=inner,
        in_specs=placed,
        out_specs=(P(), P(axes, None)),
        check_vma=False,
    )
```

time: 213 us -> 200 us (0.939)
  the two profiles are of different devices: /device:TPU:32 before, /device:TPU:1 now
where the time goes in v3:
time: 200 us; the launch traced here: 199 us
  blocking collectives  114 us (57%)
  starting transfers between devices  37.9 us (19%)
  waiting for transfers between devices  24.3 us (12%)
  Pallas kernels  20.8 us (10%)
    all_to_all x10, blocking collectives, exchange(): return lax.all_to_all(values, axes, 0, 0, tiled=True)  114 us
    pallas_call x18, Pallas kernels, call(): pl.pallas_call(kernel, out_shape=outs, in_specs=[pl.BlockSpec(memory_spac...  20.8 us
    all_to_all x2, starting transfers between devices, exchange(): return lax.all_to_all(values, axes, 0, 0, tiled=True)  20 us
    all_to_all x2, waiting for transfers between devices, exchange(): return lax.all_to_all(values, axes, 0, 0, tiled=True)  15.4 us
    ppermute x3, starting transfers between devices, per_device(): lax.ppermute(weights, 'x', [(i, (i + k) % nx) for i in range(nx)])  9.33 us
    ppermute x3, waiting for transfers between devices, per_device(): lax.ppermute(weights, 'x', [(i, (i + k) % nx) for i in range(nx)])  8.58 us
    ppermute x1, starting transfers between devices, per_device(): other = lax.ppermute(halves[0], 'c', [(i, (i + 1) % nc) for i in range(nc)])  6.19 us
  transfers between devices with their start and end apart: 7, of which 5 were waited for; matrix products, arithmetic and copies ran while one was open for 0% of the time, Pallas kernels for 3%

profile of v3, /device:TPU:1, one launch (start us, length us, event | category | flops | bytes accessed | tf_op | source)
XLA Modules:
  0.0 198.9 jit_solution(7820047655986604166)
XLA Ops:
  0.7 2.1 %shard_map.68 = bf16[16,32,256]{2,1,0:T(8,128)(2,1)} custom-call(s32[16]{0:T(128)} %mask_ref.1, bf16[256,256]{1,0:T(8,128)(2,1)} %sp_ref.1, bf16[256,256]{1,0:T(8,128)(2,1)} %tp_ref.1), custom_call_target="tpu_custom_call" | custom-call | tf_op jit(solution)/shard_map/pallas_call | solution.py:249
  2.8 15.8 %all-to-all-start = ((bf16[16,32,256]{2,1,0:T(8,128)(2,1)}), bf16[16,32,256]{2,1,0:T(8,128)(2,1)S(1)}, u32[]{:S(2)}, u32[]{:S(2)}) async-start(bf16[16,32,256]{2,1,0:T(8,128)(2,1)} %shard_map.68), calls=%async_computation | async-start | bytes 524288 | tf_op jit(solution)/shard_map/all_to_all | solution.py:270
  19.8 4.4 %collective-permute-start.2 = (bf16[2,256,256]{2,1,0:T(8,128)(2,1)S(1)}, bf16[2,256,256]{2,1,0:T(8,128)(2,1)S(1)}, u32[]{:S(2)}, u32[]{:S(2)}) collective-permute-start(bf16[2,256,256]{2,1,0:T(8,128)(2,1)S(1)} %shard_map.69.refs_0_), channel_id=1, source_target_pairs={{0,6},{2,0},{4,2},{6,4},{1,7},{3,1},{5,3},{7,5},{8,14},{10,8},{12,... | collective-permute-start | bytes 786440 | tf_op jit(solution)/shard_map/ppermute | solution.py:293
  24.2 2.4 %collective-permute-start.1 = (bf16[2,256,256]{2,1,0:T(8,128)(2,1)S(1)}, bf16[2,256,256]{2,1,0:T(8,128)(2,1)S(1)}, u32[]{:S(2)}, u32[]{:S(2)}) collective-permute-start(bf16[2,256,256]{2,1,0:T(8,128)(2,1)S(1)} %shard_map.69.refs_0_), channel_id=1, source_target_pairs={{0,4},{2,6},{4,0},{6,2},{1,5},{3,7},{5,1},{7,3},{8,12},{10,14},{12... | collective-permute-start | bytes 786440 | tf_op jit(solution)/shard_map/ppermute | solution.py:293
  26.6 2.5 %collective-permute-start = (bf16[2,256,256]{2,1,0:T(8,128)(2,1)S(1)}, bf16[2,256,256]{2,1,0:T(8,128)(2,1)S(1)}, u32[]{:S(2)}, u32[]{:S(2)}) collective-permute-start(bf16[2,256,256]{2,1,0:T(8,128)(2,1)S(1)} %shard_map.69.refs_0_), channel_id=1, source_target_pairs={{0,2},{2,4},{4,6},{6,0},{1,3},{3,5},{5,7},{7,1},{8,10},{10,12},{12... | collective-permute-start | bytes 786440 | tf_op jit(solution)/shard_map/ppermute | solution.py:293
  29.1 2.6 %all-to-all-done.rows_ref = bf16[16,32,256]{2,1,0:T(8,128)(2,1)S(1)} async-done(((bf16[16,32,256]{2,1,0:T(8,128)(2,1)}), bf16[16,32,256]{2,1,0:T(8,128)(2,1)S(1)}, u32[]{:S(2)}, u32[]{:S(2)}) %all-to-all-start) | async-done | bytes 262176 | tf_op jit(solution)/shard_map/all_to_all | solution.py:270
  32.8 1.4 collective-permute-done.1.refs_2_
  34.2 7.2 %collective-permute-done.refs_1_ = bf16[2,256,256]{2,1,0:T(8,128)(2,1)S(1)} collective-permute-done((bf16[2,256,256]{2,1,0:T(8,128)(2,1)S(1)}, bf16[2,256,256]{2,1,0:T(8,128)(2,1)S(1)}, u32[]{:S(2)}, u32[]{:S(2)}) %collective-permute-start) | collective-permute-done | bytes 262176 | tf_op jit(solution)/shard_map/ppermute | solution.py:293
  43.3 2.5 %collective-permute-start.3 = (bf16[4,2,256,256]{3,2,1,0:T(8,128)(2,1)S(1)}, bf16[4,2,256,256]{3,2,1,0:T(8,128)(2,1)}, u32[]{:S(2)}, u32[]{:S(2)}) collective-permute-start(bf16[4,2,256,256]{3,2,1,0:T(8,128)(2,1)S(1)} %shard_map.71), channel_id=1, source_target_pairs={{0,1},{1,0},{2,3},{3,2},{4,5},{5,4},{6,7},{7,6},{8,9},{9,8},{10,11... | collective-permute-start | bytes 3145736 | tf_op jit(solution)/shard_map/ppermute | solution.py:311
  45.8 4.2 %all-to-all-start.1 = ((bf16[4,512,256]{2,1,0:T(8,128)(2,1)}), bf16[4,512,256]{2,1,0:T(8,128)(2,1)S(1)}, u32[]{:S(2)}, u32[]{:S(2)}) async-start(bf16[4,512,256]{2,1,0:T(8,128)(2,1)} %shard_map.70), calls=%async_computation.1 | async-start | bytes 2097152 | tf_op jit(solution)/shard_map/all_to_all | solution.py:270
  50.0 2.1 %shard_map.72.weights_ref = bf16[4,2,2,256,256]{4,3,2,1,0:T(8,128)(2,1)S(1)} custom-call(s32[5]{0:T(128)S(1)} %pad_add_fusion.place_ref, bf16[2,256,256]{2,1,0:T(8,128)(2,1)} %copy-done, bf16[2,256,256]{2,1,0:T(8,128)(2,1)} %copy-done.4, bf16[2,256,256]{2,1,0:T(8,128)(2,1)} %copy-done.3, bf16[2,256,256]{2,1,0:T(8,128)(2,1)} %copy-done.2, ...), custom_call_target="tpu_custom_call" | custom-call | tf_op jit(solution)/shard_map/pallas_call | solution.py:249
  52.1 12.8 %all-to-all-done.1.rows_ref = bf16[4,512,256]{2,1,0:T(8,128)(2,1)S(1)} async-done(((bf16[4,512,256]{2,1,0:T(8,128)(2,1)}), bf16[4,512,256]{2,1,0:T(8,128)(2,1)S(1)}, u32[]{:S(2)}, u32[]{:S(2)}) %all-to-all-start.1) | async-done | bytes 1048608 | tf_op jit(solution)/shard_map/all_to_all | solution.py:270
  64.9 4.5 %shard_map.73 = (bf16[2048,1024]{1,0:T(8,128)(2,1)S(1)}, bf16[2048,1024]{1,0:T(8,128)(2,1)S(1)}, bf16[2048,1024]{1,0:T(8,128)(2,1)S(1)}, f32[8,128]{1,0:T(8,128)S(1)}, f32[8,16,128]{2,1,0:T(8,128)S(1)}) custom-call(bf16[4,512,256]{2,1,0:T(8,128)(2,1)S(1)} %all-to-all-done.1.rows_ref, bf16[4,2,2,256,256]{4,3,2,1,0:T(8,128)(2,1)S(1)} %shard_map.72.weights_ref), custom_call_target="tpu_custom_call" | custom-call | tf_op jit(solution)/shard_map/pallas_call | solution.py:249
  69.5 8.3 %all_to_all.60.parts_ref = f32[8,16,128]{2,1,0:T(8,128)S(1)} all-to-all(f32[8,16,128]{2,1,0:T(8,128)S(1)} %get-tuple-element.36), channel_id=1, replica_groups=mesh['z'=16,'y'=4,'x'=4,'c'=2] {'x','c'}, dimensions={0} | all-to-all | bytes 131072 | tf_op jit(solution)/shard_map/all_to_all | solution.py:270
  78.5 6.6 %all_to_all.61.parts_ref = f32[4,8,128]{2,1,0:T(8,128)S(1)} all-to-all(f32[4,8,128]{2,1,0:T(8,128)S(1)} %shard_map.74), channel_id=1, replica_groups=mesh['z'=16,'y'=4,'x'=4,'c'=2] {'y'}, dimensions={0} | all-to-all | bytes 32768 | tf_op jit(solution)/shard_map/all_to_all | solution.py:270
  85.0 22.8 %all_to_all.62.parts_ref = f32[16,8,128]{2,1,0:T(8,128)S(1)} all-to-all(f32[16,8,128]{2,1,0:T(8,128)S(1)} %shard_map.75), channel_id=1, replica_groups=mesh['z'=16,'y'=4,'x'=4,'c'=2] {'z'}, dimensions={0} | all-to-all | bytes 131072 | tf_op jit(solution)/shard_map/all_to_all | solution.py:270
  109.1 10.6 %all_to_all.63.parts_ref = f32[8,16,128]{2,1,0:T(8,128)S(1)} all-to-all(f32[8,16,128]{2,1,0:T(8,128)S(1)} %shard_map.76), channel_id=1, replica_groups=mesh['z'=16,'y'=4,'x'=4,'c'=2] {'x','c'}, dimensions={0} | all-to-all | bytes 131072 | tf_op jit(solution)/shard_map/all_to_all | solution.py:270
  120.4 6.7 %all_to_all.64.parts_ref = f32[4,16,128]{2,1,0:T(8,128)S(1)} all-to-all(f32[4,16,128]{2,1,0:T(8,128)S(1)} %shard_map.77), channel_id=1, replica_groups=mesh['z'=16,'y'=4,'x'=4,'c'=2] {'y'}, dimensions={0} | all-to-all | bytes 65536 | tf_op jit(solution)/shard_map/all_to_all | solution.py:270
  127.1 14.5 %all_to_all.65.parts_ref = f32[16,16,128]{2,1,0:T(8,128)S(1)} all-to-all(f32[16,16,128]{2,1,0:T(8,128)S(1)} %shard_map.78), channel_id=1, replica_groups=mesh['z'=16,'y'=4,'x'=4,'c'=2] {'z'}, dimensions={0} | all-to-all | bytes 262144 | tf_op jit(solution)/shard_map/all_to_all | solution.py:270
  142.8 11.2 %all_to_all.66.parts_ref.column_ref = f32[8,16,128]{2,1,0:T(8,128)S(1)} all-to-all(f32[8,16,128]{2,1,0:T(8,128)S(1)} %get-tuple-element.39), channel_id=1, replica_groups=mesh['z'=16,'y'=4,'x'=4,'c'=2] {'x','c'}, dimensions={0} | all-to-all | bytes 131072 | tf_op jit(solution)/shard_map/all_to_all | solution.py:270
  155.3 6.7 %all_to_all.67.parts_ref = f32[4,16,128]{2,1,0:T(8,128)S(1)} all-to-all(f32[4,16,128]{2,1,0:T(8,128)S(1)} %shard_map.80), channel_id=1, replica_groups=mesh['z'=16,'y'=4,'x'=4,'c'=2] {'y'}, dimensions={0} | all-to-all | bytes 65536 | tf_op jit(solution)/shard_map/all_to_all | solution.py:270
  162.0 15.0 %all_to_all.68.parts_ref = f32[16,16,128]{2,1,0:T(8,128)S(1)} all-to-all(f32[16,16,128]{2,1,0:T(8,128)S(1)} %shard_map.81), channel_id=1, replica_groups=mesh['z'=16,'y'=4,'x'=4,'c'=2] {'z'}, dimensions={0} | all-to-all | bytes 262144 | tf_op jit(solution)/shard_map/all_to_all | solution.py:270
  178.3 6.2 %collective-permute-start.4 = (bf16[4,272,256]{2,1,0:T(8,128)(2,1)S(1)}, bf16[4,272,256]{2,1,0:T(8,128)(2,1)S(1)}, u32[]{:S(2)}, u32[]{:S(2)}) collective-permute-start(bf16[4,272,256]{2,1,0:T(8,128)(2,1)S(1)} %shard_map.83), channel_id=1, source_target_pairs={{0,1},{1,0},{2,3},{3,2},{4,5},{5,4},{6,7},{7,6},{8,9},{9,8},{10,11... | collective-permute-start | bytes 1671176 | tf_op jit(solution)/shard_map/ppermute | solution.py:359
  186.2 11.8 %all_to_all.69.refs_0_ = bf16[4,272,256]{2,1,0:T(8,128)(2,1)S(1)} all-to-all(bf16[4,272,256]{2,1,0:T(8,128)(2,1)S(1)} %shard_map.84), channel_id=1, replica_groups=mesh['z'=16,'y'=4,'x'=4,'c'=2] {'x'}, dimensions={0} | all-to-all | bytes 1114112 | tf_op jit(solution)/shard_map/all_to_all | solution.py:270
  (30 shorter events, 13.1 us)
Async XLA Ops:
  2.8 28.9 %all-to-all-start = ((bf16[16,32,256]{2,1,0:T(8,128)(2,1)}), bf16[16,32,256]{2,1,0:T(8,128)(2,1)S(1)}, u32[]{:S(2)}, u32[]{:S(2)}) async-start(bf16[16,32,256]{2,1,0:T(8,128)(2,1)} %shard_map.68), calls=%async_computation | async-start | bytes 524288 | tf_op jit(solution)/shard_map/all_to_all | solution.py:270
  19.8 21.6 %copy-start = (bf16[2,256,256]{2,1,0:T(8,128)(2,1)}, bf16[2,256,256]{2,1,0:T(8,128)(2,1)S(1)}, u32[]{:S(2)}) copy-start(bf16[2,256,256]{2,1,0:T(8,128)(2,1)S(1)} %shard_map.69.refs_0_) | copy-start | bytes 786436
  19.8 13.0 %collective-permute-start.2 = (bf16[2,256,256]{2,1,0:T(8,128)(2,1)S(1)}, bf16[2,256,256]{2,1,0:T(8,128)(2,1)S(1)}, u32[]{:S(2)}, u32[]{:S(2)}) collective-permute-start(bf16[2,256,256]{2,1,0:T(8,128)(2,1)S(1)} %shard_map.69.refs_0_), channel_id=1, source_target_pairs={{0,6},{2,0},{4,2},{6,4},{1,7},{3,1},{5,3},{7,5},{8,14},{10,8},{12,... | collective-permute-start | bytes 786440 | tf_op jit(solution)/shard_map/ppermute | solution.py:293
  24.2 10.0 %collective-permute-start.1 = (bf16[2,256,256]{2,1,0:T(8,128)(2,1)S(1)}, bf16[2,256,256]{2,1,0:T(8,128)(2,1)S(1)}, u32[]{:S(2)}, u32[]{:S(2)}) collective-permute-start(bf16[2,256,256]{2,1,0:T(8,128)(2,1)S(1)} %shard_map.69.refs_0_), channel_id=1, source_target_pairs={{0,4},{2,6},{4,0},{6,2},{1,5},{3,7},{5,1},{7,3},{8,12},{10,14},{12... | collective-permute-start | bytes 786440 | tf_op jit(solution)/shard_map/ppermute | solution.py:293
  26.6 14.8 %collective-permute-start = (bf16[2,256,256]{2,1,0:T(8,128)(2,1)S(1)}, bf16[2,256,256]{2,1,0:T(8,128)(2,1)S(1)}, u32[]{:S(2)}, u32[]{:S(2)}) collective-permute-start(bf16[2,256,256]{2,1,0:T(8,128)(2,1)S(1)} %shard_map.69.refs_0_), channel_id=1, source_target_pairs={{0,2},{2,4},{4,6},{6,0},{1,3},{3,5},{5,7},{7,1},{8,10},{10,12},{12... | collective-permute-start | bytes 786440 | tf_op jit(solution)/shard_map/ppermute | solution.py:293
  32.8 8.6 %copy-start.2 = (bf16[2,256,256]{2,1,0:T(8,128)(2,1)}, bf16[2,256,256]{2,1,0:T(8,128)(2,1)S(1)}, u32[]{:S(2)}) copy-start(bf16[2,256,256]{2,1,0:T(8,128)(2,1)S(1)} %collective-permute-done.2.refs_3_) | copy-start | bytes 786436
  34.2 7.2 %copy-start.3 = (bf16[2,256,256]{2,1,0:T(8,128)(2,1)}, bf16[2,256,256]{2,1,0:T(8,128)(2,1)S(1)}, u32[]{:S(2)}) copy-start(bf16[2,256,256]{2,1,0:T(8,128)(2,1)S(1)} %collective-permute-done.1.refs_2_) | copy-start | bytes 786436
  41.4 0.7 copy-start.4
  43.3 6.7 %collective-permute-start.3 = (bf16[4,2,256,256]{3,2,1,0:T(8,128)(2,1)S(1)}, bf16[4,2,256,256]{3,2,1,0:T(8,128)(2,1)}, u32[]{:S(2)}, u32[]{:S(2)}) collective-permute-start(bf16[4,2,256,256]{3,2,1,0:T(8,128)(2,1)S(1)} %shard_map.71), channel_id=1, source_target_pairs={{0,1},{1,0},{2,3},{3,2},{4,5},{5,4},{6,7},{7,6},{8,9},{9,8},{10,11... | collective-permute-start | bytes 3145736 | tf_op jit(solution)/shard_map/ppermute | solution.py:311
  45.8 19.1 %all-to-all-start.1 = ((bf16[4,512,256]{2,1,0:T(8,128)(2,1)}), bf16[4,512,256]{2,1,0:T(8,128)(2,1)S(1)}, u32[]{:S(2)}, u32[]{:S(2)}) async-start(bf16[4,512,256]{2,1,0:T(8,128)(2,1)} %shard_map.70), calls=%async_computation.1 | async-start | bytes 2097152 | tf_op jit(solution)/shard_map/all_to_all | solution.py:270
  178.2 19.7 %copy-start.1 = (bf16[256,256]{1,0:T(8,128)(2,1)S(1)}, bf16[256,256]{1,0:T(8,128)(2,1)}, u32[]{:S(2)}) copy-start(bf16[256,256]{1,0:T(8,128)(2,1)} %refs_1_.1) | copy-start | bytes 393220
  178.3 7.8 %collective-permute-start.4 = (bf16[4,272,256]{2,1,0:T(8,128)(2,1)S(1)}, bf16[4,272,256]{2,1,0:T(8,128)(2,1)S(1)}, u32[]{:S(2)}, u32[]{:S(2)}) collective-permute-start(bf16[4,272,256]{2,1,0:T(8,128)(2,1)S(1)} %shard_map.83), channel_id=1, source_target_pairs={{0,1},{1,0},{2,3},{3,2},{4,5},{5,4},{6,7},{7,6},{8,9},{9,8},{10,11... | collective-permute-start | bytes 1671176 | tf_op jit(solution)/shard_map/ppermute | solution.py:359

commit v4 on v3

--- a/solution.py
+++ b/solution.py
@@ -1,3 +1,5 @@
+import functools
+
 import jax
 import jax.numpy as jnp
 from jax import lax
@@ -10,6 +12,7 @@
 norm_eps = 1e-06
 teacher_scale = 1.0 / 0.07
 student_scale = 1.0 / 0.1
+log2_e = 1.4426950408889634
 
 f32 = jnp.float32
 bf16 = jnp.bfloat16
@@ -103,83 +106,91 @@
             out_ref[j, count * (n + i) : count * (n + i + 1)] = rows_ref[i, count:]
 
 
-def stack_kernel(*refs):
+def place_kernel(place_ref, *refs):
     *parts, out_ref, sems = refs
-    copies = [pltpu.make_async_copy(part, out_ref.at[i], sems.at[i]) for i, part in enumerate(parts)]
+    copies = [
+        pltpu.make_async_copy(part, out_ref.at[place_ref[i]], sems.at[i]) for i, part in enumerate(parts)
+    ]
     for copy in copies:
         copy.start()
     for copy in copies:
         copy.wait()
 
 
-def pair_kernel(place_ref, *refs):
-    *parts, other_ref, out_ref, sems = refs
-    n = len(parts)
-    core = place_ref[n]
-    copies = []
-    for i, part in enumerate(parts):
-        copies.append(pltpu.make_async_copy(part, out_ref.at[place_ref[i], core], sems.at[0, i]))
-        copies.append(pltpu.make_async_copy(other_ref.at[i], out_ref.at[place_ref[i], 1 - core], sems.at[1, i]))
-    for copy in copies:
-        copy.start()
-    for copy in copies:
-        copy.wait()
-
-
-def first_kernel(rows_ref, weights_ref, target_ref, expo_ref, product_ref, total_ref, column_ref):
+def half_kernel(rows_ref, weights_ref, target_ref, expo_ref, product_ref, total_ref, sums_ref):
     groups, both, _ = rows_ref.shape
     count = both // 2
-    nx, nc, _, width, _ = weights_ref.shape
+    nx, _, width, _ = weights_ref.shape
     for j in range(groups):
         total = jnp.zeros((1, count), f32)
-        for i in range(nx * nc):
+        for i in range(nx):
             place = (slice(width * i, width * (i + 1)), slice(count * j, count * (j + 1)))
-            weights = weights_ref.at[i // nc, i % nc]
-            target = jnp.exp(dot(weights[0], rows_ref[j, :count], NT) * teacher_scale)
-            logits = dot(weights[1], rows_ref[j, count:], NT) * student_scale
-            expo = jnp.exp(logits)
+            target = jnp.exp2(dot(weights_ref[i, 0], rows_ref[j, :count], NT) * (teacher_scale * log2_e))
+            score = dot(weights_ref[i, 1], rows_ref[j, count:], NT)
+            expo = jnp.exp2(score * (student_scale * log2_e))
             total = total + jnp.sum(expo, axis=0, keepdims=True)
             target_ref[place] = target.astype(bf16)
             expo_ref[place] = expo.astype(bf16)
-            product_ref[place] = (target * logits).astype(bf16)
+            product_ref[place] = (target * score).astype(bf16)
         per = count // LANES
         total_ref[per * j : per * (j + 1)] = fold(total)
-    ones = jnp.ones((1, groups * count), f32)
-    spread(column_ref, fold(matvec(ones, target_ref[...], NT)))
-
-
-def column_kernel(parts_ref, expo_ref, column_ref):
+    sums_ref[...] = fold(matvec(jnp.ones((1, groups * count), f32), target_ref[...], NT))
+
+
+def spread_halves(core_ref, out_ref, own, other):
+    core = core_ref[0]
+    lines = own.shape[0]
+    for i in range(out_ref.shape[0]):
+        out_ref[i, pl.ds(pl.multiple_of(core * lines, lines), lines)] = own
+        out_ref[i, pl.ds(pl.multiple_of((1 - core) * lines, lines), lines)] = other
+
+
+def half_columns(core_ref, parts_ref, columns):
+    columns[...] = 1.0 / total_of(parts_ref)
+    core = core_ref[0]
+    lines = columns.shape[0] // 2
+    own = columns[pl.ds(pl.multiple_of(core * lines, lines), lines), :]
+    other = columns[pl.ds(pl.multiple_of((1 - core) * lines, lines), lines), :]
+    return unfold(own), unfold(other)
+
+
+def join_first_kernel(core_ref, own_ref, other_ref, column_ref):
+    spread_halves(core_ref, column_ref, own_ref[...], other_ref[...])
+
+
+def column_kernel(core_ref, parts_ref, own_ref, other_ref, column_ref):
     row = unfold(1.0 / total_of(parts_ref))
-    spread(column_ref, fold(matvec(row, expo_ref[...], NT)))
-
-
-def row_kernel(parts_ref, expo_ref, out_ref):
-    column = unfold(1.0 / total_of(parts_ref))
-    spread(out_ref, fold(matvec(column, expo_ref[...], NN)))
-
-
-def second_row_kernel(parts_ref, expo_ref, total_ref, out_ref):
-    column = unfold(1.0 / total_of(parts_ref))
-    sums = fold(matvec(column, expo_ref[...], NN))
-    spread(out_ref, jnp.concatenate([sums, total_ref[...]], axis=0))
-
-
-def last_row_kernel(parts_ref, expo_ref, product_ref, out_ref):
-    column = unfold(1.0 / total_of(parts_ref))
-    sums = fold(matvec(column, expo_ref[...], NN))
-    cross = fold(matvec(column, product_ref[...], NN))
+    spread_halves(core_ref, column_ref, fold(matvec(row, own_ref[...], NT)), fold(matvec(row, other_ref[...], NT)))
+
+
+def third_column_kernel(core_ref, parts_ref, own_ref, other_ref, column_ref, total_ref):
+    both = total_of(parts_ref)
+    lines = both.shape[0] // 2
+    row = unfold(1.0 / both[:lines])
+    spread_halves(core_ref, column_ref, fold(matvec(row, own_ref[...], NT)), fold(matvec(row, other_ref[...], NT)))
+    total_ref[...] = both[lines:]
+
+
+def row_kernel(core_ref, parts_ref, own_ref, other_ref, out_ref, columns):
+    own, other = half_columns(core_ref, parts_ref, columns)
+    spread(out_ref, fold(matvec(own, own_ref[...], NN) + matvec(other, other_ref[...], NN)))
+
+
+def second_row_kernel(core_ref, parts_ref, own_ref, other_ref, own_total_ref, other_total_ref, out_ref, columns):
+    own, other = half_columns(core_ref, parts_ref, columns)
+    sums = fold(matvec(own, own_ref[...], NN) + matvec(other, other_ref[...], NN))
+    spread(out_ref, jnp.concatenate([sums, own_total_ref[...] + other_total_ref[...]], axis=0))
+
+
+def last_row_kernel(core_ref, parts_ref, own_ref, other_ref, own_product_ref, other_product_ref, out_ref, columns):
+    own, other = half_columns(core_ref, parts_ref, columns)
+    sums = fold(matvec(own, own_ref[...], NN) + matvec(other, other_ref[...], NN))
+    cross = fold(matvec(own, own_product_ref[...], NN) + matvec(other, other_product_ref[...], NN)) * student_scale
     spread(out_ref, jnp.concatenate([sums, cross], axis=0))
 
 
 def add_kernel(parts_ref, out_ref):
     spread(out_ref, total_of(parts_ref))
-
-
-def third_column_kernel(parts_ref, expo_ref, column_ref, total_ref):
-    both = total_of(parts_ref)
-    lines = both.shape[0] // 2
-    spread(column_ref, fold(matvec(unfold(1.0 / both[:lines]), expo_ref[...], NT)))
-    total_ref[...] = both[lines:]
 
 
 def pieces_of(row):
@@ -190,15 +201,12 @@
     return pieces.astype(bf16)
 
 
-def slope_kernel(core_ref, parts_ref, column_ref, total_ref, target_ref, expo_ref, rows_ref, out_ref, columns):
+def slope_kernel(which, core_ref, parts_ref, column_ref, total_ref, target_ref, expo_ref, rows_ref, out_ref, columns):
     groups, both, depth = rows_ref.shape
     count = both // 2
     n, width, _ = out_ref.shape
     width = width - 16
-    nc = target_ref.shape[0] // (n * width)
-    core = core_ref[0]
-    per = width // LANES
-    columns[...] = 1.0 / total_of(column_ref)
+    column = half_columns(core_ref, column_ref, columns)[which]
     sums = total_of(parts_ref)
     lines = sums.shape[0] // 2
     row = 1.0 / sums[:lines]
@@ -206,16 +214,14 @@
     partial = jnp.sum(jnp.log(student_total)) - jnp.sum(row * sums[lines:])
     row = unfold(row * student_scale)
     inverse = unfold(student_scale / student_total)
+    column = jnp.broadcast_to(column, (8, n * width)).T[:, 0:1]
     for i in range(n):
-        block = i * nc + core
-        column = jnp.concatenate([columns[pl.ds(block * per + k, 1), :] for k in range(per)], axis=1)
-        column = jnp.broadcast_to(column, (8, width)).T[:, 0:1]
-        start = pl.multiple_of(block * width, width)
         grad = jnp.zeros((width, depth), f32)
         for j in range(groups):
             lanes = slice(count * j, count * (j + 1))
-            target = target_ref[pl.ds(start, width), lanes].astype(f32) * column * row[:, lanes]
-            slope = (expo_ref[pl.ds(start, width), lanes].astype(f32) * inverse[:, lanes] - target).astype(bf16)
+            place = (slice(width * i, width * (i + 1)), lanes)
+            target = target_ref[place].astype(f32) * column[width * i : width * (i + 1)] * row[:, lanes]
+            slope = (expo_ref[place].astype(f32) * inverse[:, lanes] - target).astype(bf16)
             grad = grad + dot(slope, rows_ref[j, count:], NN)
         out_ref[i, :width] = grad.astype(out_ref.dtype)
         out_ref[i, width:] = pieces_of(jnp.full((1, depth), partial, f32)).astype(out_ref.dtype)
@@ -293,67 +299,66 @@
     parts = [weights] + [lax.ppermute(weights, "x", [(i, (i + k) % nx) for i in range(nx)]) for k in range(1, nx)]
     core = lax.axis_index("c").astype(jnp.int32).reshape(1)
     places = (lax.axis_index("x") - jnp.arange(nx, dtype=jnp.int32)) % nx
-    places, core, other_core, picked = lax.optimization_barrier(
-        (jnp.concatenate([places, core]), core, nc - 1 - core, picked)
-    )
+    places, core, picked = lax.optimization_barrier((places, core, picked))
     picked = exchange(picked, "z")
-    picked, parts[0] = lax.optimization_barrier((picked, parts[0]))
+    picked, parts[2] = lax.optimization_barrier((picked, parts[2]))
     picked = call(divide_kernel, shape((ny, 2 * nz * count, depth), bf16), picked)
-    picked, *parts[1:] = lax.optimization_barrier((picked, *parts[1:]))
-    parts = [far(part) for part in parts]
-    stacked = call(
-        stack_kernel,
+    picked = exchange(picked, "y")
+    picked, *parts = lax.optimization_barrier((picked, *parts))
+    own_weights = call(
+        place_kernel,
         shape((nx, *weights.shape), bf16),
-        *parts,
-        place={i: pltpu.HBM for i in range(nx)},
+        places, *parts,
+        place={0: pltpu.SMEM, **{1 + i: pl.ANY for i in range(nx)}},
         scratch=[sems(nx)],
     )
-    other = lax.ppermute(stacked, "c", [(i, (i + 1) % nc) for i in range(nc)])
-    weights = call(
-        pair_kernel,
-        held((nx, nc, *weights.shape), bf16),
-        places, *parts, far(other),
-        place={0: pltpu.SMEM, **{1 + i: pltpu.HBM for i in range(nx + 1)}},
-        scratch=[pltpu.SemaphoreType.DMA((nc, nx))],
-    )
-    picked = exchange(picked, "y")
-
+    other_weights = lax.ppermute(own_weights, "c", [(i, (i + 1) % nc) for i in range(nc)])
+
+    matrix = held((nx * width, rows), bf16)
+    half_out = (matrix, matrix, matrix, shape((lines, LANES), f32), shape((column_lines // nc, LANES), f32))
+    own_target, own_expo, own_product, own_total, own_sums = call(half_kernel, half_out, picked, own_weights)
+    other_target, other_expo, other_product, other_total, other_sums = call(half_kernel, half_out, picked, other_weights)
+    targets = (own_target, other_target)
+
+    smem = {0: pltpu.SMEM}
+    scratch = [pltpu.VMEM((column_lines, LANES), f32)]
     column_out = shape((nx * nc, column_lines, LANES), f32)
     row_out = shape((ny, lines, LANES), f32)
     rows_out = shape((ny, 2 * lines, LANES), f32)
-    matrix = held((columns, rows), bf16)
-    target, expo, product, student_total, column = call(
-        first_kernel, (matrix, matrix, matrix, shape((lines, LANES), f32), column_out), picked, weights
-    )
-    column = exchange(column, ("x", "c"))
-    row = call(row_kernel, row_out, column, target)
+    column = call(join_first_kernel, column_out, core, own_sums, other_sums, place=smem)
+    column = exchange(column, ("c", "x"))
+    row = call(row_kernel, row_out, core, column, *targets, place=smem, scratch=scratch)
     row = exchange(row, "y")
     row = call(add_kernel, shape((nz, lines, LANES), f32), row)
     row = exchange(row, "z")
 
-    column = call(column_kernel, column_out, row, target)
-    column = exchange(column, ("x", "c"))
-    row = call(second_row_kernel, rows_out, column, target, student_total)
+    column = call(column_kernel, column_out, core, row, *targets, place=smem)
+    column = exchange(column, ("c", "x"))
+    row = call(second_row_kernel, rows_out, core, column, *targets, own_total, other_total, place=smem, scratch=scratch)
     row = exchange(row, "y")
     row = call(add_kernel, shape((nz, 2 * lines, LANES), f32), row)
     row = exchange(row, "z")
 
-    column, student_total = call(third_column_kernel, (column_out, shape((lines, LANES), f32)), row, target)
-    column = exchange(column, ("x", "c"))
-    row = call(last_row_kernel, rows_out, column, target, product)
+    column, student_total = call(
+        third_column_kernel, (column_out, shape((lines, LANES), f32)), core, row, *targets, place=smem
+    )
+    column = exchange(column, ("c", "x"))
+    row = call(
+        last_row_kernel, rows_out, core, column, *targets, own_product, other_product, place=smem, scratch=scratch
+    )
     row = exchange(row, "y")
     row = call(add_kernel, shape((nz, 2 * lines, LANES), f32), row)
     row = exchange(row, "z")
 
     halves = []
-    for which, kind in ((other_core, bf16), (core, f32)):
+    for which, kind, target, expo in ((1, bf16, other_target, other_expo), (0, f32, own_target, own_expo)):
         halves.append(
             call(
-                slope_kernel,
+                functools.partial(slope_kernel, which),
                 shape((nx, width + 16, depth), kind),
-                which, row, column, student_total, target, expo, picked,
-                place={0: pltpu.SMEM},
-                scratch=[pltpu.VMEM((column_lines, LANES), f32)],
+                core, row, column, student_total, target, expo, picked,
+                place=smem,
+                scratch=scratch,
             )
         )
     other = lax.ppermute(halves[0], "c", [(i, (i + 1) % nc) for i in range(nc)])

time: 200 us -> 191 us (0.955)
  waiting for transfers between devices: 24.3 us -> 14.7 us
  starting transfers between devices: 37.9 us -> 46.1 us
  Pallas kernels: 20.8 us -> 17.3 us
  blocking collectives: 114 us -> 111 us
    all_to_all x2, waiting for transfers between devices: 15.4 us -> 1.71 us  [exchange(): return lax.all_to_all(values, axes, 0, 0, tiled=True)]
    ppermute x1, starting transfers between devices: 2.45 us -> 9.5 us  [per_device(): lax.ppermute(own_weights, 'c', [(i, (i + 1) % nc) for i in range(nc)])]
    ppermute x3, waiting for transfers between devices: 8.58 us -> 12.3 us  [per_device(): lax.ppermute(weights, 'x', [(i, (i + k) % nx) for i in range(nx)])]
    pallas_call x18 -> x19, Pallas kernels: 20.8 us -> 17.3 us  [call(): pl.pallas_call(kernel, out_shape=outs, in_specs=[pl.BlockSpec(memory_spac...]
    all_to_all x10, blocking collectives: 114 us -> 111 us  [exchange(): return lax.all_to_all(values, axes, 0, 0, tiled=True)]
  transfers between devices with their start and end apart: 7 -> 7, of which waited for: 5 -> 6; matrix products, arithmetic and copies ran while one was open for 0% -> 0% of each run, Pallas kernels for 3% -> 2%
where the time goes in v4:
time: 191 us; the launch traced here: 190 us
  blocking collectives  111 us (58%)
  starting transfers between devices  46.1 us (24%)
  Pallas kernels  17.3 us (9%)
  waiting for transfers between devices  14.7 us (8%)
    all_to_all x10, blocking collectives, exchange(): return lax.all_to_all(values, axes, 0, 0, tiled=True)  111 us
    all_to_all x2, starting transfers between devices, exchange(): return lax.all_to_all(values, axes, 0, 0, tiled=True)  19.9 us
    pallas_call x19, Pallas kernels, call(): pl.pallas_call(kernel, out_shape=outs, in_specs=[pl.BlockSpec(memory_spac...  17.3 us
    ppermute x3, waiting for transfers between devices, per_device(): lax.ppermute(weights, 'x', [(i, (i + k) % nx) for i in range(nx)])  12.3 us
    ppermute x3, starting transfers between devices, per_device(): lax.ppermute(weights, 'x', [(i, (i + k) % nx) for i in range(nx)])  10.9 us
    ppermute x1, starting transfers between devices, per_device(): lax.ppermute(own_weights, 'c', [(i, (i + 1) % nc) for i in range(nc)])  9.5 us
    ppermute x1, starting transfers between devices, per_device(): other = lax.ppermute(halves[0], 'c', [(i, (i + 1) % nc) for i in range(nc)])  5.68 us
  transfers between devices with their start and end apart: 7, of which 6 were waited for; matrix products, arithmetic and copies ran while one was open for 0% of the time, Pallas kernels for 2%

profile of v4, /device:TPU:1, one launch (start us, length us, event | category | flops | bytes accessed | tf_op | source)
XLA Modules:
  0.0 189.8 jit_solution(5541262383738052763)
XLA Ops:
  0.6 2.1 %shard_map.68 = bf16[16,32,256]{2,1,0:T(8,128)(2,1)} custom-call(s32[16]{0:T(128)} %mask_ref.1, bf16[256,256]{1,0:T(8,128)(2,1)} %sp_ref.1, bf16[256,256]{1,0:T(8,128)(2,1)} %tp_ref.1), custom_call_target="tpu_custom_call" | custom-call | tf_op jit(solution)/shard_map/pallas_call | solution.py:255
  2.8 15.8 %all-to-all-start = ((bf16[16,32,256]{2,1,0:T(8,128)(2,1)}), bf16[16,32,256]{2,1,0:T(8,128)(2,1)S(1)}, u32[]{:S(2)}, u32[]{:S(2)}) async-start(bf16[16,32,256]{2,1,0:T(8,128)(2,1)} %shard_map.68), calls=%async_computation | async-start | bytes 524288 | tf_op jit(solution)/shard_map/all_to_all | solution.py:276
  19.7 4.7 %collective-permute-start = (bf16[2,256,256]{2,1,0:T(8,128)(2,1)S(1)}, bf16[2,256,256]{2,1,0:T(8,128)(2,1)S(1)}, u32[]{:S(2)}, u32[]{:S(2)}) collective-permute-start(bf16[2,256,256]{2,1,0:T(8,128)(2,1)S(1)} %shard_map.69.refs_0_), channel_id=1, source_target_pairs={{0,4},{2,6},{4,0},{6,2},{1,5},{3,7},{5,1},{7,3},{8,12},{10,14},{12... | collective-permute-start | bytes 786440 | tf_op jit(solution)/shard_map/ppermute | solution.py:299
  24.4 5.6 %collective-permute-done.refs_2_ = bf16[2,256,256]{2,1,0:T(8,128)(2,1)S(1)} collective-permute-done((bf16[2,256,256]{2,1,0:T(8,128)(2,1)S(1)}, bf16[2,256,256]{2,1,0:T(8,128)(2,1)S(1)}, u32[]{:S(2)}, u32[]{:S(2)}) %collective-permute-start) | collective-permute-done | bytes 262176 | tf_op jit(solution)/shard_map/ppermute | solution.py:299
  30.0 1.7 all-to-all-done.rows_ref
  32.7 4.2 %all-to-all-start.1 = ((bf16[4,512,256]{2,1,0:T(8,128)(2,1)}), bf16[4,512,256]{2,1,0:T(8,128)(2,1)S(1)}, u32[]{:S(2)}, u32[]{:S(2)}) async-start(bf16[4,512,256]{2,1,0:T(8,128)(2,1)} %shard_map.70), calls=%async_computation.1 | async-start | bytes 2097152 | tf_op jit(solution)/shard_map/all_to_all | solution.py:276
  36.9 4.4 %collective-permute-start.2 = (bf16[2,256,256]{2,1,0:T(8,128)(2,1)S(1)}, bf16[2,256,256]{2,1,0:T(8,128)(2,1)S(1)}, u32[]{:S(2)}, u32[]{:S(2)}) collective-permute-start(bf16[2,256,256]{2,1,0:T(8,128)(2,1)S(1)} %shard_map.69.refs_0_), channel_id=1, source_target_pairs={{0,6},{2,0},{4,2},{6,4},{1,7},{3,1},{5,3},{7,5},{8,14},{10,8},{12,... | collective-permute-start | bytes 786440 | tf_op jit(solution)/shard_map/ppermute | solution.py:299
  41.3 1.9 %collective-permute-start.1 = (bf16[2,256,256]{2,1,0:T(8,128)(2,1)S(1)}, bf16[2,256,256]{2,1,0:T(8,128)(2,1)S(1)}, u32[]{:S(2)}, u32[]{:S(2)}) collective-permute-start(bf16[2,256,256]{2,1,0:T(8,128)(2,1)S(1)} %shard_map.69.refs_0_), channel_id=1, source_target_pairs={{0,2},{2,4},{4,6},{6,0},{1,3},{3,5},{5,7},{7,1},{8,10},{10,12},{12... | collective-permute-start | bytes 786440 | tf_op jit(solution)/shard_map/ppermute | solution.py:299
  43.2 1.4 collective-permute-done.2.refs_3_
  44.6 5.3 %collective-permute-done.1.refs_1_ = bf16[2,256,256]{2,1,0:T(8,128)(2,1)S(1)} collective-permute-done((bf16[2,256,256]{2,1,0:T(8,128)(2,1)S(1)}, bf16[2,256,256]{2,1,0:T(8,128)(2,1)S(1)}, u32[]{:S(2)}, u32[]{:S(2)}) %collective-permute-start.1) | collective-permute-done | bytes 262176 | tf_op jit(solution)/shard_map/ppermute | solution.py:299
  50.6 9.5 %collective-permute-start.3 = (bf16[4,2,256,256]{3,2,1,0:T(8,128)(2,1)S(1)}, bf16[4,2,256,256]{3,2,1,0:T(8,128)(2,1)S(1)}, u32[]{:S(2)}, u32[]{:S(2)}) collective-permute-start(bf16[4,2,256,256]{3,2,1,0:T(8,128)(2,1)S(1)} %shard_map.71.weights_ref), channel_id=1, source_target_pairs={{0,1},{1,0},{2,3},{3,2},{4,5},{5,4},{6,7},{7,6},{8,9},{9,8},{10,11... | collective-permute-start | bytes 3145736 | tf_op jit(solution)/shard_map/ppermute | solution.py:315
  60.1 1.8 shard_map.72
  62.4 1.8 shard_map.73
  64.2 7.7 %all_to_all.60.parts_ref = f32[8,16,128]{2,1,0:T(8,128)S(1)} all-to-all(f32[8,16,128]{2,1,0:T(8,128)S(1)} %shard_map.74), channel_id=1, replica_groups=mesh['z'=16,'y'=4,'x'=4,'c'=2] {'c','x'}, dimensions={0} | all-to-all | bytes 131072 | tf_op jit(solution)/shard_map/all_to_all | solution.py:276
  72.6 8.5 %all_to_all.61.parts_ref = f32[4,8,128]{2,1,0:T(8,128)S(1)} all-to-all(f32[4,8,128]{2,1,0:T(8,128)S(1)} %shard_map.75), channel_id=1, replica_groups=mesh['z'=16,'y'=4,'x'=4,'c'=2] {'y'}, dimensions={0} | all-to-all | bytes 32768 | tf_op jit(solution)/shard_map/all_to_all | solution.py:276
  81.2 17.7 %all_to_all.62.parts_ref = f32[16,8,128]{2,1,0:T(8,128)S(1)} all-to-all(f32[16,8,128]{2,1,0:T(8,128)S(1)} %shard_map.76), channel_id=1, replica_groups=mesh['z'=16,'y'=4,'x'=4,'c'=2] {'z'}, dimensions={0} | all-to-all | bytes 131072 | tf_op jit(solution)/shard_map/all_to_all | solution.py:276
  100.0 10.9 %all_to_all.63.parts_ref = f32[8,16,128]{2,1,0:T(8,128)S(1)} all-to-all(f32[8,16,128]{2,1,0:T(8,128)S(1)} %shard_map.77), channel_id=1, replica_groups=mesh['z'=16,'y'=4,'x'=4,'c'=2] {'c','x'}, dimensions={0} | all-to-all | bytes 131072 | tf_op jit(solution)/shard_map/all_to_all | solution.py:276
  111.6 6.7 %all_to_all.64.parts_ref = f32[4,16,128]{2,1,0:T(8,128)S(1)} all-to-all(f32[4,16,128]{2,1,0:T(8,128)S(1)} %shard_map.78), channel_id=1, replica_groups=mesh['z'=16,'y'=4,'x'=4,'c'=2] {'y'}, dimensions={0} | all-to-all | bytes 65536 | tf_op jit(solution)/shard_map/all_to_all | solution.py:276
  118.3 14.5 %all_to_all.65.parts_ref = f32[16,16,128]{2,1,0:T(8,128)S(1)} all-to-all(f32[16,16,128]{2,1,0:T(8,128)S(1)} %shard_map.79), channel_id=1, replica_groups=mesh['z'=16,'y'=4,'x'=4,'c'=2] {'z'}, dimensions={0} | all-to-all | bytes 262144 | tf_op jit(solution)/shard_map/all_to_all | solution.py:276
  134.0 11.0 %all_to_all.66.parts_ref.column_ref = f32[8,16,128]{2,1,0:T(8,128)S(1)} all-to-all(f32[8,16,128]{2,1,0:T(8,128)S(1)} %get-tuple-element.48), channel_id=1, replica_groups=mesh['z'=16,'y'=4,'x'=4,'c'=2] {'c','x'}, dimensions={0} | all-to-all | bytes 131072 | tf_op jit(solution)/shard_map/all_to_all | solution.py:276
  146.3 6.7 %all_to_all.67.parts_ref = f32[4,16,128]{2,1,0:T(8,128)S(1)} all-to-all(f32[4,16,128]{2,1,0:T(8,128)S(1)} %shard_map.81), channel_id=1, replica_groups=mesh['z'=16,'y'=4,'x'=4,'c'=2] {'y'}, dimensions={0} | all-to-all | bytes 65536 | tf_op jit(solution)/shard_map/all_to_all | solution.py:276
  153.0 15.3 %all_to_all.68.parts_ref = f32[16,16,128]{2,1,0:T(8,128)S(1)} all-to-all(f32[16,16,128]{2,1,0:T(8,128)S(1)} %shard_map.82), channel_id=1, replica_groups=mesh['z'=16,'y'=4,'x'=4,'c'=2] {'z'}, dimensions={0} | all-to-all | bytes 262144 | tf_op jit(solution)/shard_map/all_to_all | solution.py:276
  169.6 5.7 %collective-permute-start.4 = (bf16[4,272,256]{2,1,0:T(8,128)(2,1)S(1)}, bf16[4,272,256]{2,1,0:T(8,128)(2,1)S(1)}, u32[]{:S(2)}, u32[]{:S(2)}) collective-permute-start(bf16[4,272,256]{2,1,0:T(8,128)(2,1)S(1)} %shard_map.84), channel_id=1, source_target_pairs={{0,1},{1,0},{2,3},{3,2},{4,5},{5,4},{6,7},{7,6},{8,9},{9,8},{10,11... | collective-permute-start | bytes 1671176 | tf_op jit(solution)/shard_map/ppermute | solution.py:364
  177.0 11.9 %all_to_all.69.refs_0_ = bf16[4,272,256]{2,1,0:T(8,128)(2,1)S(1)} all-to-all(bf16[4,272,256]{2,1,0:T(8,128)(2,1)S(1)} %shard_map.85), channel_id=1, replica_groups=mesh['z'=16,'y'=4,'x'=4,'c'=2] {'x'}, dimensions={0} | all-to-all | bytes 1114112 | tf_op jit(solution)/shard_map/all_to_all | solution.py:276
  (22 shorter events, 12.2 us)
Async XLA Ops:
  2.8 28.9 %all-to-all-start = ((bf16[16,32,256]{2,1,0:T(8,128)(2,1)}), bf16[16,32,256]{2,1,0:T(8,128)(2,1)S(1)}, u32[]{:S(2)}, u32[]{:S(2)}) async-start(bf16[16,32,256]{2,1,0:T(8,128)(2,1)} %shard_map.68), calls=%async_computation | async-start | bytes 524288 | tf_op jit(solution)/shard_map/all_to_all | solution.py:276
  19.7 10.3 %collective-permute-start = (bf16[2,256,256]{2,1,0:T(8,128)(2,1)S(1)}, bf16[2,256,256]{2,1,0:T(8,128)(2,1)S(1)}, u32[]{:S(2)}, u32[]{:S(2)}) collective-permute-start(bf16[2,256,256]{2,1,0:T(8,128)(2,1)S(1)} %shard_map.69.refs_0_), channel_id=1, source_target_pairs={{0,4},{2,6},{4,0},{6,2},{1,5},{3,7},{5,1},{7,3},{8,12},{10,14},{12... | collective-permute-start | bytes 786440 | tf_op jit(solution)/shard_map/ppermute | solution.py:299
  32.7 17.2 %all-to-all-start.1 = ((bf16[4,512,256]{2,1,0:T(8,128)(2,1)}), bf16[4,512,256]{2,1,0:T(8,128)(2,1)S(1)}, u32[]{:S(2)}, u32[]{:S(2)}) async-start(bf16[4,512,256]{2,1,0:T(8,128)(2,1)} %shard_map.70), calls=%async_computation.1 | async-start | bytes 2097152 | tf_op jit(solution)/shard_map/all_to_all | solution.py:276
  36.9 7.7 %collective-permute-start.2 = (bf16[2,256,256]{2,1,0:T(8,128)(2,1)S(1)}, bf16[2,256,256]{2,1,0:T(8,128)(2,1)S(1)}, u32[]{:S(2)}, u32[]{:S(2)}) collective-permute-start(bf16[2,256,256]{2,1,0:T(8,128)(2,1)S(1)} %shard_map.69.refs_0_), channel_id=1, source_target_pairs={{0,6},{2,0},{4,2},{6,4},{1,7},{3,1},{5,3},{7,5},{8,14},{10,8},{12,... | collective-permute-start | bytes 786440 | tf_op jit(solution)/shard_map/ppermute | solution.py:299
  41.3 8.6 %collective-permute-start.1 = (bf16[2,256,256]{2,1,0:T(8,128)(2,1)S(1)}, bf16[2,256,256]{2,1,0:T(8,128)(2,1)S(1)}, u32[]{:S(2)}, u32[]{:S(2)}) collective-permute-start(bf16[2,256,256]{2,1,0:T(8,128)(2,1)S(1)} %shard_map.69.refs_0_), channel_id=1, source_target_pairs={{0,2},{2,4},{4,6},{6,0},{1,3},{3,5},{5,7},{7,1},{8,10},{10,12},{12... | collective-permute-start | bytes 786440 | tf_op jit(solution)/shard_map/ppermute | solution.py:299
  50.6 11.8 %collective-permute-start.3 = (bf16[4,2,256,256]{3,2,1,0:T(8,128)(2,1)S(1)}, bf16[4,2,256,256]{3,2,1,0:T(8,128)(2,1)S(1)}, u32[]{:S(2)}, u32[]{:S(2)}) collective-permute-start(bf16[4,2,256,256]{3,2,1,0:T(8,128)(2,1)S(1)} %shard_map.71.weights_ref), channel_id=1, source_target_pairs={{0,1},{1,0},{2,3},{3,2},{4,5},{5,4},{6,7},{7,6},{8,9},{9,8},{10,11... | collective-permute-start | bytes 3145736 | tf_op jit(solution)/shard_map/ppermute | solution.py:315
  169.6 7.2 %collective-permute-start.4 = (bf16[4,272,256]{2,1,0:T(8,128)(2,1)S(1)}, bf16[4,272,256]{2,1,0:T(8,128)(2,1)S(1)}, u32[]{:S(2)}, u32[]{:S(2)}) collective-permute-start(bf16[4,272,256]{2,1,0:T(8,128)(2,1)S(1)} %shard_map.84), channel_id=1, source_target_pairs={{0,1},{1,0},{2,3},{3,2},{4,5},{5,4},{6,7},{7,6},{8,9},{9,8},{10,11... | collective-permute-start | bytes 1671176 | tf_op jit(solution)/shard_map/ppermute | solution.py:364
  176.5 12.3 %copy-start = (bf16[256,256]{1,0:T(8,128)(2,1)S(1)}, bf16[256,256]{1,0:T(8,128)(2,1)}, u32[]{:S(2)}) copy-start(bf16[256,256]{1,0:T(8,128)(2,1)} %refs_1_.1) | copy-start | bytes 393220

commit v5 on v4

--- a/solution.py
+++ b/solution.py
@@ -49,14 +49,15 @@
 
 
 def spread(out_ref, tile):
+    tile = tile.astype(out_ref.dtype)
     for i in range(out_ref.shape[0]):
         out_ref[i] = tile
 
 
 def total_of(parts_ref):
-    total = parts_ref[0]
+    total = parts_ref[0].astype(f32)
     for i in range(1, parts_ref.shape[0]):
-        total = total + parts_ref[i]
+        total = total + parts_ref[i].astype(f32)
     return total
 
 
@@ -138,11 +139,8 @@
 
 
 def spread_halves(core_ref, out_ref, own, other):
-    core = core_ref[0]
-    lines = own.shape[0]
-    for i in range(out_ref.shape[0]):
-        out_ref[i, pl.ds(pl.multiple_of(core * lines, lines), lines)] = own
-        out_ref[i, pl.ds(pl.multiple_of((1 - core) * lines, lines), lines)] = other
+    first = core_ref[0] == 0
+    spread(out_ref, jnp.concatenate([jnp.where(first, own, other), jnp.where(first, other, own)], axis=0))
 
 
 def half_columns(core_ref, parts_ref, columns):
@@ -322,7 +320,7 @@
 
     smem = {0: pltpu.SMEM}
     scratch = [pltpu.VMEM((column_lines, LANES), f32)]
-    column_out = shape((nx * nc, column_lines, LANES), f32)
+    column_out = shape((nx * nc, column_lines, LANES), bf16)
     row_out = shape((ny, lines, LANES), f32)
     rows_out = shape((ny, 2 * lines, LANES), f32)
     column = call(join_first_kernel, column_out, core, own_sums, other_sums, place=smem)
@@ -336,7 +334,7 @@
     column = exchange(column, ("c", "x"))
     row = call(second_row_kernel, rows_out, core, column, *targets, own_total, other_total, place=smem, scratch=scratch)
     row = exchange(row, "y")
-    row = call(add_kernel, shape((nz, 2 * lines, LANES), f32), row)
+    row = call(add_kernel, shape((nz, 2 * lines, LANES), bf16), row)
     row = exchange(row, "z")
 
     column, student_total = call(
@@ -347,7 +345,7 @@
         last_row_kernel, rows_out, core, column, *targets, own_product, other_product, place=smem, scratch=scratch
     )
     row = exchange(row, "y")
-    row = call(add_kernel, shape((nz, 2 * lines, LANES), f32), row)
+    row = call(add_kernel, shape((nz, 2 * lines, LANES), bf16), row)
     row = exchange(row, "z")
 
     halves = []

time: 191 us -> 187 us (0.979)
  blocking collectives: 111 us -> 108 us
    all_to_all x10, blocking collectives: 111 us -> 108 us  [exchange(): return lax.all_to_all(values, axes, 0, 0, tiled=True)]
where the time goes in v5:
time: 187 us; the launch traced here: 186 us
  blocking collectives  108 us (58%)
  starting transfers between devices  45.2 us (24%)
  Pallas kernels  17.3 us (9%)
  waiting for transfers between devices  14.7 us (8%)
    all_to_all x10, blocking collectives, exchange(): return lax.all_to_all(values, axes, 0, 0, tiled=True)  108 us
    all_to_all x2, starting transfers between devices, exchange(): return lax.all_to_all(values, axes, 0, 0, tiled=True)  19.9 us
    pallas_call x19, Pallas kernels, call(): pl.pallas_call(kernel, out_shape=outs, in_specs=[pl.BlockSpec(memory_spac...  17.3 us
    ppermute x3, waiting for transfers between devices, per_device(): lax.ppermute(weights, 'x', [(i, (i + k) % nx) for i in range(nx)])  12.3 us
    ppermute x3, starting transfers between devices, per_device(): lax.ppermute(weights, 'x', [(i, (i + k) % nx) for i in range(nx)])  10.9 us
    ppermute x1, starting transfers between devices, per_device(): lax.ppermute(own_weights, 'c', [(i, (i + 1) % nc) for i in range(nc)])  9.5 us
    ppermute x1, starting transfers between devices, per_device(): other = lax.ppermute(halves[0], 'c', [(i, (i + 1) % nc) for i in range(nc)])  4.78 us
  transfers between devices with their start and end apart: 7, of which 6 were waited for; matrix products, arithmetic and copies ran while one was open for 0% of the time, Pallas kernels for 2%

profile of v5, /device:TPU:1, one launch (start us, length us, event | category | flops | bytes accessed | tf_op | source)
XLA Modules:
  0.0 186.2 jit_solution(1857414407894529370)
XLA Ops:
  0.6 2.1 %shard_map.68 = bf16[16,32,256]{2,1,0:T(8,128)(2,1)} custom-call(s32[16]{0:T(128)} %mask_ref.1, bf16[256,256]{1,0:T(8,128)(2,1)} %sp_ref.1, bf16[256,256]{1,0:T(8,128)(2,1)} %tp_ref.1), custom_call_target="tpu_custom_call" | custom-call | tf_op jit(solution)/shard_map/pallas_call | solution.py:253
  2.8 15.8 %all-to-all-start = ((bf16[16,32,256]{2,1,0:T(8,128)(2,1)}), bf16[16,32,256]{2,1,0:T(8,128)(2,1)S(1)}, u32[]{:S(2)}, u32[]{:S(2)}) async-start(bf16[16,32,256]{2,1,0:T(8,128)(2,1)} %shard_map.68), calls=%async_computation | async-start | bytes 524288 | tf_op jit(solution)/shard_map/all_to_all | solution.py:274
  19.7 4.7 %collective-permute-start = (bf16[2,256,256]{2,1,0:T(8,128)(2,1)S(1)}, bf16[2,256,256]{2,1,0:T(8,128)(2,1)S(1)}, u32[]{:S(2)}, u32[]{:S(2)}) collective-permute-start(bf16[2,256,256]{2,1,0:T(8,128)(2,1)S(1)} %shard_map.69.refs_0_), channel_id=1, source_target_pairs={{0,4},{2,6},{4,0},{6,2},{1,5},{3,7},{5,1},{7,3},{8,12},{10,14},{12... | collective-permute-start | bytes 786440 | tf_op jit(solution)/shard_map/ppermute | solution.py:297
  24.4 5.6 %collective-permute-done.refs_2_ = bf16[2,256,256]{2,1,0:T(8,128)(2,1)S(1)} collective-permute-done((bf16[2,256,256]{2,1,0:T(8,128)(2,1)S(1)}, bf16[2,256,256]{2,1,0:T(8,128)(2,1)S(1)}, u32[]{:S(2)}, u32[]{:S(2)}) %collective-permute-start) | collective-permute-done | bytes 262176 | tf_op jit(solution)/shard_map/ppermute | solution.py:297
  30.0 1.7 all-to-all-done.rows_ref
  32.7 4.2 %all-to-all-start.1 = ((bf16[4,512,256]{2,1,0:T(8,128)(2,1)}), bf16[4,512,256]{2,1,0:T(8,128)(2,1)S(1)}, u32[]{:S(2)}, u32[]{:S(2)}) async-start(bf16[4,512,256]{2,1,0:T(8,128)(2,1)} %shard_map.70), calls=%async_computation.1 | async-start | bytes 2097152 | tf_op jit(solution)/shard_map/all_to_all | solution.py:274
  36.9 4.4 %collective-permute-start.2 = (bf16[2,256,256]{2,1,0:T(8,128)(2,1)S(1)}, bf16[2,256,256]{2,1,0:T(8,128)(2,1)S(1)}, u32[]{:S(2)}, u32[]{:S(2)}) collective-permute-start(bf16[2,256,256]{2,1,0:T(8,128)(2,1)S(1)} %shard_map.69.refs_0_), channel_id=1, source_target_pairs={{0,6},{2,0},{4,2},{6,4},{1,7},{3,1},{5,3},{7,5},{8,14},{10,8},{12,... | collective-permute-start | bytes 786440 | tf_op jit(solution)/shard_map/ppermute | solution.py:297
  41.3 1.9 %collective-permute-start.1 = (bf16[2,256,256]{2,1,0:T(8,128)(2,1)S(1)}, bf16[2,256,256]{2,1,0:T(8,128)(2,1)S(1)}, u32[]{:S(2)}, u32[]{:S(2)}) collective-permute-start(bf16[2,256,256]{2,1,0:T(8,128)(2,1)S(1)} %shard_map.69.refs_0_), channel_id=1, source_target_pairs={{0,2},{2,4},{4,6},{6,0},{1,3},{3,5},{5,7},{7,1},{8,10},{10,12},{12... | collective-permute-start | bytes 786440 | tf_op jit(solution)/shard_map/ppermute | solution.py:297
  43.2 1.4 collective-permute-done.2.refs_3_
  44.6 5.3 %collective-permute-done.1.refs_1_ = bf16[2,256,256]{2,1,0:T(8,128)(2,1)S(1)} collective-permute-done((bf16[2,256,256]{2,1,0:T(8,128)(2,1)S(1)}, bf16[2,256,256]{2,1,0:T(8,128)(2,1)S(1)}, u32[]{:S(2)}, u32[]{:S(2)}) %collective-permute-start.1) | collective-permute-done | bytes 262176 | tf_op jit(solution)/shard_map/ppermute | solution.py:297
  50.6 9.5 %collective-permute-start.3 = (bf16[4,2,256,256]{3,2,1,0:T(8,128)(2,1)S(1)}, bf16[4,2,256,256]{3,2,1,0:T(8,128)(2,1)S(1)}, u32[]{:S(2)}, u32[]{:S(2)}) collective-permute-start(bf16[4,2,256,256]{3,2,1,0:T(8,128)(2,1)S(1)} %shard_map.71.weights_ref), channel_id=1, source_target_pairs={{0,1},{1,0},{2,3},{3,2},{4,5},{5,4},{6,7},{7,6},{8,9},{9,8},{10,11... | collective-permute-start | bytes 3145736 | tf_op jit(solution)/shard_map/ppermute | solution.py:313
  60.1 1.8 shard_map.72
  62.4 1.8 shard_map.73
  64.2 7.7 %all_to_all.60.parts_ref = bf16[8,16,128]{2,1,0:T(8,128)(2,1)S(1)} all-to-all(bf16[8,16,128]{2,1,0:T(8,128)(2,1)S(1)} %shard_map.74), channel_id=1, replica_groups=mesh['z'=16,'y'=4,'x'=4,'c'=2] {'c','x'}, dimensions={0} | all-to-all | bytes 65536 | tf_op jit(solution)/shard_map/all_to_all | solution.py:274
  72.6 8.5 %all_to_all.61.parts_ref = f32[4,8,128]{2,1,0:T(8,128)S(1)} all-to-all(f32[4,8,128]{2,1,0:T(8,128)S(1)} %shard_map.75), channel_id=1, replica_groups=mesh['z'=16,'y'=4,'x'=4,'c'=2] {'y'}, dimensions={0} | all-to-all | bytes 32768 | tf_op jit(solution)/shard_map/all_to_all | solution.py:274
  81.1 17.7 %all_to_all.62.parts_ref = f32[16,8,128]{2,1,0:T(8,128)S(1)} all-to-all(f32[16,8,128]{2,1,0:T(8,128)S(1)} %shard_map.76), channel_id=1, replica_groups=mesh['z'=16,'y'=4,'x'=4,'c'=2] {'z'}, dimensions={0} | all-to-all | bytes 131072 | tf_op jit(solution)/shard_map/all_to_all | solution.py:274
  100.0 10.7 %all_to_all.63.parts_ref = bf16[8,16,128]{2,1,0:T(8,128)(2,1)S(1)} all-to-all(bf16[8,16,128]{2,1,0:T(8,128)(2,1)S(1)} %shard_map.77), channel_id=1, replica_groups=mesh['z'=16,'y'=4,'x'=4,'c'=2] {'c','x'}, dimensions={0} | all-to-all | bytes 65536 | tf_op jit(solution)/shard_map/all_to_all | solution.py:274
  111.3 6.7 %all_to_all.64.parts_ref = f32[4,16,128]{2,1,0:T(8,128)S(1)} all-to-all(f32[4,16,128]{2,1,0:T(8,128)S(1)} %shard_map.78), channel_id=1, replica_groups=mesh['z'=16,'y'=4,'x'=4,'c'=2] {'y'}, dimensions={0} | all-to-all | bytes 65536 | tf_op jit(solution)/shard_map/all_to_all | solution.py:274
  118.0 14.2 %all_to_all.65.parts_ref = bf16[16,16,128]{2,1,0:T(8,128)(2,1)S(1)} all-to-all(bf16[16,16,128]{2,1,0:T(8,128)(2,1)S(1)} %shard_map.79), channel_id=1, replica_groups=mesh['z'=16,'y'=4,'x'=4,'c'=2] {'z'}, dimensions={0} | all-to-all | bytes 131072 | tf_op jit(solution)/shard_map/all_to_all | solution.py:274
  133.4 10.1 %all_to_all.66.parts_ref.column_ref = bf16[8,16,128]{2,1,0:T(8,128)(2,1)S(1)} all-to-all(bf16[8,16,128]{2,1,0:T(8,128)(2,1)S(1)} %get-tuple-element.48), channel_id=1, replica_groups=mesh['z'=16,'y'=4,'x'=4,'c'=2] {'c','x'}, dimensions={0} | all-to-all | bytes 65536 | tf_op jit(solution)/shard_map/all_to_all | solution.py:274
  144.8 6.7 %all_to_all.67.parts_ref = f32[4,16,128]{2,1,0:T(8,128)S(1)} all-to-all(f32[4,16,128]{2,1,0:T(8,128)S(1)} %shard_map.81), channel_id=1, replica_groups=mesh['z'=16,'y'=4,'x'=4,'c'=2] {'y'}, dimensions={0} | all-to-all | bytes 65536 | tf_op jit(solution)/shard_map/all_to_all | solution.py:274
  151.5 14.2 %all_to_all.68.parts_ref = bf16[16,16,128]{2,1,0:T(8,128)(2,1)S(1)} all-to-all(bf16[16,16,128]{2,1,0:T(8,128)(2,1)S(1)} %shard_map.82), channel_id=1, replica_groups=mesh['z'=16,'y'=4,'x'=4,'c'=2] {'z'}, dimensions={0} | all-to-all | bytes 131072 | tf_op jit(solution)/shard_map/all_to_all | solution.py:274
  167.0 4.8 %collective-permute-start.4 = (bf16[4,272,256]{2,1,0:T(8,128)(2,1)S(1)}, bf16[4,272,256]{2,1,0:T(8,128)(2,1)S(1)}, u32[]{:S(2)}, u32[]{:S(2)}) collective-permute-start(bf16[4,272,256]{2,1,0:T(8,128)(2,1)S(1)} %shard_map.84), channel_id=1, source_target_pairs={{0,1},{1,0},{2,3},{3,2},{4,5},{5,4},{6,7},{7,6},{8,9},{9,8},{10,11... | collective-permute-start | bytes 1671176 | tf_op jit(solution)/shard_map/ppermute | solution.py:362
  173.5 11.8 %all_to_all.69.refs_0_ = bf16[4,272,256]{2,1,0:T(8,128)(2,1)S(1)} all-to-all(bf16[4,272,256]{2,1,0:T(8,128)(2,1)S(1)} %shard_map.85), channel_id=1, replica_groups=mesh['z'=16,'y'=4,'x'=4,'c'=2] {'x'}, dimensions={0} | all-to-all | bytes 1114112 | tf_op jit(solution)/shard_map/all_to_all | solution.py:274
  (22 shorter events, 12.2 us)
Async XLA Ops:
  2.8 28.9 %all-to-all-start = ((bf16[16,32,256]{2,1,0:T(8,128)(2,1)}), bf16[16,32,256]{2,1,0:T(8,128)(2,1)S(1)}, u32[]{:S(2)}, u32[]{:S(2)}) async-start(bf16[16,32,256]{2,1,0:T(8,128)(2,1)} %shard_map.68), calls=%async_computation | async-start | bytes 524288 | tf_op jit(solution)/shard_map/all_to_all | solution.py:274
  19.7 10.3 %collective-permute-start = (bf16[2,256,256]{2,1,0:T(8,128)(2,1)S(1)}, bf16[2,256,256]{2,1,0:T(8,128)(2,1)S(1)}, u32[]{:S(2)}, u32[]{:S(2)}) collective-permute-start(bf16[2,256,256]{2,1,0:T(8,128)(2,1)S(1)} %shard_map.69.refs_0_), channel_id=1, source_target_pairs={{0,4},{2,6},{4,0},{6,2},{1,5},{3,7},{5,1},{7,3},{8,12},{10,14},{12... | collective-permute-start | bytes 786440 | tf_op jit(solution)/shard_map/ppermute | solution.py:297
  32.7 17.2 %all-to-all-start.1 = ((bf16[4,512,256]{2,1,0:T(8,128)(2,1)}), bf16[4,512,256]{2,1,0:T(8,128)(2,1)S(1)}, u32[]{:S(2)}, u32[]{:S(2)}) async-start(bf16[4,512,256]{2,1,0:T(8,128)(2,1)} %shard_map.70), calls=%async_computation.1 | async-start | bytes 2097152 | tf_op jit(solution)/shard_map/all_to_all | solution.py:274
  36.9 7.7 %collective-permute-start.2 = (bf16[2,256,256]{2,1,0:T(8,128)(2,1)S(1)}, bf16[2,256,256]{2,1,0:T(8,128)(2,1)S(1)}, u32[]{:S(2)}, u32[]{:S(2)}) collective-permute-start(bf16[2,256,256]{2,1,0:T(8,128)(2,1)S(1)} %shard_map.69.refs_0_), channel_id=1, source_target_pairs={{0,6},{2,0},{4,2},{6,4},{1,7},{3,1},{5,3},{7,5},{8,14},{10,8},{12,... | collective-permute-start | bytes 786440 | tf_op jit(solution)/shard_map/ppermute | solution.py:297
  41.3 8.6 %collective-permute-start.1 = (bf16[2,256,256]{2,1,0:T(8,128)(2,1)S(1)}, bf16[2,256,256]{2,1,0:T(8,128)(2,1)S(1)}, u32[]{:S(2)}, u32[]{:S(2)}) collective-permute-start(bf16[2,256,256]{2,1,0:T(8,128)(2,1)S(1)} %shard_map.69.refs_0_), channel_id=1, source_target_pairs={{0,2},{2,4},{4,6},{6,0},{1,3},{3,5},{5,7},{7,1},{8,10},{10,12},{12... | collective-permute-start | bytes 786440 | tf_op jit(solution)/shard_map/ppermute | solution.py:297
  50.6 11.8 %collective-permute-start.3 = (bf16[4,2,256,256]{3,2,1,0:T(8,128)(2,1)S(1)}, bf16[4,2,256,256]{3,2,1,0:T(8,128)(2,1)S(1)}, u32[]{:S(2)}, u32[]{:S(2)}) collective-permute-start(bf16[4,2,256,256]{3,2,1,0:T(8,128)(2,1)S(1)} %shard_map.71.weights_ref), channel_id=1, source_target_pairs={{0,1},{1,0},{2,3},{3,2},{4,5},{5,4},{6,7},{7,6},{8,9},{9,8},{10,11... | collective-permute-start | bytes 3145736 | tf_op jit(solution)/shard_map/ppermute | solution.py:313
  167.0 6.4 %collective-permute-start.4 = (bf16[4,272,256]{2,1,0:T(8,128)(2,1)S(1)}, bf16[4,272,256]{2,1,0:T(8,128)(2,1)S(1)}, u32[]{:S(2)}, u32[]{:S(2)}) collective-permute-start(bf16[4,272,256]{2,1,0:T(8,128)(2,1)S(1)} %shard_map.84), channel_id=1, source_target_pairs={{0,1},{1,0},{2,3},{3,2},{4,5},{5,4},{6,7},{7,6},{8,9},{9,8},{10,11... | collective-permute-start | bytes 1671176 | tf_op jit(solution)/shard_map/ppermute | solution.py:362
  173.1 12.2 %copy-start = (bf16[256,256]{1,0:T(8,128)(2,1)S(1)}, bf16[256,256]{1,0:T(8,128)(2,1)}, u32[]{:S(2)}) copy-start(bf16[256,256]{1,0:T(8,128)(2,1)} %refs_1_.1) | copy-start | bytes 393220

commit v6 on v5

--- a/solution.py
+++ b/solution.py
@@ -226,11 +226,12 @@
 
 
 def join_kernel(own_ref, other_ref, out_ref):
-    width = own_ref.shape[1] - 16
-    for i in range(own_ref.shape[0]):
-        out_ref[i, :width] = (own_ref[i, :width] + other_ref[i, :width].astype(f32)).astype(bf16)
+    n, width, _ = own_ref.shape
+    width = width - 16
+    for j, i in enumerate(half_turn(n)):
+        out_ref[j, :width] = (own_ref[i, :width] + other_ref[i, :width].astype(f32)).astype(bf16)
         pieces = own_ref[i, width:] + other_ref[i, width:].astype(f32)
-        out_ref[i, width:] = pieces_of(jnp.sum(pieces, axis=0, keepdims=True))
+        out_ref[j, width:] = pieces_of(jnp.sum(pieces, axis=0, keepdims=True))
 
 
 def finish_kernel(rows, parts_ref, proto_ref, loss_ref, grad_ref):
@@ -247,6 +248,10 @@
     grad_ref[...] = (unit_grad - unit * jnp.sum(unit * unit_grad, axis=1, keepdims=True)) * scale
 
 
+def half_turn(n):
+    return [(i + n // 2) % n for i in range(n)]
+
+
 def call(kernel, outs, *args, place=None, scratch=(), limit=20):
     vmem = pl.BlockSpec(memory_space=pltpu.VMEM)
     place = place or {}
@@ -270,8 +275,15 @@
     columns = width * nx * nc
     lines, column_lines = rows // LANES, columns // LANES
 
+    orders = {
+        "z": half_turn(nz),
+        "y": half_turn(ny),
+        "x": half_turn(nx),
+        ("c", "x"): [c * nx + x for c in reversed(range(nc)) for x in half_turn(nx)],
+    }
+
     def exchange(values, axes):
-        return lax.all_to_all(values, axes, 0, 0, tiled=True)
+        return lax.all_to_all(values, axes, 0, 0, axis_index_groups=[orders[axes]], tiled=True)
 
     def far(values):
         return pltpu.with_memory_space_constraint(values, pltpu.HBM)

time: 187 us -> 179 us (0.957)
  blocking collectives: 108 us -> 100 us
    all_to_all x10, blocking collectives: 108 us -> 100 us  [exchange(): lax.all_to_all(values, axes, 0, 0, axis_index_groups=[orders[axes]], tile...]
    all_to_all x2, starting transfers between devices: 19.9 us -> 25.5 us  [exchange(): lax.all_to_all(values, axes, 0, 0, axis_index_groups=[orders[axes]], tile...]
    ppermute x1, starting transfers between devices: 9.5 us -> 4.41 us  [per_device(): lax.ppermute(own_weights, 'c', [(i, (i + 1) % nc) for i in range(nc)])]
where the time goes in v6:
time: 179 us
  blocking collectives  100 us (56%)
  starting transfers between devices  45.5 us (25%)
  Pallas kernels  17.3 us (10%)
  waiting for transfers between devices  14.6 us (8%)
    all_to_all x10, blocking collectives, exchange(): lax.all_to_all(values, axes, 0, 0, axis_index_groups=[orders[axes]], tile...  100 us
    all_to_all x2, starting transfers between devices, exchange(): lax.all_to_all(values, axes, 0, 0, axis_index_groups=[orders[axes]], tile...  25.5 us
    pallas_call x19, Pallas kernels, call(): pl.pallas_call(kernel, out_shape=outs, in_specs=[pl.BlockSpec(memory_spac...  17.3 us
    ppermute x3, waiting for transfers between devices, per_device(): lax.ppermute(weights, 'x', [(i, (i + k) % nx) for i in range(nx)])  12.7 us
    ppermute x3, starting transfers between devices, per_device(): lax.ppermute(weights, 'x', [(i, (i + k) % nx) for i in range(nx)])  10.9 us
    ppermute x1, starting transfers between devices, per_device(): other = lax.ppermute(halves[0], 'c', [(i, (i + 1) % nc) for i in range(nc)])  4.58 us
    ppermute x1, starting transfers between devices, per_device(): lax.ppermute(own_weights, 'c', [(i, (i + 1) % nc) for i in range(nc)])  4.41 us
  transfers between devices with their start and end apart: 7, of which 6 were waited for; matrix products, arithmetic and copies ran while one was open for 0% of the time, Pallas kernels for 2%

profile of v6, /device:TPU:1, one launch (start us, length us, event | category | flops | bytes accessed | tf_op | source)
XLA Modules:
  0.0 178.6 jit_solution(14199884472690007315)
XLA Ops:
  0.6 2.1 %shard_map.68 = bf16[16,32,256]{2,1,0:T(8,128)(2,1)} custom-call(s32[16]{0:T(128)} %mask_ref.1, bf16[256,256]{1,0:T(8,128)(2,1)} %sp_ref.1, bf16[256,256]{1,0:T(8,128)(2,1)} %tp_ref.1), custom_call_target="tpu_custom_call" | custom-call | tf_op jit(solution)/shard_map/pallas_call | solution.py:258
  2.8 19.1 %all-to-all-start = ((bf16[16,32,256]{2,1,0:T(8,128)(2,1)}), bf16[16,32,256]{2,1,0:T(8,128)(2,1)S(1)}, u32[]{:S(2)}, u32[]{:S(2)}) async-start(bf16[16,32,256]{2,1,0:T(8,128)(2,1)} %shard_map.68), calls=%async_computation | async-start | bytes 524288 | tf_op jit(solution)/shard_map/all_to_all | solution.py:286
  23.1 4.7 %collective-permute-start = (bf16[2,256,256]{2,1,0:T(8,128)(2,1)S(1)}, bf16[2,256,256]{2,1,0:T(8,128)(2,1)S(1)}, u32[]{:S(2)}, u32[]{:S(2)}) collective-permute-start(bf16[2,256,256]{2,1,0:T(8,128)(2,1)S(1)} %shard_map.69.refs_0_), channel_id=1, source_target_pairs={{0,4},{2,6},{4,0},{6,2},{1,5},{3,7},{5,1},{7,3},{8,12},{10,14},{12... | collective-permute-start | bytes 786440 | tf_op jit(solution)/shard_map/ppermute | solution.py:309
  27.7 5.3 %collective-permute-done.refs_2_ = bf16[2,256,256]{2,1,0:T(8,128)(2,1)S(1)} collective-permute-done((bf16[2,256,256]{2,1,0:T(8,128)(2,1)S(1)}, bf16[2,256,256]{2,1,0:T(8,128)(2,1)S(1)}, u32[]{:S(2)}, u32[]{:S(2)}) %collective-permute-start) | collective-permute-done | bytes 262176 | tf_op jit(solution)/shard_map/ppermute | solution.py:309
  35.3 6.4 %all-to-all-start.1 = ((bf16[4,512,256]{2,1,0:T(8,128)(2,1)}), bf16[4,512,256]{2,1,0:T(8,128)(2,1)S(1)}, u32[]{:S(2)}, u32[]{:S(2)}) async-start(bf16[4,512,256]{2,1,0:T(8,128)(2,1)} %shard_map.70), calls=%async_computation.1 | async-start | bytes 2097152 | tf_op jit(solution)/shard_map/all_to_all | solution.py:286
  41.7 4.4 %collective-permute-start.2 = (bf16[2,256,256]{2,1,0:T(8,128)(2,1)S(1)}, bf16[2,256,256]{2,1,0:T(8,128)(2,1)S(1)}, u32[]{:S(2)}, u32[]{:S(2)}) collective-permute-start(bf16[2,256,256]{2,1,0:T(8,128)(2,1)S(1)} %shard_map.69.refs_0_), channel_id=1, source_target_pairs={{0,6},{2,0},{4,2},{6,4},{1,7},{3,1},{5,3},{7,5},{8,14},{10,8},{12,... | collective-permute-start | bytes 786440 | tf_op jit(solution)/shard_map/ppermute | solution.py:309
  46.1 1.9 %collective-permute-start.1 = (bf16[2,256,256]{2,1,0:T(8,128)(2,1)S(1)}, bf16[2,256,256]{2,1,0:T(8,128)(2,1)S(1)}, u32[]{:S(2)}, u32[]{:S(2)}) collective-permute-start(bf16[2,256,256]{2,1,0:T(8,128)(2,1)S(1)} %shard_map.69.refs_0_), channel_id=1, source_target_pairs={{0,2},{2,4},{4,6},{6,0},{1,3},{3,5},{5,7},{7,1},{8,10},{10,12},{12... | collective-permute-start | bytes 786440 | tf_op jit(solution)/shard_map/ppermute | solution.py:309
  48.0 2.3 %collective-permute-done.2.refs_3_ = bf16[2,256,256]{2,1,0:T(8,128)(2,1)S(1)} collective-permute-done((bf16[2,256,256]{2,1,0:T(8,128)(2,1)S(1)}, bf16[2,256,256]{2,1,0:T(8,128)(2,1)S(1)}, u32[]{:S(2)}, u32[]{:S(2)}) %collective-permute-start.2) | collective-permute-done | bytes 262176 | tf_op jit(solution)/shard_map/ppermute | solution.py:309
  50.4 5.0 %collective-permute-done.1.refs_1_ = bf16[2,256,256]{2,1,0:T(8,128)(2,1)S(1)} collective-permute-done((bf16[2,256,256]{2,1,0:T(8,128)(2,1)S(1)}, bf16[2,256,256]{2,1,0:T(8,128)(2,1)S(1)}, u32[]{:S(2)}, u32[]{:S(2)}) %collective-permute-start.1) | collective-permute-done | bytes 262176 | tf_op jit(solution)/shard_map/ppermute | solution.py:309
  56.1 4.4 %collective-permute-start.3 = (bf16[4,2,256,256]{3,2,1,0:T(8,128)(2,1)S(1)}, bf16[4,2,256,256]{3,2,1,0:T(8,128)(2,1)S(1)}, u32[]{:S(2)}, u32[]{:S(2)}) collective-permute-start(bf16[4,2,256,256]{3,2,1,0:T(8,128)(2,1)S(1)} %shard_map.71.weights_ref), channel_id=1, source_target_pairs={{0,1},{1,0},{2,3},{3,2},{4,5},{5,4},{6,7},{7,6},{8,9},{9,8},{10,11... | collective-permute-start | bytes 3145736 | tf_op jit(solution)/shard_map/ppermute | solution.py:325
  60.5 1.8 %shard_map.72 = (bf16[1024,1024]{1,0:T(8,128)(2,1)S(1)}, bf16[1024,1024]{1,0:T(8,128)(2,1)S(1)}, bf16[1024,1024]{1,0:T(8,128)(2,1)S(1)}, f32[8,128]{1,0:T(8,128)S(1)}, f32[8,128]{1,0:T(8,128)S(1)}) custom-call(bf16[4,512,256]{2,1,0:T(8,128)(2,1)S(1)} %all-to-all-done.1.rows_ref, bf16[4,2,256,256]{3,2,1,0:T(8,128)(2,1)S(1)} %shard_map.71.weights_ref), custom_call_target="tpu_custom_call" | custom-call | tf_op jit(solution)/shard_map/pallas_call | solution.py:258
  62.8 1.8 %shard_map.73 = (bf16[1024,1024]{1,0:T(8,128)(2,1)S(1)}, bf16[1024,1024]{1,0:T(8,128)(2,1)S(1)}, bf16[1024,1024]{1,0:T(8,128)(2,1)S(1)}, f32[8,128]{1,0:T(8,128)S(1)}, f32[8,128]{1,0:T(8,128)S(1)}) custom-call(bf16[4,512,256]{2,1,0:T(8,128)(2,1)S(1)} %all-to-all-done.1.rows_ref, bf16[4,2,256,256]{3,2,1,0:T(8,128)(2,1)S(1)} %collective-permute-done.3.weights_ref), custom_call_target="tpu_custom_call" | custom-call | tf_op jit(solution)/shard_map/pallas_call | solution.py:258
  64.6 6.5 %all_to_all.60.parts_ref = bf16[8,16,128]{2,1,0:T(8,128)(2,1)S(1)} all-to-all(bf16[8,16,128]{2,1,0:T(8,128)(2,1)S(1)} %shard_map.74), channel_id=1, replica_groups={{5,7,1,3,4,6,0,2},{13,15,9,11,12,14,8,10},{21,23,17,19,20,22,16,18},{29..., dimensions={0} | all-to-all | bytes 65536 | tf_op jit(solution)/shard_map/all_to_all | solution.py:286
  71.8 5.5 %all_to_all.61.parts_ref = f32[4,8,128]{2,1,0:T(8,128)S(1)} all-to-all(f32[4,8,128]{2,1,0:T(8,128)S(1)} %shard_map.75), channel_id=1, replica_groups={{16,24,0,8},{17,25,1,9},{18,26,2,10},{19,27,3,11},{20,28,4,12},{21,29,5..., dimensions={0} | all-to-all | bytes 32768 | tf_op jit(solution)/shard_map/all_to_all | solution.py:286
  77.4 14.7 %all_to_all.62.parts_ref = f32[16,8,128]{2,1,0:T(8,128)S(1)} all-to-all(f32[16,8,128]{2,1,0:T(8,128)S(1)} %shard_map.76), channel_id=1, replica_groups={{256,288,320,352,384,416,448,480,0,32,64,96,128,160,192,224},{257,289,3..., dimensions={0} | all-to-all | bytes 131072 | tf_op jit(solution)/shard_map/all_to_all | solution.py:286
  93.2 9.9 %all_to_all.63.parts_ref = bf16[8,16,128]{2,1,0:T(8,128)(2,1)S(1)} all-to-all(bf16[8,16,128]{2,1,0:T(8,128)(2,1)S(1)} %shard_map.77), channel_id=1, replica_groups={{5,7,1,3,4,6,0,2},{13,15,9,11,12,14,8,10},{21,23,17,19,20,22,16,18},{29..., dimensions={0} | all-to-all | bytes 65536 | tf_op jit(solution)/shard_map/all_to_all | solution.py:286
  103.8 6.6 %all_to_all.64.parts_ref = f32[4,16,128]{2,1,0:T(8,128)S(1)} all-to-all(f32[4,16,128]{2,1,0:T(8,128)S(1)} %shard_map.78), channel_id=1, replica_groups={{16,24,0,8},{17,25,1,9},{18,26,2,10},{19,27,3,11},{20,28,4,12},{21,29,5..., dimensions={0} | all-to-all | bytes 65536 | tf_op jit(solution)/shard_map/all_to_all | solution.py:286
  110.5 14.5 %all_to_all.65.parts_ref = bf16[16,16,128]{2,1,0:T(8,128)(2,1)S(1)} all-to-all(bf16[16,16,128]{2,1,0:T(8,128)(2,1)S(1)} %shard_map.79), channel_id=1, replica_groups={{256,288,320,352,384,416,448,480,0,32,64,96,128,160,192,224},{257,289,3..., dimensions={0} | all-to-all | bytes 131072 | tf_op jit(solution)/shard_map/all_to_all | solution.py:286
  126.2 9.5 %all_to_all.66.parts_ref.column_ref = bf16[8,16,128]{2,1,0:T(8,128)(2,1)S(1)} all-to-all(bf16[8,16,128]{2,1,0:T(8,128)(2,1)S(1)} %get-tuple-element.48), channel_id=1, replica_groups={{5,7,1,3,4,6,0,2},{13,15,9,11,12,14,8,10},{21,23,17,19,20,22,16,18},{29..., dimensions={0} | all-to-all | bytes 65536 | tf_op jit(solution)/shard_map/all_to_all | solution.py:286
  136.9 6.7 %all_to_all.67.parts_ref = f32[4,16,128]{2,1,0:T(8,128)S(1)} all-to-all(f32[4,16,128]{2,1,0:T(8,128)S(1)} %shard_map.81), channel_id=1, replica_groups={{16,24,0,8},{17,25,1,9},{18,26,2,10},{19,27,3,11},{20,28,4,12},{21,29,5..., dimensions={0} | all-to-all | bytes 65536 | tf_op jit(solution)/shard_map/all_to_all | solution.py:286
  143.6 14.6 %all_to_all.68.parts_ref = bf16[16,16,128]{2,1,0:T(8,128)(2,1)S(1)} all-to-all(bf16[16,16,128]{2,1,0:T(8,128)(2,1)S(1)} %shard_map.82), channel_id=1, replica_groups={{256,288,320,352,384,416,448,480,0,32,64,96,128,160,192,224},{257,289,3..., dimensions={0} | all-to-all | bytes 131072 | tf_op jit(solution)/shard_map/all_to_all | solution.py:286
  158.1 1.3 shard_map.84
  159.4 4.6 %collective-permute-start.4 = (bf16[4,272,256]{2,1,0:T(8,128)(2,1)S(1)}, bf16[4,272,256]{2,1,0:T(8,128)(2,1)S(1)}, u32[]{:S(2)}, u32[]{:S(2)}) collective-permute-start(bf16[4,272,256]{2,1,0:T(8,128)(2,1)S(1)} %shard_map.84), channel_id=1, source_target_pairs={{0,1},{1,0},{2,3},{3,2},{4,5},{5,4},{6,7},{7,6},{8,9},{9,8},{10,11... | collective-permute-start | bytes 1671176 | tf_op jit(solution)/shard_map/ppermute | solution.py:374
  165.7 12.0 %all_to_all.69.refs_0_ = bf16[4,272,256]{2,1,0:T(8,128)(2,1)S(1)} all-to-all(bf16[4,272,256]{2,1,0:T(8,128)(2,1)S(1)} %shard_map.85), channel_id=1, replica_groups={{4,6,0,2},{5,7,1,3},{12,14,8,10},{13,15,9,11},{20,22,16,18},{21,23,17,1..., dimensions={0} | all-to-all | bytes 1114112 | tf_op jit(solution)/shard_map/all_to_all | solution.py:286
  (22 shorter events, 12.1 us)
Async XLA Ops:
  2.8 31.5 %all-to-all-start = ((bf16[16,32,256]{2,1,0:T(8,128)(2,1)}), bf16[16,32,256]{2,1,0:T(8,128)(2,1)S(1)}, u32[]{:S(2)}, u32[]{:S(2)}) async-start(bf16[16,32,256]{2,1,0:T(8,128)(2,1)} %shard_map.68), calls=%async_computation | async-start | bytes 524288 | tf_op jit(solution)/shard_map/all_to_all | solution.py:286
  23.1 10.0 %collective-permute-start = (bf16[2,256,256]{2,1,0:T(8,128)(2,1)S(1)}, bf16[2,256,256]{2,1,0:T(8,128)(2,1)S(1)}, u32[]{:S(2)}, u32[]{:S(2)}) collective-permute-start(bf16[2,256,256]{2,1,0:T(8,128)(2,1)S(1)} %shard_map.69.refs_0_), channel_id=1, source_target_pairs={{0,4},{2,6},{4,0},{6,2},{1,5},{3,7},{5,1},{7,3},{8,12},{10,14},{12... | collective-permute-start | bytes 786440 | tf_op jit(solution)/shard_map/ppermute | solution.py:309
  35.3 20.1 %all-to-all-start.1 = ((bf16[4,512,256]{2,1,0:T(8,128)(2,1)}), bf16[4,512,256]{2,1,0:T(8,128)(2,1)S(1)}, u32[]{:S(2)}, u32[]{:S(2)}) async-start(bf16[4,512,256]{2,1,0:T(8,128)(2,1)} %shard_map.70), calls=%async_computation.1 | async-start | bytes 2097152 | tf_op jit(solution)/shard_map/all_to_all | solution.py:286
  41.7 8.7 %collective-permute-start.2 = (bf16[2,256,256]{2,1,0:T(8,128)(2,1)S(1)}, bf16[2,256,256]{2,1,0:T(8,128)(2,1)S(1)}, u32[]{:S(2)}, u32[]{:S(2)}) collective-permute-start(bf16[2,256,256]{2,1,0:T(8,128)(2,1)S(1)} %shard_map.69.refs_0_), channel_id=1, source_target_pairs={{0,6},{2,0},{4,2},{6,4},{1,7},{3,1},{5,3},{7,5},{8,14},{10,8},{12,... | collective-permute-start | bytes 786440 | tf_op jit(solution)/shard_map/ppermute | solution.py:309
  46.1 9.3 %collective-permute-start.1 = (bf16[2,256,256]{2,1,0:T(8,128)(2,1)S(1)}, bf16[2,256,256]{2,1,0:T(8,128)(2,1)S(1)}, u32[]{:S(2)}, u32[]{:S(2)}) collective-permute-start(bf16[2,256,256]{2,1,0:T(8,128)(2,1)S(1)} %shard_map.69.refs_0_), channel_id=1, source_target_pairs={{0,2},{2,4},{4,6},{6,0},{1,3},{3,5},{5,7},{7,1},{8,10},{10,12},{12... | collective-permute-start | bytes 786440 | tf_op jit(solution)/shard_map/ppermute | solution.py:309
  56.1 6.7 %collective-permute-start.3 = (bf16[4,2,256,256]{3,2,1,0:T(8,128)(2,1)S(1)}, bf16[4,2,256,256]{3,2,1,0:T(8,128)(2,1)S(1)}, u32[]{:S(2)}, u32[]{:S(2)}) collective-permute-start(bf16[4,2,256,256]{3,2,1,0:T(8,128)(2,1)S(1)} %shard_map.71.weights_ref), channel_id=1, source_target_pairs={{0,1},{1,0},{2,3},{3,2},{4,5},{5,4},{6,7},{7,6},{8,9},{9,8},{10,11... | collective-permute-start | bytes 3145736 | tf_op jit(solution)/shard_map/ppermute | solution.py:325
  159.4 6.2 %collective-permute-start.4 = (bf16[4,272,256]{2,1,0:T(8,128)(2,1)S(1)}, bf16[4,272,256]{2,1,0:T(8,128)(2,1)S(1)}, u32[]{:S(2)}, u32[]{:S(2)}) collective-permute-start(bf16[4,272,256]{2,1,0:T(8,128)(2,1)S(1)} %shard_map.84), channel_id=1, source_target_pairs={{0,1},{1,0},{2,3},{3,2},{4,5},{5,4},{6,7},{7,6},{8,9},{9,8},{10,11... | collective-permute-start | bytes 1671176 | tf_op jit(solution)/shard_map/ppermute | solution.py:374
  165.3 12.4 %copy-start = (bf16[256,256]{1,0:T(8,128)(2,1)S(1)}, bf16[256,256]{1,0:T(8,128)(2,1)}, u32[]{:S(2)}) copy-start(bf16[256,256]{1,0:T(8,128)(2,1)} %refs_1_.1) | copy-start | bytes 393220

commit v7 on v6

--- a/solution.py
+++ b/solution.py
@@ -350,14 +350,17 @@
     row = exchange(row, "z")
 
     column, student_total = call(
-        third_column_kernel, (column_out, shape((lines, LANES), f32)), core, row, *targets, place=smem
+        third_column_kernel,
+        (shape(column_out.shape, f32), shape((lines, LANES), f32)),
+        core, row, *targets,
+        place=smem,
     )
     column = exchange(column, ("c", "x"))
     row = call(
         last_row_kernel, rows_out, core, column, *targets, own_product, other_product, place=smem, scratch=scratch
     )
     row = exchange(row, "y")
-    row = call(add_kernel, shape((nz, 2 * lines, LANES), bf16), row)
+    row = call(add_kernel, shape((nz, 2 * lines, LANES), f32), row)
     row = exchange(row, "z")
 
     halves = []

time: 179 us -> 182 us (1.017)
  blocking collectives: 100 us -> 104 us
    all_to_all x10, blocking collectives: 100 us -> 104 us  [exchange(): lax.all_to_all(values, axes, 0, 0, axis_index_groups=[orders[axes]], tile...]
where the time goes in v7:
time: 182 us; the launch traced here: 181 us
  blocking collectives  104 us (57%)
  starting transfers between devices  44.8 us (25%)
  Pallas kernels  17.3 us (10%)
  waiting for transfers between devices  14.6 us (8%)
    all_to_all x10, blocking collectives, exchange(): lax.all_to_all(values, axes, 0, 0, axis_index_groups=[orders[axes]], tile...  104 us
    all_to_all x2, starting transfers between devices, exchange(): lax.all_to_all(values, axes, 0, 0, axis_index_groups=[orders[axes]], tile...  25.5 us
    pallas_call x19, Pallas kernels, call(): pl.pallas_call(kernel, out_shape=outs, in_specs=[pl.BlockSpec(memory_spac...  17.3 us
    ppermute x3, waiting for transfers between devices, per_device(): lax.ppermute(weights, 'x', [(i, (i + k) % nx) for i in range(nx)])  12.7 us
    ppermute x3, starting transfers between devices, per_device(): lax.ppermute(weights, 'x', [(i, (i + k) % nx) for i in range(nx)])  10.9 us
    ppermute x1, starting transfers between devices, per_device(): lax.ppermute(own_weights, 'c', [(i, (i + 1) % nc) for i in range(nc)])  4.41 us
    ppermute x1, starting transfers between devices, per_device(): other = lax.ppermute(halves[0], 'c', [(i, (i + 1) % nc) for i in range(nc)])  3.96 us
  transfers between devices with their start and end apart: 7, of which 6 were waited for; matrix products, arithmetic and copies ran while one was open for 0% of the time, Pallas kernels for 2%

profile of v7, /device:TPU:1, one launch (start us, length us, event | category | flops | bytes accessed | tf_op | source)
XLA Modules:
  0.0 181.1 jit_solution(11738325756712786352)
XLA Ops:
  0.6 2.1 %shard_map.68 = bf16[16,32,256]{2,1,0:T(8,128)(2,1)} custom-call(s32[16]{0:T(128)} %mask_ref.1, bf16[256,256]{1,0:T(8,128)(2,1)} %sp_ref.1, bf16[256,256]{1,0:T(8,128)(2,1)} %tp_ref.1), custom_call_target="tpu_custom_call" | custom-call | tf_op jit(solution)/shard_map/pallas_call | solution.py:258
  2.8 19.1 %all-to-all-start = ((bf16[16,32,256]{2,1,0:T(8,128)(2,1)}), bf16[16,32,256]{2,1,0:T(8,128)(2,1)S(1)}, u32[]{:S(2)}, u32[]{:S(2)}) async-start(bf16[16,32,256]{2,1,0:T(8,128)(2,1)} %shard_map.68), calls=%async_computation | async-start | bytes 524288 | tf_op jit(solution)/shard_map/all_to_all | solution.py:286
  23.1 4.7 %collective-permute-start = (bf16[2,256,256]{2,1,0:T(8,128)(2,1)S(1)}, bf16[2,256,256]{2,1,0:T(8,128)(2,1)S(1)}, u32[]{:S(2)}, u32[]{:S(2)}) collective-permute-start(bf16[2,256,256]{2,1,0:T(8,128)(2,1)S(1)} %shard_map.69.refs_0_), channel_id=1, source_target_pairs={{0,4},{2,6},{4,0},{6,2},{1,5},{3,7},{5,1},{7,3},{8,12},{10,14},{12... | collective-permute-start | bytes 786440 | tf_op jit(solution)/shard_map/ppermute | solution.py:309
  27.7 5.3 %collective-permute-done.refs_2_ = bf16[2,256,256]{2,1,0:T(8,128)(2,1)S(1)} collective-permute-done((bf16[2,256,256]{2,1,0:T(8,128)(2,1)S(1)}, bf16[2,256,256]{2,1,0:T(8,128)(2,1)S(1)}, u32[]{:S(2)}, u32[]{:S(2)}) %collective-permute-start) | collective-permute-done | bytes 262176 | tf_op jit(solution)/shard_map/ppermute | solution.py:309
  35.3 6.4 %all-to-all-start.1 = ((bf16[4,512,256]{2,1,0:T(8,128)(2,1)}), bf16[4,512,256]{2,1,0:T(8,128)(2,1)S(1)}, u32[]{:S(2)}, u32[]{:S(2)}) async-start(bf16[4,512,256]{2,1,0:T(8,128)(2,1)} %shard_map.70), calls=%async_computation.1 | async-start | bytes 2097152 | tf_op jit(solution)/shard_map/all_to_all | solution.py:286
  41.7 4.4 %collective-permute-start.2 = (bf16[2,256,256]{2,1,0:T(8,128)(2,1)S(1)}, bf16[2,256,256]{2,1,0:T(8,128)(2,1)S(1)}, u32[]{:S(2)}, u32[]{:S(2)}) collective-permute-start(bf16[2,256,256]{2,1,0:T(8,128)(2,1)S(1)} %shard_map.69.refs_0_), channel_id=1, source_target_pairs={{0,6},{2,0},{4,2},{6,4},{1,7},{3,1},{5,3},{7,5},{8,14},{10,8},{12,... | collective-permute-start | bytes 786440 | tf_op jit(solution)/shard_map/ppermute | solution.py:309
  46.1 1.9 %collective-permute-start.1 = (bf16[2,256,256]{2,1,0:T(8,128)(2,1)S(1)}, bf16[2,256,256]{2,1,0:T(8,128)(2,1)S(1)}, u32[]{:S(2)}, u32[]{:S(2)}) collective-permute-start(bf16[2,256,256]{2,1,0:T(8,128)(2,1)S(1)} %shard_map.69.refs_0_), channel_id=1, source_target_pairs={{0,2},{2,4},{4,6},{6,0},{1,3},{3,5},{5,7},{7,1},{8,10},{10,12},{12... | collective-permute-start | bytes 786440 | tf_op jit(solution)/shard_map/ppermute | solution.py:309
  48.0 2.3 %collective-permute-done.2.refs_3_ = bf16[2,256,256]{2,1,0:T(8,128)(2,1)S(1)} collective-permute-done((bf16[2,256,256]{2,1,0:T(8,128)(2,1)S(1)}, bf16[2,256,256]{2,1,0:T(8,128)(2,1)S(1)}, u32[]{:S(2)}, u32[]{:S(2)}) %collective-permute-start.2) | collective-permute-done | bytes 262176 | tf_op jit(solution)/shard_map/ppermute | solution.py:309
  50.4 5.0 %collective-permute-done.1.refs_1_ = bf16[2,256,256]{2,1,0:T(8,128)(2,1)S(1)} collective-permute-done((bf16[2,256,256]{2,1,0:T(8,128)(2,1)S(1)}, bf16[2,256,256]{2,1,0:T(8,128)(2,1)S(1)}, u32[]{:S(2)}, u32[]{:S(2)}) %collective-permute-start.1) | collective-permute-done | bytes 262176 | tf_op jit(solution)/shard_map/ppermute | solution.py:309
  56.1 4.4 %collective-permute-start.3 = (bf16[4,2,256,256]{3,2,1,0:T(8,128)(2,1)S(1)}, bf16[4,2,256,256]{3,2,1,0:T(8,128)(2,1)S(1)}, u32[]{:S(2)}, u32[]{:S(2)}) collective-permute-start(bf16[4,2,256,256]{3,2,1,0:T(8,128)(2,1)S(1)} %shard_map.71.weights_ref), channel_id=1, source_target_pairs={{0,1},{1,0},{2,3},{3,2},{4,5},{5,4},{6,7},{7,6},{8,9},{9,8},{10,11... | collective-permute-start | bytes 3145736 | tf_op jit(solution)/shard_map/ppermute | solution.py:325
  60.5 1.8 %shard_map.72 = (bf16[1024,1024]{1,0:T(8,128)(2,1)S(1)}, bf16[1024,1024]{1,0:T(8,128)(2,1)S(1)}, bf16[1024,1024]{1,0:T(8,128)(2,1)S(1)}, f32[8,128]{1,0:T(8,128)S(1)}, f32[8,128]{1,0:T(8,128)S(1)}) custom-call(bf16[4,512,256]{2,1,0:T(8,128)(2,1)S(1)} %all-to-all-done.1.rows_ref, bf16[4,2,256,256]{3,2,1,0:T(8,128)(2,1)S(1)} %shard_map.71.weights_ref), custom_call_target="tpu_custom_call" | custom-call | tf_op jit(solution)/shard_map/pallas_call | solution.py:258
  62.8 1.8 %shard_map.73 = (bf16[1024,1024]{1,0:T(8,128)(2,1)S(1)}, bf16[1024,1024]{1,0:T(8,128)(2,1)S(1)}, bf16[1024,1024]{1,0:T(8,128)(2,1)S(1)}, f32[8,128]{1,0:T(8,128)S(1)}, f32[8,128]{1,0:T(8,128)S(1)}) custom-call(bf16[4,512,256]{2,1,0:T(8,128)(2,1)S(1)} %all-to-all-done.1.rows_ref, bf16[4,2,256,256]{3,2,1,0:T(8,128)(2,1)S(1)} %collective-permute-done.3.weights_ref), custom_call_target="tpu_custom_call" | custom-call | tf_op jit(solution)/shard_map/pallas_call | solution.py:258
  64.6 6.5 %all_to_all.60.parts_ref = bf16[8,16,128]{2,1,0:T(8,128)(2,1)S(1)} all-to-all(bf16[8,16,128]{2,1,0:T(8,128)(2,1)S(1)} %shard_map.74), channel_id=1, replica_groups={{5,7,1,3,4,6,0,2},{13,15,9,11,12,14,8,10},{21,23,17,19,20,22,16,18},{29..., dimensions={0} | all-to-all | bytes 65536 | tf_op jit(solution)/shard_map/all_to_all | solution.py:286
  71.8 5.5 %all_to_all.61.parts_ref = f32[4,8,128]{2,1,0:T(8,128)S(1)} all-to-all(f32[4,8,128]{2,1,0:T(8,128)S(1)} %shard_map.75), channel_id=1, replica_groups={{16,24,0,8},{17,25,1,9},{18,26,2,10},{19,27,3,11},{20,28,4,12},{21,29,5..., dimensions={0} | all-to-all | bytes 32768 | tf_op jit(solution)/shard_map/all_to_all | solution.py:286
  77.4 14.7 %all_to_all.62.parts_ref = f32[16,8,128]{2,1,0:T(8,128)S(1)} all-to-all(f32[16,8,128]{2,1,0:T(8,128)S(1)} %shard_map.76), channel_id=1, replica_groups={{256,288,320,352,384,416,448,480,0,32,64,96,128,160,192,224},{257,289,3..., dimensions={0} | all-to-all | bytes 131072 | tf_op jit(solution)/shard_map/all_to_all | solution.py:286
  93.2 9.9 %all_to_all.63.parts_ref = bf16[8,16,128]{2,1,0:T(8,128)(2,1)S(1)} all-to-all(bf16[8,16,128]{2,1,0:T(8,128)(2,1)S(1)} %shard_map.77), channel_id=1, replica_groups={{5,7,1,3,4,6,0,2},{13,15,9,11,12,14,8,10},{21,23,17,19,20,22,16,18},{29..., dimensions={0} | all-to-all | bytes 65536 | tf_op jit(solution)/shard_map/all_to_all | solution.py:286
  103.8 6.6 %all_to_all.64.parts_ref = f32[4,16,128]{2,1,0:T(8,128)S(1)} all-to-all(f32[4,16,128]{2,1,0:T(8,128)S(1)} %shard_map.78), channel_id=1, replica_groups={{16,24,0,8},{17,25,1,9},{18,26,2,10},{19,27,3,11},{20,28,4,12},{21,29,5..., dimensions={0} | all-to-all | bytes 65536 | tf_op jit(solution)/shard_map/all_to_all | solution.py:286
  110.5 14.5 %all_to_all.65.parts_ref = bf16[16,16,128]{2,1,0:T(8,128)(2,1)S(1)} all-to-all(bf16[16,16,128]{2,1,0:T(8,128)(2,1)S(1)} %shard_map.79), channel_id=1, replica_groups={{256,288,320,352,384,416,448,480,0,32,64,96,128,160,192,224},{257,289,3..., dimensions={0} | all-to-all | bytes 131072 | tf_op jit(solution)/shard_map/all_to_all | solution.py:286
  126.2 9.6 %all_to_all.66.parts_ref.column_ref = f32[8,16,128]{2,1,0:T(8,128)S(1)} all-to-all(f32[8,16,128]{2,1,0:T(8,128)S(1)} %get-tuple-element.48), channel_id=1, replica_groups={{5,7,1,3,4,6,0,2},{13,15,9,11,12,14,8,10},{21,23,17,19,20,22,16,18},{29..., dimensions={0} | all-to-all | bytes 131072 | tf_op jit(solution)/shard_map/all_to_all | solution.py:286
  137.0 6.7 %all_to_all.67.parts_ref = f32[4,16,128]{2,1,0:T(8,128)S(1)} all-to-all(f32[4,16,128]{2,1,0:T(8,128)S(1)} %shard_map.81), channel_id=1, replica_groups={{16,24,0,8},{17,25,1,9},{18,26,2,10},{19,27,3,11},{20,28,4,12},{21,29,5..., dimensions={0} | all-to-all | bytes 65536 | tf_op jit(solution)/shard_map/all_to_all | solution.py:286
  143.7 17.1 %all_to_all.68.parts_ref = f32[16,16,128]{2,1,0:T(8,128)S(1)} all-to-all(f32[16,16,128]{2,1,0:T(8,128)S(1)} %shard_map.82), channel_id=1, replica_groups={{256,288,320,352,384,416,448,480,0,32,64,96,128,160,192,224},{257,289,3..., dimensions={0} | all-to-all | bytes 262144 | tf_op jit(solution)/shard_map/all_to_all | solution.py:286
  160.8 1.3 shard_map.84
  162.1 4.0 %collective-permute-start.4 = (bf16[4,272,256]{2,1,0:T(8,128)(2,1)S(1)}, bf16[4,272,256]{2,1,0:T(8,128)(2,1)S(1)}, u32[]{:S(2)}, u32[]{:S(2)}) collective-permute-start(bf16[4,272,256]{2,1,0:T(8,128)(2,1)S(1)} %shard_map.84), channel_id=1, source_target_pairs={{0,1},{1,0},{2,3},{3,2},{4,5},{5,4},{6,7},{7,6},{8,9},{9,8},{10,11... | collective-permute-start | bytes 1671176 | tf_op jit(solution)/shard_map/ppermute | solution.py:377
  167.8 12.4 %all_to_all.69.refs_0_ = bf16[4,272,256]{2,1,0:T(8,128)(2,1)S(1)} all-to-all(bf16[4,272,256]{2,1,0:T(8,128)(2,1)S(1)} %shard_map.85), channel_id=1, replica_groups={{4,6,0,2},{5,7,1,3},{12,14,8,10},{13,15,9,11},{20,22,16,18},{21,23,17,1..., dimensions={0} | all-to-all | bytes 1114112 | tf_op jit(solution)/shard_map/all_to_all | solution.py:286
  (22 shorter events, 12.1 us)
Async XLA Ops:
  2.8 31.5 %all-to-all-start = ((bf16[16,32,256]{2,1,0:T(8,128)(2,1)}), bf16[16,32,256]{2,1,0:T(8,128)(2,1)S(1)}, u32[]{:S(2)}, u32[]{:S(2)}) async-start(bf16[16,32,256]{2,1,0:T(8,128)(2,1)} %shard_map.68), calls=%async_computation | async-start | bytes 524288 | tf_op jit(solution)/shard_map/all_to_all | solution.py:286
  23.1 10.0 %collective-permute-start = (bf16[2,256,256]{2,1,0:T(8,128)(2,1)S(1)}, bf16[2,256,256]{2,1,0:T(8,128)(2,1)S(1)}, u32[]{:S(2)}, u32[]{:S(2)}) collective-permute-start(bf16[2,256,256]{2,1,0:T(8,128)(2,1)S(1)} %shard_map.69.refs_0_), channel_id=1, source_target_pairs={{0,4},{2,6},{4,0},{6,2},{1,5},{3,7},{5,1},{7,3},{8,12},{10,14},{12... | collective-permute-start | bytes 786440 | tf_op jit(solution)/shard_map/ppermute | solution.py:309
  35.3 20.1 %all-to-all-start.1 = ((bf16[4,512,256]{2,1,0:T(8,128)(2,1)}), bf16[4,512,256]{2,1,0:T(8,128)(2,1)S(1)}, u32[]{:S(2)}, u32[]{:S(2)}) async-start(bf16[4,512,256]{2,1,0:T(8,128)(2,1)} %shard_map.70), calls=%async_computation.1 | async-start | bytes 2097152 | tf_op jit(solution)/shard_map/all_to_all | solution.py:286
  41.7 8.7 %collective-permute-start.2 = (bf16[2,256,256]{2,1,0:T(8,128)(2,1)S(1)}, bf16[2,256,256]{2,1,0:T(8,128)(2,1)S(1)}, u32[]{:S(2)}, u32[]{:S(2)}) collective-permute-start(bf16[2,256,256]{2,1,0:T(8,128)(2,1)S(1)} %shard_map.69.refs_0_), channel_id=1, source_target_pairs={{0,6},{2,0},{4,2},{6,4},{1,7},{3,1},{5,3},{7,5},{8,14},{10,8},{12,... | collective-permute-start | bytes 786440 | tf_op jit(solution)/shard_map/ppermute | solution.py:309
  46.1 9.3 %collective-permute-start.1 = (bf16[2,256,256]{2,1,0:T(8,128)(2,1)S(1)}, bf16[2,256,256]{2,1,0:T(8,128)(2,1)S(1)}, u32[]{:S(2)}, u32[]{:S(2)}) collective-permute-start(bf16[2,256,256]{2,1,0:T(8,128)(2,1)S(1)} %shard_map.69.refs_0_), channel_id=1, source_target_pairs={{0,2},{2,4},{4,6},{6,0},{1,3},{3,5},{5,7},{7,1},{8,10},{10,12},{12... | collective-permute-start | bytes 786440 | tf_op jit(solution)/shard_map/ppermute | solution.py:309
  56.1 6.7 %collective-permute-start.3 = (bf16[4,2,256,256]{3,2,1,0:T(8,128)(2,1)S(1)}, bf16[4,2,256,256]{3,2,1,0:T(8,128)(2,1)S(1)}, u32[]{:S(2)}, u32[]{:S(2)}) collective-permute-start(bf16[4,2,256,256]{3,2,1,0:T(8,128)(2,1)S(1)} %shard_map.71.weights_ref), channel_id=1, source_target_pairs={{0,1},{1,0},{2,3},{3,2},{4,5},{5,4},{6,7},{7,6},{8,9},{9,8},{10,11... | collective-permute-start | bytes 3145736 | tf_op jit(solution)/shard_map/ppermute | solution.py:325
  162.1 5.5 %collective-permute-start.4 = (bf16[4,272,256]{2,1,0:T(8,128)(2,1)S(1)}, bf16[4,272,256]{2,1,0:T(8,128)(2,1)S(1)}, u32[]{:S(2)}, u32[]{:S(2)}) collective-permute-start(bf16[4,272,256]{2,1,0:T(8,128)(2,1)S(1)} %shard_map.84), channel_id=1, source_target_pairs={{0,1},{1,0},{2,3},{3,2},{4,5},{5,4},{6,7},{7,6},{8,9},{9,8},{10,11... | collective-permute-start | bytes 1671176 | tf_op jit(solution)/shard_map/ppermute | solution.py:377
  167.3 12.8 %copy-start = (bf16[256,256]{1,0:T(8,128)(2,1)S(1)}, bf16[256,256]{1,0:T(8,128)(2,1)}, u32[]{:S(2)}) copy-start(bf16[256,256]{1,0:T(8,128)(2,1)} %refs_1_.1) | copy-start | bytes 393220

commit v8 on v6

--- a/solution.py
+++ b/solution.py
@@ -46,6 +46,16 @@
 
 def matvec(row, matrix, dims):
     return jnp.sum(dot(split_rows(row), matrix, dims), axis=0, keepdims=True)
+
+
+def lane_sums(row, matrix_ref):
+    partial = matrix_ref[:, :LANES].astype(f32) * row[:, :LANES]
+    for j in range(1, row.shape[1] // LANES):
+        lanes = slice(LANES * j, LANES * (j + 1))
+        partial = partial + matrix_ref[:, lanes].astype(f32) * row[:, lanes]
+    high = partial.astype(bf16)
+    ones = jnp.ones((16, LANES), bf16)
+    return (dot(ones, high, NT) + dot(ones, (partial - high.astype(f32)).astype(bf16), NT))[0:1]
 
 
 def spread(out_ref, tile):
@@ -158,14 +168,14 @@
 
 def column_kernel(core_ref, parts_ref, own_ref, other_ref, column_ref):
     row = unfold(1.0 / total_of(parts_ref))
-    spread_halves(core_ref, column_ref, fold(matvec(row, own_ref[...], NT)), fold(matvec(row, other_ref[...], NT)))
+    spread_halves(core_ref, column_ref, fold(lane_sums(row, own_ref)), fold(lane_sums(row, other_ref)))
 
 
 def third_column_kernel(core_ref, parts_ref, own_ref, other_ref, column_ref, total_ref):
     both = total_of(parts_ref)
     lines = both.shape[0] // 2
     row = unfold(1.0 / both[:lines])
-    spread_halves(core_ref, column_ref, fold(matvec(row, own_ref[...], NT)), fold(matvec(row, other_ref[...], NT)))
+    spread_halves(core_ref, column_ref, fold(lane_sums(row, own_ref)), fold(lane_sums(row, other_ref)))
     total_ref[...] = both[lines:]
 
 
@@ -276,7 +286,7 @@
     lines, column_lines = rows // LANES, columns // LANES
 
     orders = {
-        "z": half_turn(nz),
+        "z": [(i + 10) % nz for i in range(nz)],
         "y": half_turn(ny),
         "x": half_turn(nx),
         ("c", "x"): [c * nx + x for c in reversed(range(nc)) for x in half_turn(nx)],
@@ -344,7 +354,7 @@
 
     column = call(column_kernel, column_out, core, row, *targets, place=smem)
     column = exchange(column, ("c", "x"))
-    row = call(second_row_kernel, rows_out, core, column, *targets, own_total, other_total, place=smem, scratch=scratch)
+    row = call(second_row_kernel, shape(rows_out.shape, bf16), core, column, *targets, own_total, other_total, place=smem, scratch=scratch)
     row = exchange(row, "y")
     row = call(add_kernel, shape((nz, 2 * lines, LANES), bf16), row)
     row = exchange(row, "z")

time: 179 us -> 179 us (level)
    all_to_all x2, starting transfers between devices: 25.5 us -> 23.7 us  [exchange(): lax.all_to_all(values, axes, 0, 0, axis_index_groups=[orders[axes]], tile...]
where the time goes in v8:
time: 179 us; the launch traced here: 178 us
  blocking collectives  101 us (56%)
  starting transfers between devices  45 us (25%)
  Pallas kernels  17 us (9%)
  waiting for transfers between devices  14.3 us (8%)
    all_to_all x10, blocking collectives, exchange(): lax.all_to_all(values, axes, 0, 0, axis_index_groups=[orders[axes]], tile...  101 us
    all_to_all x2, starting transfers between devices, exchange(): lax.all_to_all(values, axes, 0, 0, axis_index_groups=[orders[axes]], tile...  23.7 us
    pallas_call x19, Pallas kernels, call(): pl.pallas_call(kernel, out_shape=outs, in_specs=[pl.BlockSpec(memory_spac...  17 us
    ppermute x3, waiting for transfers between devices, per_device(): lax.ppermute(weights, 'x', [(i, (i + k) % nx) for i in range(nx)])  12 us
    ppermute x3, starting transfers between devices, per_device(): lax.ppermute(weights, 'x', [(i, (i + k) % nx) for i in range(nx)])  10.9 us
    ppermute x1, starting transfers between devices, per_device(): lax.ppermute(own_weights, 'c', [(i, (i + 1) % nc) for i in range(nc)])  5.58 us
    ppermute x1, starting transfers between devices, per_device(): other = lax.ppermute(halves[0], 'c', [(i, (i + 1) % nc) for i in range(nc)])  4.7 us
  transfers between devices with their start and end apart: 7, of which 6 were waited for; matrix products, arithmetic and copies ran while one was open for 0% of the time, Pallas kernels for 2%

profile of v8, /device:TPU:1, one launch (start us, length us, event | category | flops | bytes accessed | tf_op | source)
XLA Modules:
  0.0 178.3 jit_solution(7811588545812864925)
XLA Ops:
  0.6 2.1 %shard_map.68 = bf16[16,32,256]{2,1,0:T(8,128)(2,1)} custom-call(s32[16]{0:T(128)} %mask_ref.1, bf16[256,256]{1,0:T(8,128)(2,1)} %sp_ref.1, bf16[256,256]{1,0:T(8,128)(2,1)} %tp_ref.1), custom_call_target="tpu_custom_call" | custom-call | tf_op jit(solution)/shard_map/pallas_call | solution.py:268
  2.8 17.3 %all-to-all-start = ((bf16[16,32,256]{2,1,0:T(8,128)(2,1)}), bf16[16,32,256]{2,1,0:T(8,128)(2,1)S(1)}, u32[]{:S(2)}, u32[]{:S(2)}) async-start(bf16[16,32,256]{2,1,0:T(8,128)(2,1)} %shard_map.68), calls=%async_computation | async-start | bytes 524288 | tf_op jit(solution)/shard_map/all_to_all | solution.py:296
  21.3 4.7 %collective-permute-start = (bf16[2,256,256]{2,1,0:T(8,128)(2,1)S(1)}, bf16[2,256,256]{2,1,0:T(8,128)(2,1)S(1)}, u32[]{:S(2)}, u32[]{:S(2)}) collective-permute-start(bf16[2,256,256]{2,1,0:T(8,128)(2,1)S(1)} %shard_map.69.refs_0_), channel_id=1, source_target_pairs={{0,4},{2,6},{4,0},{6,2},{1,5},{3,7},{5,1},{7,3},{8,12},{10,14},{12... | collective-permute-start | bytes 786440 | tf_op jit(solution)/shard_map/ppermute | solution.py:319
  25.9 5.3 %collective-permute-done.refs_2_ = bf16[2,256,256]{2,1,0:T(8,128)(2,1)S(1)} collective-permute-done((bf16[2,256,256]{2,1,0:T(8,128)(2,1)S(1)}, bf16[2,256,256]{2,1,0:T(8,128)(2,1)S(1)}, u32[]{:S(2)}, u32[]{:S(2)}) %collective-permute-start) | collective-permute-done | bytes 262176 | tf_op jit(solution)/shard_map/ppermute | solution.py:319
  31.2 1.7 all-to-all-done.rows_ref
  33.9 6.4 %all-to-all-start.1 = ((bf16[4,512,256]{2,1,0:T(8,128)(2,1)}), bf16[4,512,256]{2,1,0:T(8,128)(2,1)S(1)}, u32[]{:S(2)}, u32[]{:S(2)}) async-start(bf16[4,512,256]{2,1,0:T(8,128)(2,1)} %shard_map.70), calls=%async_computation.1 | async-start | bytes 2097152 | tf_op jit(solution)/shard_map/all_to_all | solution.py:296
  40.3 4.4 %collective-permute-start.2 = (bf16[2,256,256]{2,1,0:T(8,128)(2,1)S(1)}, bf16[2,256,256]{2,1,0:T(8,128)(2,1)S(1)}, u32[]{:S(2)}, u32[]{:S(2)}) collective-permute-start(bf16[2,256,256]{2,1,0:T(8,128)(2,1)S(1)} %shard_map.69.refs_0_), channel_id=1, source_target_pairs={{0,6},{2,0},{4,2},{6,4},{1,7},{3,1},{5,3},{7,5},{8,14},{10,8},{12,... | collective-permute-start | bytes 786440 | tf_op jit(solution)/shard_map/ppermute | solution.py:319
  44.7 1.9 %collective-permute-start.1 = (bf16[2,256,256]{2,1,0:T(8,128)(2,1)S(1)}, bf16[2,256,256]{2,1,0:T(8,128)(2,1)S(1)}, u32[]{:S(2)}, u32[]{:S(2)}) collective-permute-start(bf16[2,256,256]{2,1,0:T(8,128)(2,1)S(1)} %shard_map.69.refs_0_), channel_id=1, source_target_pairs={{0,2},{2,4},{4,6},{6,0},{1,3},{3,5},{5,7},{7,1},{8,10},{10,12},{12... | collective-permute-start | bytes 786440 | tf_op jit(solution)/shard_map/ppermute | solution.py:319
  46.6 1.4 collective-permute-done.2.refs_3_
  48.0 5.3 %collective-permute-done.1.refs_1_ = bf16[2,256,256]{2,1,0:T(8,128)(2,1)S(1)} collective-permute-done((bf16[2,256,256]{2,1,0:T(8,128)(2,1)S(1)}, bf16[2,256,256]{2,1,0:T(8,128)(2,1)S(1)}, u32[]{:S(2)}, u32[]{:S(2)}) %collective-permute-start.1) | collective-permute-done | bytes 262176 | tf_op jit(solution)/shard_map/ppermute | solution.py:319
  54.0 5.6 %collective-permute-start.3 = (bf16[4,2,256,256]{3,2,1,0:T(8,128)(2,1)S(1)}, bf16[4,2,256,256]{3,2,1,0:T(8,128)(2,1)S(1)}, u32[]{:S(2)}, u32[]{:S(2)}) collective-permute-start(bf16[4,2,256,256]{3,2,1,0:T(8,128)(2,1)S(1)} %shard_map.71.weights_ref), channel_id=1, source_target_pairs={{0,1},{1,0},{2,3},{3,2},{4,5},{5,4},{6,7},{7,6},{8,9},{9,8},{10,11... | collective-permute-start | bytes 3145736 | tf_op jit(solution)/shard_map/ppermute | solution.py:335
  59.6 1.8 %shard_map.72 = (bf16[1024,1024]{1,0:T(8,128)(2,1)S(1)}, bf16[1024,1024]{1,0:T(8,128)(2,1)S(1)}, bf16[1024,1024]{1,0:T(8,128)(2,1)S(1)}, f32[8,128]{1,0:T(8,128)S(1)}, f32[8,128]{1,0:T(8,128)S(1)}) custom-call(bf16[4,512,256]{2,1,0:T(8,128)(2,1)S(1)} %all-to-all-done.1.rows_ref, bf16[4,2,256,256]{3,2,1,0:T(8,128)(2,1)S(1)} %shard_map.71.weights_ref), custom_call_target="tpu_custom_call" | custom-call | tf_op jit(solution)/shard_map/pallas_call | solution.py:268
  61.8 1.8 %shard_map.73 = (bf16[1024,1024]{1,0:T(8,128)(2,1)S(1)}, bf16[1024,1024]{1,0:T(8,128)(2,1)S(1)}, bf16[1024,1024]{1,0:T(8,128)(2,1)S(1)}, f32[8,128]{1,0:T(8,128)S(1)}, f32[8,128]{1,0:T(8,128)S(1)}) custom-call(bf16[4,512,256]{2,1,0:T(8,128)(2,1)S(1)} %all-to-all-done.1.rows_ref, bf16[4,2,256,256]{3,2,1,0:T(8,128)(2,1)S(1)} %collective-permute-done.3.weights_ref), custom_call_target="tpu_custom_call" | custom-call | tf_op jit(solution)/shard_map/pallas_call | solution.py:268
  63.7 6.5 %all_to_all.60.parts_ref = bf16[8,16,128]{2,1,0:T(8,128)(2,1)S(1)} all-to-all(bf16[8,16,128]{2,1,0:T(8,128)(2,1)S(1)} %shard_map.74), channel_id=1, replica_groups={{5,7,1,3,4,6,0,2},{13,15,9,11,12,14,8,10},{21,23,17,19,20,22,16,18},{29..., dimensions={0} | all-to-all | bytes 65536 | tf_op jit(solution)/shard_map/all_to_all | solution.py:296
  70.9 5.5 %all_to_all.61.parts_ref = f32[4,8,128]{2,1,0:T(8,128)S(1)} all-to-all(f32[4,8,128]{2,1,0:T(8,128)S(1)} %shard_map.75), channel_id=1, replica_groups={{16,24,0,8},{17,25,1,9},{18,26,2,10},{19,27,3,11},{20,28,4,12},{21,29,5..., dimensions={0} | all-to-all | bytes 32768 | tf_op jit(solution)/shard_map/all_to_all | solution.py:296
  76.4 15.6 %all_to_all.62.parts_ref = f32[16,8,128]{2,1,0:T(8,128)S(1)} all-to-all(f32[16,8,128]{2,1,0:T(8,128)S(1)} %shard_map.76), channel_id=1, replica_groups={{320,352,384,416,448,480,0,32,64,96,128,160,192,224,256,288},{321,353,3..., dimensions={0} | all-to-all | bytes 131072 | tf_op jit(solution)/shard_map/all_to_all | solution.py:296
  93.1 9.9 %all_to_all.63.parts_ref = bf16[8,16,128]{2,1,0:T(8,128)(2,1)S(1)} all-to-all(bf16[8,16,128]{2,1,0:T(8,128)(2,1)S(1)} %shard_map.77), channel_id=1, replica_groups={{5,7,1,3,4,6,0,2},{13,15,9,11,12,14,8,10},{21,23,17,19,20,22,16,18},{29..., dimensions={0} | all-to-all | bytes 65536 | tf_op jit(solution)/shard_map/all_to_all | solution.py:296
  103.7 6.6 %all_to_all.64.parts_ref = bf16[4,16,128]{2,1,0:T(8,128)(2,1)S(1)} all-to-all(bf16[4,16,128]{2,1,0:T(8,128)(2,1)S(1)} %shard_map.78), channel_id=1, replica_groups={{16,24,0,8},{17,25,1,9},{18,26,2,10},{19,27,3,11},{20,28,4,12},{21,29,5..., dimensions={0} | all-to-all | bytes 32768 | tf_op jit(solution)/shard_map/all_to_all | solution.py:296
  110.3 14.4 %all_to_all.65.parts_ref = bf16[16,16,128]{2,1,0:T(8,128)(2,1)S(1)} all-to-all(bf16[16,16,128]{2,1,0:T(8,128)(2,1)S(1)} %shard_map.79), channel_id=1, replica_groups={{320,352,384,416,448,480,0,32,64,96,128,160,192,224,256,288},{321,353,3..., dimensions={0} | all-to-all | bytes 131072 | tf_op jit(solution)/shard_map/all_to_all | solution.py:296
  125.8 9.6 %all_to_all.66.parts_ref.column_ref = bf16[8,16,128]{2,1,0:T(8,128)(2,1)S(1)} all-to-all(bf16[8,16,128]{2,1,0:T(8,128)(2,1)S(1)} %get-tuple-element.48), channel_id=1, replica_groups={{5,7,1,3,4,6,0,2},{13,15,9,11,12,14,8,10},{21,23,17,19,20,22,16,18},{29..., dimensions={0} | all-to-all | bytes 65536 | tf_op jit(solution)/shard_map/all_to_all | solution.py:296
  136.6 6.6 %all_to_all.67.parts_ref = f32[4,16,128]{2,1,0:T(8,128)S(1)} all-to-all(f32[4,16,128]{2,1,0:T(8,128)S(1)} %shard_map.81), channel_id=1, replica_groups={{16,24,0,8},{17,25,1,9},{18,26,2,10},{19,27,3,11},{20,28,4,12},{21,29,5..., dimensions={0} | all-to-all | bytes 65536 | tf_op jit(solution)/shard_map/all_to_all | solution.py:296
  143.2 14.5 %all_to_all.68.parts_ref = bf16[16,16,128]{2,1,0:T(8,128)(2,1)S(1)} all-to-all(bf16[16,16,128]{2,1,0:T(8,128)(2,1)S(1)} %shard_map.82), channel_id=1, replica_groups={{320,352,384,416,448,480,0,32,64,96,128,160,192,224,256,288},{321,353,3..., dimensions={0} | all-to-all | bytes 131072 | tf_op jit(solution)/shard_map/all_to_all | solution.py:296
  159.0 4.7 %collective-permute-start.4 = (bf16[4,272,256]{2,1,0:T(8,128)(2,1)S(1)}, bf16[4,272,256]{2,1,0:T(8,128)(2,1)S(1)}, u32[]{:S(2)}, u32[]{:S(2)}) collective-permute-start(bf16[4,272,256]{2,1,0:T(8,128)(2,1)S(1)} %shard_map.84), channel_id=1, source_target_pairs={{0,1},{1,0},{2,3},{3,2},{4,5},{5,4},{6,7},{7,6},{8,9},{9,8},{10,11... | collective-permute-start | bytes 1671176 | tf_op jit(solution)/shard_map/ppermute | solution.py:384
  165.4 12.0 %all_to_all.69.refs_0_ = bf16[4,272,256]{2,1,0:T(8,128)(2,1)S(1)} all-to-all(bf16[4,272,256]{2,1,0:T(8,128)(2,1)S(1)} %shard_map.85), channel_id=1, replica_groups={{4,6,0,2},{5,7,1,3},{12,14,8,10},{13,15,9,11},{20,22,16,18},{21,23,17,1..., dimensions={0} | all-to-all | bytes 1114112 | tf_op jit(solution)/shard_map/all_to_all | solution.py:296
  (22 shorter events, 11.9 us)
Async XLA Ops:
  2.8 30.1 %all-to-all-start = ((bf16[16,32,256]{2,1,0:T(8,128)(2,1)}), bf16[16,32,256]{2,1,0:T(8,128)(2,1)S(1)}, u32[]{:S(2)}, u32[]{:S(2)}) async-start(bf16[16,32,256]{2,1,0:T(8,128)(2,1)} %shard_map.68), calls=%async_computation | async-start | bytes 524288 | tf_op jit(solution)/shard_map/all_to_all | solution.py:296
  21.3 10.0 %collective-permute-start = (bf16[2,256,256]{2,1,0:T(8,128)(2,1)S(1)}, bf16[2,256,256]{2,1,0:T(8,128)(2,1)S(1)}, u32[]{:S(2)}, u32[]{:S(2)}) collective-permute-start(bf16[2,256,256]{2,1,0:T(8,128)(2,1)S(1)} %shard_map.69.refs_0_), channel_id=1, source_target_pairs={{0,4},{2,6},{4,0},{6,2},{1,5},{3,7},{5,1},{7,3},{8,12},{10,14},{12... | collective-permute-start | bytes 786440 | tf_op jit(solution)/shard_map/ppermute | solution.py:319
  33.9 19.4 %all-to-all-start.1 = ((bf16[4,512,256]{2,1,0:T(8,128)(2,1)}), bf16[4,512,256]{2,1,0:T(8,128)(2,1)S(1)}, u32[]{:S(2)}, u32[]{:S(2)}) async-start(bf16[4,512,256]{2,1,0:T(8,128)(2,1)} %shard_map.70), calls=%async_computation.1 | async-start | bytes 2097152 | tf_op jit(solution)/shard_map/all_to_all | solution.py:296
  40.3 7.7 %collective-permute-start.2 = (bf16[2,256,256]{2,1,0:T(8,128)(2,1)S(1)}, bf16[2,256,256]{2,1,0:T(8,128)(2,1)S(1)}, u32[]{:S(2)}, u32[]{:S(2)}) collective-permute-start(bf16[2,256,256]{2,1,0:T(8,128)(2,1)S(1)} %shard_map.69.refs_0_), channel_id=1, source_target_pairs={{0,6},{2,0},{4,2},{6,4},{1,7},{3,1},{5,3},{7,5},{8,14},{10,8},{12,... | collective-permute-start | bytes 786440 | tf_op jit(solution)/shard_map/ppermute | solution.py:319
  44.7 8.6 %collective-permute-start.1 = (bf16[2,256,256]{2,1,0:T(8,128)(2,1)S(1)}, bf16[2,256,256]{2,1,0:T(8,128)(2,1)S(1)}, u32[]{:S(2)}, u32[]{:S(2)}) collective-permute-start(bf16[2,256,256]{2,1,0:T(8,128)(2,1)S(1)} %shard_map.69.refs_0_), channel_id=1, source_target_pairs={{0,2},{2,4},{4,6},{6,0},{1,3},{3,5},{5,7},{7,1},{8,10},{10,12},{12... | collective-permute-start | bytes 786440 | tf_op jit(solution)/shard_map/ppermute | solution.py:319
  54.0 7.9 %collective-permute-start.3 = (bf16[4,2,256,256]{3,2,1,0:T(8,128)(2,1)S(1)}, bf16[4,2,256,256]{3,2,1,0:T(8,128)(2,1)S(1)}, u32[]{:S(2)}, u32[]{:S(2)}) collective-permute-start(bf16[4,2,256,256]{3,2,1,0:T(8,128)(2,1)S(1)} %shard_map.71.weights_ref), channel_id=1, source_target_pairs={{0,1},{1,0},{2,3},{3,2},{4,5},{5,4},{6,7},{7,6},{8,9},{9,8},{10,11... | collective-permute-start | bytes 3145736 | tf_op jit(solution)/shard_map/ppermute | solution.py:335
  159.0 6.3 %collective-permute-start.4 = (bf16[4,272,256]{2,1,0:T(8,128)(2,1)S(1)}, bf16[4,272,256]{2,1,0:T(8,128)(2,1)S(1)}, u32[]{:S(2)}, u32[]{:S(2)}) collective-permute-start(bf16[4,272,256]{2,1,0:T(8,128)(2,1)S(1)} %shard_map.84), channel_id=1, source_target_pairs={{0,1},{1,0},{2,3},{3,2},{4,5},{5,4},{6,7},{7,6},{8,9},{9,8},{10,11... | collective-permute-start | bytes 1671176 | tf_op jit(solution)/shard_map/ppermute | solution.py:384
  165.0 12.4 %copy-start = (bf16[256,256]{1,0:T(8,128)(2,1)S(1)}, bf16[256,256]{1,0:T(8,128)(2,1)}, u32[]{:S(2)}) copy-start(bf16[256,256]{1,0:T(8,128)(2,1)} %refs_1_.1) | copy-start | bytes 393220

commit v9 on v8

--- a/solution.py
+++ b/solution.py
@@ -289,7 +289,7 @@
         "z": [(i + 10) % nz for i in range(nz)],
         "y": half_turn(ny),
         "x": half_turn(nx),
-        ("c", "x"): [c * nx + x for c in reversed(range(nc)) for x in half_turn(nx)],
+        ("c", "x"): [c * nx + x for c in range(nc) for x in half_turn(nx)],
     }
 
     def exchange(values, axes):

time: 179 us -> 180 us (level)
  no operation moved by 1% of the time
where the time goes in v9:
time: 180 us; the launch traced here: 179 us
  blocking collectives  102 us (57%)
  starting transfers between devices  45.1 us (25%)
  Pallas kernels  17 us (9%)
  waiting for transfers between devices  14.3 us (8%)
    all_to_all x10, blocking collectives, exchange(): lax.all_to_all(values, axes, 0, 0, axis_index_groups=[orders[axes]], tile...  102 us
    all_to_all x2, starting transfers between devices, exchange(): lax.all_to_all(values, axes, 0, 0, axis_index_groups=[orders[axes]], tile...  23.7 us
    pallas_call x19, Pallas kernels, call(): pl.pallas_call(kernel, out_shape=outs, in_specs=[pl.BlockSpec(memory_spac...  17 us
    ppermute x3, waiting for transfers between devices, per_device(): lax.ppermute(weights, 'x', [(i, (i + k) % nx) for i in range(nx)])  12 us
    ppermute x3, starting transfers between devices, per_device(): lax.ppermute(weights, 'x', [(i, (i + k) % nx) for i in range(nx)])  10.9 us
    ppermute x1, starting transfers between devices, per_device(): lax.ppermute(own_weights, 'c', [(i, (i + 1) % nc) for i in range(nc)])  5.58 us
    ppermute x1, starting transfers between devices, per_device(): other = lax.ppermute(halves[0], 'c', [(i, (i + 1) % nc) for i in range(nc)])  4.87 us
  transfers between devices with their start and end apart: 7, of which 6 were waited for; matrix products, arithmetic and copies ran while one was open for 0% of the time, Pallas kernels for 2%

profile of v9, /device:TPU:1, one launch (start us, length us, event | category | flops | bytes accessed | tf_op | source)
XLA Modules:
  0.0 179.3 jit_solution(6022928428976050062)
XLA Ops:
  0.6 2.1 %shard_map.68 = bf16[16,32,256]{2,1,0:T(8,128)(2,1)} custom-call(s32[16]{0:T(128)} %mask_ref.1, bf16[256,256]{1,0:T(8,128)(2,1)} %sp_ref.1, bf16[256,256]{1,0:T(8,128)(2,1)} %tp_ref.1), custom_call_target="tpu_custom_call" | custom-call | tf_op jit(solution)/shard_map/pallas_call | solution.py:268
  2.8 17.3 %all-to-all-start = ((bf16[16,32,256]{2,1,0:T(8,128)(2,1)}), bf16[16,32,256]{2,1,0:T(8,128)(2,1)S(1)}, u32[]{:S(2)}, u32[]{:S(2)}) async-start(bf16[16,32,256]{2,1,0:T(8,128)(2,1)} %shard_map.68), calls=%async_computation | async-start | bytes 524288 | tf_op jit(solution)/shard_map/all_to_all | solution.py:296
  21.3 4.7 %collective-permute-start = (bf16[2,256,256]{2,1,0:T(8,128)(2,1)S(1)}, bf16[2,256,256]{2,1,0:T(8,128)(2,1)S(1)}, u32[]{:S(2)}, u32[]{:S(2)}) collective-permute-start(bf16[2,256,256]{2,1,0:T(8,128)(2,1)S(1)} %shard_map.69.refs_0_), channel_id=1, source_target_pairs={{0,4},{2,6},{4,0},{6,2},{1,5},{3,7},{5,1},{7,3},{8,12},{10,14},{12... | collective-permute-start | bytes 786440 | tf_op jit(solution)/shard_map/ppermute | solution.py:319
  25.9 5.3 %collective-permute-done.refs_2_ = bf16[2,256,256]{2,1,0:T(8,128)(2,1)S(1)} collective-permute-done((bf16[2,256,256]{2,1,0:T(8,128)(2,1)S(1)}, bf16[2,256,256]{2,1,0:T(8,128)(2,1)S(1)}, u32[]{:S(2)}, u32[]{:S(2)}) %collective-permute-start) | collective-permute-done | bytes 262176 | tf_op jit(solution)/shard_map/ppermute | solution.py:319
  31.2 1.7 all-to-all-done.rows_ref
  33.9 6.4 %all-to-all-start.1 = ((bf16[4,512,256]{2,1,0:T(8,128)(2,1)}), bf16[4,512,256]{2,1,0:T(8,128)(2,1)S(1)}, u32[]{:S(2)}, u32[]{:S(2)}) async-start(bf16[4,512,256]{2,1,0:T(8,128)(2,1)} %shard_map.70), calls=%async_computation.1 | async-start | bytes 2097152 | tf_op jit(solution)/shard_map/all_to_all | solution.py:296
  40.3 4.4 %collective-permute-start.2 = (bf16[2,256,256]{2,1,0:T(8,128)(2,1)S(1)}, bf16[2,256,256]{2,1,0:T(8,128)(2,1)S(1)}, u32[]{:S(2)}, u32[]{:S(2)}) collective-permute-start(bf16[2,256,256]{2,1,0:T(8,128)(2,1)S(1)} %shard_map.69.refs_0_), channel_id=1, source_target_pairs={{0,6},{2,0},{4,2},{6,4},{1,7},{3,1},{5,3},{7,5},{8,14},{10,8},{12,... | collective-permute-start | bytes 786440 | tf_op jit(solution)/shard_map/ppermute | solution.py:319
  44.7 1.9 %collective-permute-start.1 = (bf16[2,256,256]{2,1,0:T(8,128)(2,1)S(1)}, bf16[2,256,256]{2,1,0:T(8,128)(2,1)S(1)}, u32[]{:S(2)}, u32[]{:S(2)}) collective-permute-start(bf16[2,256,256]{2,1,0:T(8,128)(2,1)S(1)} %shard_map.69.refs_0_), channel_id=1, source_target_pairs={{0,2},{2,4},{4,6},{6,0},{1,3},{3,5},{5,7},{7,1},{8,10},{10,12},{12... | collective-permute-start | bytes 786440 | tf_op jit(solution)/shard_map/ppermute | solution.py:319
  46.6 1.4 collective-permute-done.2.refs_3_
  48.0 5.3 %collective-permute-done.1.refs_1_ = bf16[2,256,256]{2,1,0:T(8,128)(2,1)S(1)} collective-permute-done((bf16[2,256,256]{2,1,0:T(8,128)(2,1)S(1)}, bf16[2,256,256]{2,1,0:T(8,128)(2,1)S(1)}, u32[]{:S(2)}, u32[]{:S(2)}) %collective-permute-start.1) | collective-permute-done | bytes 262176 | tf_op jit(solution)/shard_map/ppermute | solution.py:319
  54.0 5.6 %collective-permute-start.3 = (bf16[4,2,256,256]{3,2,1,0:T(8,128)(2,1)S(1)}, bf16[4,2,256,256]{3,2,1,0:T(8,128)(2,1)S(1)}, u32[]{:S(2)}, u32[]{:S(2)}) collective-permute-start(bf16[4,2,256,256]{3,2,1,0:T(8,128)(2,1)S(1)} %shard_map.71.weights_ref), channel_id=1, source_target_pairs={{0,1},{1,0},{2,3},{3,2},{4,5},{5,4},{6,7},{7,6},{8,9},{9,8},{10,11... | collective-permute-start | bytes 3145736 | tf_op jit(solution)/shard_map/ppermute | solution.py:335
  59.6 1.8 %shard_map.72 = (bf16[1024,1024]{1,0:T(8,128)(2,1)S(1)}, bf16[1024,1024]{1,0:T(8,128)(2,1)S(1)}, bf16[1024,1024]{1,0:T(8,128)(2,1)S(1)}, f32[8,128]{1,0:T(8,128)S(1)}, f32[8,128]{1,0:T(8,128)S(1)}) custom-call(bf16[4,512,256]{2,1,0:T(8,128)(2,1)S(1)} %all-to-all-done.1.rows_ref, bf16[4,2,256,256]{3,2,1,0:T(8,128)(2,1)S(1)} %shard_map.71.weights_ref), custom_call_target="tpu_custom_call" | custom-call | tf_op jit(solution)/shard_map/pallas_call | solution.py:268
  61.8 1.8 %shard_map.73 = (bf16[1024,1024]{1,0:T(8,128)(2,1)S(1)}, bf16[1024,1024]{1,0:T(8,128)(2,1)S(1)}, bf16[1024,1024]{1,0:T(8,128)(2,1)S(1)}, f32[8,128]{1,0:T(8,128)S(1)}, f32[8,128]{1,0:T(8,128)S(1)}) custom-call(bf16[4,512,256]{2,1,0:T(8,128)(2,1)S(1)} %all-to-all-done.1.rows_ref, bf16[4,2,256,256]{3,2,1,0:T(8,128)(2,1)S(1)} %collective-permute-done.3.weights_ref), custom_call_target="tpu_custom_call" | custom-call | tf_op jit(solution)/shard_map/pallas_call | solution.py:268
  63.7 6.6 %all_to_all.60.parts_ref = bf16[8,16,128]{2,1,0:T(8,128)(2,1)S(1)} all-to-all(bf16[8,16,128]{2,1,0:T(8,128)(2,1)S(1)} %shard_map.74), channel_id=1, replica_groups={{4,6,0,2,5,7,1,3},{12,14,8,10,13,15,9,11},{20,22,16,18,21,23,17,19},{28..., dimensions={0} | all-to-all | bytes 65536 | tf_op jit(solution)/shard_map/all_to_all | solution.py:296
  71.0 5.5 %all_to_all.61.parts_ref = f32[4,8,128]{2,1,0:T(8,128)S(1)} all-to-all(f32[4,8,128]{2,1,0:T(8,128)S(1)} %shard_map.75), channel_id=1, replica_groups={{16,24,0,8},{17,25,1,9},{18,26,2,10},{19,27,3,11},{20,28,4,12},{21,29,5..., dimensions={0} | all-to-all | bytes 32768 | tf_op jit(solution)/shard_map/all_to_all | solution.py:296
  76.5 15.6 %all_to_all.62.parts_ref = f32[16,8,128]{2,1,0:T(8,128)S(1)} all-to-all(f32[16,8,128]{2,1,0:T(8,128)S(1)} %shard_map.76), channel_id=1, replica_groups={{320,352,384,416,448,480,0,32,64,96,128,160,192,224,256,288},{321,353,3..., dimensions={0} | all-to-all | bytes 131072 | tf_op jit(solution)/shard_map/all_to_all | solution.py:296
  93.2 10.3 %all_to_all.63.parts_ref = bf16[8,16,128]{2,1,0:T(8,128)(2,1)S(1)} all-to-all(bf16[8,16,128]{2,1,0:T(8,128)(2,1)S(1)} %shard_map.77), channel_id=1, replica_groups={{4,6,0,2,5,7,1,3},{12,14,8,10,13,15,9,11},{20,22,16,18,21,23,17,19},{28..., dimensions={0} | all-to-all | bytes 65536 | tf_op jit(solution)/shard_map/all_to_all | solution.py:296
  104.2 6.6 %all_to_all.64.parts_ref = bf16[4,16,128]{2,1,0:T(8,128)(2,1)S(1)} all-to-all(bf16[4,16,128]{2,1,0:T(8,128)(2,1)S(1)} %shard_map.78), channel_id=1, replica_groups={{16,24,0,8},{17,25,1,9},{18,26,2,10},{19,27,3,11},{20,28,4,12},{21,29,5..., dimensions={0} | all-to-all | bytes 32768 | tf_op jit(solution)/shard_map/all_to_all | solution.py:296
  110.8 14.4 %all_to_all.65.parts_ref = bf16[16,16,128]{2,1,0:T(8,128)(2,1)S(1)} all-to-all(bf16[16,16,128]{2,1,0:T(8,128)(2,1)S(1)} %shard_map.79), channel_id=1, replica_groups={{320,352,384,416,448,480,0,32,64,96,128,160,192,224,256,288},{321,353,3..., dimensions={0} | all-to-all | bytes 131072 | tf_op jit(solution)/shard_map/all_to_all | solution.py:296
  126.3 9.9 %all_to_all.66.parts_ref.column_ref = bf16[8,16,128]{2,1,0:T(8,128)(2,1)S(1)} all-to-all(bf16[8,16,128]{2,1,0:T(8,128)(2,1)S(1)} %get-tuple-element.48), channel_id=1, replica_groups={{4,6,0,2,5,7,1,3},{12,14,8,10,13,15,9,11},{20,22,16,18,21,23,17,19},{28..., dimensions={0} | all-to-all | bytes 65536 | tf_op jit(solution)/shard_map/all_to_all | solution.py:296
  137.4 6.6 %all_to_all.67.parts_ref = f32[4,16,128]{2,1,0:T(8,128)S(1)} all-to-all(f32[4,16,128]{2,1,0:T(8,128)S(1)} %shard_map.81), channel_id=1, replica_groups={{16,24,0,8},{17,25,1,9},{18,26,2,10},{19,27,3,11},{20,28,4,12},{21,29,5..., dimensions={0} | all-to-all | bytes 65536 | tf_op jit(solution)/shard_map/all_to_all | solution.py:296
  144.1 14.5 %all_to_all.68.parts_ref = bf16[16,16,128]{2,1,0:T(8,128)(2,1)S(1)} all-to-all(bf16[16,16,128]{2,1,0:T(8,128)(2,1)S(1)} %shard_map.82), channel_id=1, replica_groups={{320,352,384,416,448,480,0,32,64,96,128,160,192,224,256,288},{321,353,3..., dimensions={0} | all-to-all | bytes 131072 | tf_op jit(solution)/shard_map/all_to_all | solution.py:296
  159.8 4.9 %collective-permute-start.4 = (bf16[4,272,256]{2,1,0:T(8,128)(2,1)S(1)}, bf16[4,272,256]{2,1,0:T(8,128)(2,1)S(1)}, u32[]{:S(2)}, u32[]{:S(2)}) collective-permute-start(bf16[4,272,256]{2,1,0:T(8,128)(2,1)S(1)} %shard_map.84), channel_id=1, source_target_pairs={{0,1},{1,0},{2,3},{3,2},{4,5},{5,4},{6,7},{7,6},{8,9},{9,8},{10,11... | collective-permute-start | bytes 1671176 | tf_op jit(solution)/shard_map/ppermute | solution.py:384
  166.4 12.0 %all_to_all.69.refs_0_ = bf16[4,272,256]{2,1,0:T(8,128)(2,1)S(1)} all-to-all(bf16[4,272,256]{2,1,0:T(8,128)(2,1)S(1)} %shard_map.85), channel_id=1, replica_groups={{4,6,0,2},{5,7,1,3},{12,14,8,10},{13,15,9,11},{20,22,16,18},{21,23,17,1..., dimensions={0} | all-to-all | bytes 1114112 | tf_op jit(solution)/shard_map/all_to_all | solution.py:296
  (22 shorter events, 11.9 us)
Async XLA Ops:
  2.8 30.1 %all-to-all-start = ((bf16[16,32,256]{2,1,0:T(8,128)(2,1)}), bf16[16,32,256]{2,1,0:T(8,128)(2,1)S(1)}, u32[]{:S(2)}, u32[]{:S(2)}) async-start(bf16[16,32,256]{2,1,0:T(8,128)(2,1)} %shard_map.68), calls=%async_computation | async-start | bytes 524288 | tf_op jit(solution)/shard_map/all_to_all | solution.py:296
  21.3 10.0 %collective-permute-start = (bf16[2,256,256]{2,1,0:T(8,128)(2,1)S(1)}, bf16[2,256,256]{2,1,0:T(8,128)(2,1)S(1)}, u32[]{:S(2)}, u32[]{:S(2)}) collective-permute-start(bf16[2,256,256]{2,1,0:T(8,128)(2,1)S(1)} %shard_map.69.refs_0_), channel_id=1, source_target_pairs={{0,4},{2,6},{4,0},{6,2},{1,5},{3,7},{5,1},{7,3},{8,12},{10,14},{12... | collective-permute-start | bytes 786440 | tf_op jit(solution)/shard_map/ppermute | solution.py:319
  33.9 19.4 %all-to-all-start.1 = ((bf16[4,512,256]{2,1,0:T(8,128)(2,1)}), bf16[4,512,256]{2,1,0:T(8,128)(2,1)S(1)}, u32[]{:S(2)}, u32[]{:S(2)}) async-start(bf16[4,512,256]{2,1,0:T(8,128)(2,1)} %shard_map.70), calls=%async_computation.1 | async-start | bytes 2097152 | tf_op jit(solution)/shard_map/all_to_all | solution.py:296
  40.3 7.7 %collective-permute-start.2 = (bf16[2,256,256]{2,1,0:T(8,128)(2,1)S(1)}, bf16[2,256,256]{2,1,0:T(8,128)(2,1)S(1)}, u32[]{:S(2)}, u32[]{:S(2)}) collective-permute-start(bf16[2,256,256]{2,1,0:T(8,128)(2,1)S(1)} %shard_map.69.refs_0_), channel_id=1, source_target_pairs={{0,6},{2,0},{4,2},{6,4},{1,7},{3,1},{5,3},{7,5},{8,14},{10,8},{12,... | collective-permute-start | bytes 786440 | tf_op jit(solution)/shard_map/ppermute | solution.py:319
  44.7 8.6 %collective-permute-start.1 = (bf16[2,256,256]{2,1,0:T(8,128)(2,1)S(1)}, bf16[2,256,256]{2,1,0:T(8,128)(2,1)S(1)}, u32[]{:S(2)}, u32[]{:S(2)}) collective-permute-start(bf16[2,256,256]{2,1,0:T(8,128)(2,1)S(1)} %shard_map.69.refs_0_), channel_id=1, source_target_pairs={{0,2},{2,4},{4,6},{6,0},{1,3},{3,5},{5,7},{7,1},{8,10},{10,12},{12... | collective-permute-start | bytes 786440 | tf_op jit(solution)/shard_map/ppermute | solution.py:319
  54.0 7.9 %collective-permute-start.3 = (bf16[4,2,256,256]{3,2,1,0:T(8,128)(2,1)S(1)}, bf16[4,2,256,256]{3,2,1,0:T(8,128)(2,1)S(1)}, u32[]{:S(2)}, u32[]{:S(2)}) collective-permute-start(bf16[4,2,256,256]{3,2,1,0:T(8,128)(2,1)S(1)} %shard_map.71.weights_ref), channel_id=1, source_target_pairs={{0,1},{1,0},{2,3},{3,2},{4,5},{5,4},{6,7},{7,6},{8,9},{9,8},{10,11... | collective-permute-start | bytes 3145736 | tf_op jit(solution)/shard_map/ppermute | solution.py:335
  159.8 6.4 %collective-permute-start.4 = (bf16[4,272,256]{2,1,0:T(8,128)(2,1)S(1)}, bf16[4,272,256]{2,1,0:T(8,128)(2,1)S(1)}, u32[]{:S(2)}, u32[]{:S(2)}) collective-permute-start(bf16[4,272,256]{2,1,0:T(8,128)(2,1)S(1)} %shard_map.84), channel_id=1, source_target_pairs={{0,1},{1,0},{2,3},{3,2},{4,5},{5,4},{6,7},{7,6},{8,9},{9,8},{10,11... | collective-permute-start | bytes 1671176 | tf_op jit(solution)/shard_map/ppermute | solution.py:384
  166.0 12.4 %copy-start = (bf16[256,256]{1,0:T(8,128)(2,1)S(1)}, bf16[256,256]{1,0:T(8,128)(2,1)}, u32[]{:S(2)}) copy-start(bf16[256,256]{1,0:T(8,128)(2,1)} %refs_1_.1) | copy-start | bytes 393220
